TPU v7x, 256 devices: a whole 4x4x8 slice. The times are simulated.
256 devices in a mesh: dp: 4 (over x), expert: 64 (over y, z, core).
Axes of the slice: x: 4, y: 4, z: 8, core: 2. Of those that a mesh axis runs over, the one named last changes fastest.
Arguments:
- grad_out: bfloat16 [32768, 3584], P(('dp', 'expert')), may hold values from -6 to 6
- expert_ids: int32 [32768, 8], P(('dp', 'expert')), may hold values from 0 to 63, all different within a row; in each aligned block of 128 rows (0 to 127, 128 to 255, ...) at most 24 rows name the same one
- gate_weights: float32 [32768, 8], P(('dp', 'expert')), may hold values from 0.05 to 0.4
- hidden_saved: bfloat16 [4, 64, 64, 24, 1024], P('dp', 'expert'), may hold values from -6 to 6
- swap_flags: int32 [64], replicated, may hold values from 0 to 1, as said below
Outputs:
- panel_grads: float32 [64, 3584, 1024], P('expert', 'dp')
Inputs may be any that keep to these rules, and one draw needn't show every extreme that they name: `expert_ids`: each row names 8 different experts; the rows of one device name no expert more than 24 times, and in some devices one expert exactly 24 times. swap_flags[e] = swap_flags[(e + 32) mod 64]; swap_flags[0] = swap_flags[31] = 1 and swap_flags[1] = 0.
All inputs are finite; a program needn't handle non-finite values.
Results may differ from a plain program's by a relative error of at most 0.0029.
Values may be sent and summed in bfloat16 or wider, within the bound.
No kernel may reach another device: no remote copies, remote signals or barrier semaphores. Data moves between devices by JAX's collectives and lax.ppermute only.
A program may use at most 128 MiB of HBM per device.

v0:
```python
import functools

import jax
import jax.numpy as jnp
from jax import lax
from jax.experimental import pallas as pl
from jax.experimental.pallas import tpu as pltpu
from jax.sharding import Mesh, PartitionSpec as P

NX, NY, NZ, NC = 4, 4, 8, 2
GATHERS = ((0, 1), (3, 2))
SPACE = 56 * 1024 * 1024
PARTS = 3
META = 128
LIGHT = pl.CostEstimate(flops=1024, bytes_accessed=1024, transcendentals=0)


def dispatch_kernel(target_ref, gate_ref, token_ref, *refs):
    out_ref = refs[-1]
    dests, rows = out_ref.shape[:2]
    tokens = target_ref.shape[2]
    slot = lax.broadcasted_iota(jnp.int32, (rows, tokens), 0).astype(jnp.float32)
    picks, weights = [], []
    for r in range(dests):
        hit = slot == target_ref[0, r : r + 1, :]
        picks.append(jnp.where(hit, 1.0, 0.0))
        weights.append(jnp.sum(jnp.where(hit, gate_ref[0, r : r + 1, :], 0.0), axis=1, keepdims=True))
    pick = jnp.concatenate(picks, axis=0).astype(jnp.bfloat16)
    weight = jnp.concatenate(weights, axis=0)
    scaled = jnp.dot(pick, token_ref[...], preferred_element_type=jnp.float32) * weight
    scaled = scaled.astype(jnp.bfloat16)
    for r in range(dests):
        out_ref[r] = scaled[r * rows : (r + 1) * rows]


def dispatch(target, gate, tokens, cols, capacity, after=()):
    pairs, dests, width = target.shape
    rows = 2 * capacity
    return pl.pallas_call(
        dispatch_kernel,
        grid=(pairs,),
        in_specs=[
            pl.BlockSpec((1, dests, width), lambda i: (i, 0, 0)),
            pl.BlockSpec((1, dests, width), lambda i: (i, 0, 0)),
            pl.BlockSpec((width, cols), lambda i: (i, 0)),
        ]
        + [pl.BlockSpec(memory_space=pl.ANY)] * len(after),
        out_specs=pl.BlockSpec((dests, rows, cols), lambda i: (0, i, 0)),
        out_shape=jax.ShapeDtypeStruct((dests, pairs * rows, cols), jnp.bfloat16),
        compiler_params=pltpu.CompilerParams(vmem_limit_bytes=SPACE),
        cost_estimate=LIGHT,
    )(target, gate, tokens, *after)


def later_kernel(value_ref, *refs):
    refs[-1][0] = value_ref[0]


def later(value, *after):
    return pl.pallas_call(
        later_kernel,
        in_specs=[pl.BlockSpec(memory_space=pltpu.SMEM)] + [pl.BlockSpec(memory_space=pl.ANY)] * len(after),
        out_specs=pl.BlockSpec(memory_space=pltpu.SMEM),
        out_shape=jax.ShapeDtypeStruct((1,), jnp.int32),
        cost_estimate=LIGHT,
    )(jnp.asarray(value, jnp.int32).reshape(1), *after)[0]


def ring(size, step):
    return [(i, (i + step) % size) for i in range(size)]


def routing(ids, gates):
    columns = [ids.astype(jnp.float32)]
    for _ in range(PARTS):
        high = lax.reduce_precision(gates, 8, 7)
        columns.append(high)
        gates = gates - high
    meta = jnp.concatenate(columns, axis=1)
    return jnp.pad(meta, ((0, 0), (0, META - meta.shape[1]))).astype(jnp.bfloat16)


def tables(meta, tok, top, wanted, capacity):
    sources = meta.shape[0] // tok
    meta = meta.astype(jnp.float32).reshape(sources, tok, -1).transpose(0, 2, 1)
    ids, gates = meta[:, :top], 0.0
    for i in reversed(range(PARTS)):
        gates = gates + meta[:, (i + 1) * top : (i + 2) * top]
    match = ids[:, None] == wanted[None, :, None, None]
    member = jnp.any(match, axis=2)
    gate = jnp.sum(jnp.where(match, gates[:, None], 0.0), axis=2)
    before = (jnp.arange(tok)[:, None] < jnp.arange(tok)[None, :]).astype(jnp.bfloat16)
    slot = jnp.dot(member.astype(jnp.bfloat16), before, preferred_element_type=jnp.float32)
    odd = (jnp.arange(sources) % 2 * capacity).astype(jnp.float32)
    target = jnp.where(member, slot + odd[:, None, None], -1.0)

    def paired(table):
        table = table.reshape(sources // 2, 2, len(wanted), tok).transpose(0, 2, 1, 3)
        return table.reshape(sources // 2, len(wanted), 2 * tok)

    return paired(target), paired(gate)


def product_kernel(spans, *refs):
    rows_ref, states, out_ref = refs[0], refs[1 : 1 + len(spans)], refs[-1]
    step = pl.program_id(0)

    @pl.when(step == 0)
    def _():
        out_ref[...] = refs[-2][...] if len(refs) > len(spans) + 2 else jnp.zeros_like(out_ref)

    depth, width = states[0].shape[1:]

    def add(chunk, states_ref):
        rows = rows_ref[:, chunk * depth : (chunk + 1) * depth, :]
        out_ref[...] += lax.dot_general(
            rows.reshape(-1, rows.shape[-1]),
            states_ref[...].reshape(-1, width),
            (((0,), (0,)), ((), ())),
            preferred_element_type=jnp.float32,
        )

    for (chunk, low, high), states_ref in zip(spans, states):
        pl.when((step >= low) & (step < high))(functools.partial(add, chunk, states_ref))


def product(total, rows, states):
    senders, _, cols = rows.shape
    group = senders // 2
    depth, width = states[0][0].shape[1:]
    whole = pl.BlockSpec((cols, width), lambda i: (0, 0))
    spans, arrays, specs = [], [], []
    for chunk, parts in enumerate(states):
        low = 0
        for array in parts:
            count = array.shape[0] // group
            spans.append((chunk, low, low + count))
            arrays.append(array)
            specs.append(
                pl.BlockSpec(
                    (group, depth, width),
                    functools.partial(lambda low, count, i: (jnp.clip(i - low, 0, count - 1), 0, 0), low, count),
                )
            )
            low += count
    return pl.pallas_call(
        functools.partial(product_kernel, tuple(spans)),
        grid=(senders // group,),
        in_specs=[pl.BlockSpec((group,) + rows.shape[1:], lambda i: (i, 0, 0))]
        + specs
        + ([] if total is None else [whole]),
        out_specs=whole,
        out_shape=jax.ShapeDtypeStruct((cols, width), jnp.float32),
        compiler_params=pltpu.CompilerParams(vmem_limit_bytes=SPACE),
        cost_estimate=LIGHT,
    )(rows, *arrays, *([] if total is None else [total]))


def local(grad_out, expert_ids, gate_weights, hidden_saved, swap_flags):
    x, y = lax.axis_index("x"), lax.axis_index("y")
    z, c = lax.axis_index("z"), lax.axis_index("c")
    experts, capacity, width = hidden_saved.shape[2:]
    tok, cols = grad_out.shape[0], grad_out.shape[1] // NX
    top = expert_ids.shape[1]
    flag_here = lax.dynamic_index_in_dim(swap_flags, (y * NZ + z) * NC + c, 0, False)
    hidden = hidden_saved.reshape(NY, NZ, NC, capacity, width)
    traded = lax.ppermute(hidden, "y", ring(NY, 2))

    meta = routing(expert_ids, gate_weights)

    def columns(step):
        part = lax.dynamic_slice_in_dim(grad_out, ((x + step) % NX) * cols, cols, 1)
        part = jnp.concatenate([part, meta], axis=1)
        return part if step == 0 else lax.ppermute(part, "x", ring(NX, step))

    gathered = []
    for group in GATHERS:
        block = jnp.stack([columns(s) for s in group])
        gathered.append(lax.all_gather(block, "z", axis=1, tiled=True).reshape(-1, cols + META))

    devices = ((jnp.arange(NY)[:, None] * NZ + z) * NC + jnp.arange(NC)[None]).reshape(-1)
    flags = jnp.take(swap_flags, devices)
    wanted = jnp.where(flags == 1, (devices + experts // 2) % experts, devices).astype(jnp.float32)

    def exchange(tokens, place, after=()):
        pick = tables(lax.dynamic_slice_in_dim(tokens, place, META, 1), tok, top, wanted, capacity)
        rows = dispatch(*pick, tokens, cols, capacity, after)
        return rows, lax.all_to_all(rows, ("y", "c"), 0, 0, tiled=True)

    rows0, arrived0 = exchange(gathered[0], cols, (traded,))
    flag = later(flag_here, rows0)
    own = jnp.where(flag == 1, traded, hidden).transpose(0, 2, 1, 3, 4)
    own = own.reshape(NY * NC, NZ * capacity, width)
    left = lax.ppermute(own, "x", ring(NX, 1))
    right = lax.ppermute(own, "x", ring(NX, 3))
    rows1, arrived1 = exchange(gathered[1], later(cols, own))
    half = own.shape[0] // 2
    start = later(0, rows1)
    far = [
        lax.ppermute(lax.dynamic_slice_in_dim(left, start, half), "x", ring(NX, 1)),
        lax.ppermute(lax.dynamic_slice_in_dim(right, start + half, half), "x", ring(NX, 3)),
    ]
    total = product(None, arrived0, [[own], [left]])
    total = product(total, arrived1, [[right], far])
    return total[None]


def solution(mesh):
    fine = Mesh(mesh.devices.reshape(NX, NY, NZ, NC), ("x", "y", "z", "c"))
    every = ("x", "y", "z", "c")
    return jax.shard_map(
        local,
        mesh=fine,
        in_specs=(
            P(every, None),
            P(every, None),
            P(every, None),
            P("x", ("y", "z", "c"), None, None, None),
            P(),
        ),
        out_specs=P(("y", "z", "c"), "x", None),
        check_vma=False,
    )
```

profile of v0, /device:TPU:1, one launch (start us, length us, event | category | flops | bytes accessed | tf_op | source)
XLA Modules:
  0.0 270.7 jit_solution(9362767034234892080)
XLA Ops:
  6.5 0.7 convert_convert_fusion
  7.2 0.7 reduce-precision_convert_fusion.1
  7.9 0.1 copy.33
  8.1 1.4 constant_dynamic-slice_fusion.4
  9.4 0.1 fusion.9
  9.5 2.1 collective-permute-start.2
  11.7 5.0 %collective-permute-done.2 = bf16[128,1024]{1,0:T(8,128)(2,1)S(1)} collective-permute-done((bf16[128,1024]{1,0:T(8,128)(2,1)S(1)}, bf16[128,1024]{1,0:T(8,128)(2,1)S(1)}, u32[]{:S(2)}, u32[]{:S(2)}) %collective-permute-start.2) | collective-permute-done | bytes 262176 | tf_op jit(solution)/shard_map/ppermute | solution.py:174
  16.7 0.8 pad_maximum_fusion.1
  17.5 0.0 all-gather.5.cloned.1.call-update
  17.6 0.0 all-gather.3.cloned.1.call-start
  17.6 3.5 %collective-permute-start = (bf16[128,1024]{1,0:T(8,128)(2,1)S(1)}, bf16[128,1024]{1,0:T(8,128)(2,1)S(1)}, u32[]{:S(2)}, u32[]{:S(2)}) collective-permute-start(bf16[128,1024]{1,0:T(8,128)(2,1)S(1)} %get-tuple-element.14), channel_id=1, source_target_pairs={{0,192},{64,0},{128,64},{192,128},{1,193},{65,1},{129,65},{193,129... | collective-permute-start | bytes 786440 | tf_op jit(solution)/shard_map/ppermute | solution.py:174
  21.1 0.4 collective-permute-start.1
  21.5 10.1 %collective-permute-done = bf16[128,1024]{1,0:T(8,128)(2,1)S(1)} collective-permute-done((bf16[128,1024]{1,0:T(8,128)(2,1)S(1)}, bf16[128,1024]{1,0:T(8,128)(2,1)S(1)}, u32[]{:S(2)}, u32[]{:S(2)}) %collective-permute-start) | collective-permute-done | bytes 262176 | tf_op jit(solution)/shard_map/ppermute | solution.py:174
  31.6 0.8 pad_maximum_fusion
  32.4 0.0 all-gather.3.cloned.1.call-update
  32.4 0.1 collective-permute-start.3
  32.5 0.1 iota_add_fusion
  32.6 0.1 add.204
  32.7 0.1 add.202
  32.8 0.6 gather_fusion
  33.5 43.8 %all-gather.5.cloned.1.call-done = bf16[2,1024,1024]{2,1,0:T(8,128)(2,1)} async-done(((bf16[2,128,1024]{2,1,0:T(8,128)(2,1)}), bf16[2,1024,1024]{2,1,0:T(8,128)(2,1)}) %all-gather.5.cloned.1.call-update) | async-done | bytes 4194320 | tf_op jit(solution)/shard_map/all_gather | solution.py:179
  77.3 1.1 dynamic_slice.37
  78.4 0.1 convert_bitcast_fusion.1
  78.5 2.2 slice_add_fusion.2
  80.7 1.5 copy.29
  82.2 1.5 copy.28
  83.7 0.2 compare_reduce_fusion.1
  84.0 0.9 fusion.2
  84.8 0.8 fusion.1
  85.6 16.5 %collective-permute-done.3.refs_0_ = bf16[4,8,2,24,1024]{4,3,2,1,0:T(8,128)(2,1)S(1)} collective-permute-done((bf16[4,8,2,24,1024]{4,3,2,1,0:T(8,128)(2,1)}, bf16[4,8,2,24,1024]{4,3,2,1,0:T(8,128)(2,1)S(1)}, u32[]{:S(2)}, u32[]{:S(2)}) %collective-permute-start.3) | collective-permute-done | bytes 3145760 | tf_op jit(solution)/shard_map/ppermute | solution.py:167
  102.1 1.7 copy-done.2
  103.8 8.2 %shard_map.55.refs_0_ = bf16[8,384,896]{2,1,0:T(8,128)(2,1)} custom-call(f32[8,8,256]{2,1,0:T(8,128)} %bitcast.69, f32[8,8,256]{2,1,0:T(8,128)} %bitcast.63, bf16[2048,1024]{1,0:T(8,128)(2,1)} %bitcast.56, bf16[4,8,2,24,1024]{4,3,2,1,0:T(8,128)(2,1)} %copy-done.2), custom_call_target="tpu_custom_call" | custom-call | flops 1024 | bytes 1024 | tf_op jit(solution)/shard_map/pallas_call | solution.py:39
  111.9 7.2 %all-to-all-start.1 = ((bf16[8,384,896]{2,1,0:T(8,128)(2,1)}), bf16[8,384,896]{2,1,0:T(8,128)(2,1)}, u32[]{:S(2)}, u32[]{:S(2)}) async-start(bf16[8,384,896]{2,1,0:T(8,128)(2,1)} %shard_map.55.refs_0_), calls=%async_computation.1 | async-start | bytes 11010048 | tf_op jit(solution)/shard_map/all_to_all | solution.py:188
  119.1 0.6 dynamic_slice.30.value_ref
  119.7 1.5 shard_map.56
  121.9 2.2 select_bitcast_fusion
  124.1 0.3 copy.30
  124.4 0.0 copy-start.1
  124.4 1.1 collective-permute-start.5
  125.6 2.6 collective-permute-start.4
  128.1 0.5 shard_map.57
  130.6 2.0 all-gather.3.cloned.1.call-done
  132.6 1.3 constant_dynamic-slice_fusion.2
  133.8 0.1 convert_bitcast_fusion
  133.9 2.3 slice_add_fusion
  136.2 1.5 copy.31
  137.7 0.2 compare_reduce_fusion
  138.0 0.8 fusion
  138.8 1.5 copy.32
  140.3 0.8 fusion.3
  141.1 8.1 %shard_map.58.refs_0_ = bf16[8,384,896]{2,1,0:T(8,128)(2,1)} custom-call(f32[8,8,256]{2,1,0:T(8,128)} %bitcast.68, f32[8,8,256]{2,1,0:T(8,128)} %bitcast.64, bf16[2048,1024]{1,0:T(8,128)(2,1)} %bitcast.58), custom_call_target="tpu_custom_call" | custom-call | flops 1024 | bytes 1024 | tf_op jit(solution)/shard_map/pallas_call | solution.py:39
  149.2 32.9 %all-to-all-done.1.refs_0_ = bf16[8,384,896]{2,1,0:T(8,128)(2,1)} async-done(((bf16[8,384,896]{2,1,0:T(8,128)(2,1)}), bf16[8,384,896]{2,1,0:T(8,128)(2,1)}, u32[]{:S(2)}, u32[]{:S(2)}) %all-to-all-start.1) | async-done | bytes 5505056 | tf_op jit(solution)/shard_map/all_to_all | solution.py:188
  182.1 5.4 %all-to-all-start = ((bf16[8,384,896]{2,1,0:T(8,128)(2,1)}), bf16[8,384,896]{2,1,0:T(8,128)(2,1)}, u32[]{:S(2)}, u32[]{:S(2)}) async-start(bf16[8,384,896]{2,1,0:T(8,128)(2,1)} %shard_map.58.refs_0_), calls=%async_computation | async-start | bytes 11010048 | tf_op jit(solution)/shard_map/all_to_all | solution.py:188
  187.5 0.5 shard_map.59
  191.5 3.8 %collective-permute-done.5.refs_2_ = bf16[8,192,1024]{2,1,0:T(8,128)(2,1)} collective-permute-done((bf16[8,192,1024]{2,1,0:T(8,128)(2,1)S(1)}, bf16[8,192,1024]{2,1,0:T(8,128)(2,1)}, u32[]{:S(2)}, u32[]{:S(2)}) %collective-permute-start.5) | collective-permute-done | bytes 3145760 | tf_op jit(solution)/shard_map/ppermute | solution.py:194
  195.3 1.5 constant_dynamic-slice_fusion.1
  196.8 0.1 collective-permute-start.6
  196.9 1.5 constant_dynamic-slice_fusion
  198.4 2.9 %collective-permute-start.7 = (bf16[4,192,1024]{2,1,0:T(8,128)(2,1)S(1)}, bf16[4,192,1024]{2,1,0:T(8,128)(2,1)S(1)}, u32[]{:S(2)}, u32[]{:S(2)}) collective-permute-start(bf16[4,192,1024]{2,1,0:T(8,128)(2,1)S(1)} %constant_dynamic-slice_fusion), channel_id=1, source_target_pairs={{0,192},{64,0},{128,64},{192,128},{1,193},{65,1},{129,65},{193,129... | collective-permute-start | bytes 4718600 | tf_op jit(solution)/shard_map/ppermute | solution.py:201
  201.4 10.9 %shard_map.60.refs_4_ = f32[896,1024]{1,0:T(8,128)} custom-call(bf16[8,384,896]{2,1,0:T(8,128)(2,1)} %all-to-all-done.1.refs_0_, bf16[8,192,1024]{2,1,0:T(8,128)(2,1)} %bitcast.54, bf16[8,192,1024]{2,1,0:T(8,128)(2,1)} %collective-permute-done.5.refs_2_), custom_call_target="tpu_custom_call" | custom-call | flops 1024 | bytes 1024 | tf_op jit(solution)/shard_map/pallas_call | solution.py:146
  212.2 21.7 %collective-permute-done.6.refs_2_ = bf16[4,192,1024]{2,1,0:T(8,128)(2,1)} collective-permute-done((bf16[4,192,1024]{2,1,0:T(8,128)(2,1)S(1)}, bf16[4,192,1024]{2,1,0:T(8,128)(2,1)}, u32[]{:S(2)}, u32[]{:S(2)}) %collective-permute-start.6) | collective-permute-done | bytes 1572896 | tf_op jit(solution)/shard_map/ppermute | solution.py:200
  233.9 1.2 collective-permute-done.7.refs_3_
  235.1 15.4 %all-to-all-done.refs_0_ = bf16[8,384,896]{2,1,0:T(8,128)(2,1)} async-done(((bf16[8,384,896]{2,1,0:T(8,128)(2,1)}), bf16[8,384,896]{2,1,0:T(8,128)(2,1)}, u32[]{:S(2)}, u32[]{:S(2)}) %all-to-all-start) | async-done | bytes 5505056 | tf_op jit(solution)/shard_map/all_to_all | solution.py:188
  250.5 13.3 %shard_map.61 = f32[896,1024]{1,0:T(8,128)} custom-call(bf16[8,384,896]{2,1,0:T(8,128)(2,1)} %all-to-all-done.refs_0_, bf16[8,192,1024]{2,1,0:T(8,128)(2,1)} %collective-permute-done.4.refs_1_, bf16[4,192,1024]{2,1,0:T(8,128)(2,1)} %collective-permute-done.6.refs_2_, bf16[4,192,1024]{2,1,0:T(8,128)(2,1)} %copy-done.4, f32[896,1024]{1,0:T(8,128)} %shard_map.60.refs_4_), custom_call_target="tpu_custom_call" | custom-call | flops 1024 | bytes 1024 | tf_op jit(solution)/shard_map/pallas_call | solution.py:146
  (17 shorter events, 0.1 us)
Async XLA Ops:
  6.5 70.8 %all-gather.5.cloned.1.call-start = ((), (), s32[]{:S(2)}) async-start(), calls=%async_computation.3 | async-start | bytes 4718592 | tf_op jit(solution)/shard_map/all_gather | solution.py:179
  8.1 24.7 %copy-start = (s32[64]{0:T(128)S(1)}, s32[64]{0:T(128)}, u32[]{:S(2)}) copy-start(s32[64]{0:T(128)} %param.9) | copy-start | bytes 772
  9.5 7.1 %collective-permute-start.2 = (bf16[128,1024]{1,0:T(8,128)(2,1)S(1)}, bf16[128,1024]{1,0:T(8,128)(2,1)S(1)}, u32[]{:S(2)}, u32[]{:S(2)}) collective-permute-start(bf16[128,1024]{1,0:T(8,128)(2,1)S(1)} %get-tuple-element.16), channel_id=1, source_target_pairs={{0,64},{64,128},{128,192},{192,0},{1,65},{65,129},{129,193},{193,1... | collective-permute-start | bytes 786440 | tf_op jit(solution)/shard_map/ppermute | solution.py:174
  17.6 115.0 %all-gather.3.cloned.1.call-start = ((), (), s32[]{:S(2)}) async-start(), calls=%async_computation.2 | async-start | bytes 4718592 | tf_op jit(solution)/shard_map/all_gather | solution.py:179
  17.6 13.9 %collective-permute-start = (bf16[128,1024]{1,0:T(8,128)(2,1)S(1)}, bf16[128,1024]{1,0:T(8,128)(2,1)S(1)}, u32[]{:S(2)}, u32[]{:S(2)}) collective-permute-start(bf16[128,1024]{1,0:T(8,128)(2,1)S(1)} %get-tuple-element.14), channel_id=1, source_target_pairs={{0,192},{64,0},{128,64},{192,128},{1,193},{65,1},{129,65},{193,129... | collective-permute-start | bytes 786440 | tf_op jit(solution)/shard_map/ppermute | solution.py:174
  21.1 10.5 %collective-permute-start.1 = (bf16[128,1024]{1,0:T(8,128)(2,1)S(1)}, bf16[128,1024]{1,0:T(8,128)(2,1)S(1)}, u32[]{:S(2)}, u32[]{:S(2)}) collective-permute-start(bf16[128,1024]{1,0:T(8,128)(2,1)S(1)} %get-tuple-element.15), channel_id=1, source_target_pairs={{0,128},{64,192},{128,0},{192,64},{1,129},{65,193},{129,1},{193,65... | collective-permute-start | bytes 786440 | tf_op jit(solution)/shard_map/ppermute | solution.py:174
  32.4 69.7 %collective-permute-start.3 = (bf16[4,8,2,24,1024]{4,3,2,1,0:T(8,128)(2,1)}, bf16[4,8,2,24,1024]{4,3,2,1,0:T(8,128)(2,1)S(1)}, u32[]{:S(2)}, u32[]{:S(2)}) collective-permute-start(bf16[4,8,2,24,1024]{4,3,2,1,0:T(8,128)(2,1)} %bitcast.59), channel_id=1, source_target_pairs={{0,32},{16,48},{32,0},{48,16},{1,33},{17,49},{33,1},{49,17},{2,34}... | collective-permute-start | bytes 9437192 | tf_op jit(solution)/shard_map/ppermute | solution.py:167
  102.1 1.7 copy-start.2
  111.9 70.2 %all-to-all-start.1 = ((bf16[8,384,896]{2,1,0:T(8,128)(2,1)}), bf16[8,384,896]{2,1,0:T(8,128)(2,1)}, u32[]{:S(2)}, u32[]{:S(2)}) async-start(bf16[8,384,896]{2,1,0:T(8,128)(2,1)} %shard_map.55.refs_0_), calls=%async_computation.1 | async-start | bytes 11010048 | tf_op jit(solution)/shard_map/all_to_all | solution.py:188
  119.1 2.7 %copy-start.3 = (bf16[4,8,2,24,1024]{4,3,2,1,0:T(8,128)(2,1)S(1)}, bf16[4,8,2,24,1024]{4,3,2,1,0:T(8,128)(2,1)}, u32[]{:S(2)}) copy-start(bf16[4,8,2,24,1024]{4,3,2,1,0:T(8,128)(2,1)} %copy-done.2) | copy-start | bytes 9437188
  124.4 3.7 %copy-start.1 = (bf16[4,2,8,24,1024]{4,3,2,1,0:T(8,128)(2,1)}, bf16[4,2,8,24,1024]{4,3,2,1,0:T(8,128)(2,1)S(1)}, u32[]{:S(2)}) copy-start(bf16[4,2,8,24,1024]{4,3,2,1,0:T(8,128)(2,1)S(1)} %copy.30) | copy-start | bytes 9437188
  124.4 70.8 %collective-permute-start.5 = (bf16[8,192,1024]{2,1,0:T(8,128)(2,1)S(1)}, bf16[8,192,1024]{2,1,0:T(8,128)(2,1)}, u32[]{:S(2)}, u32[]{:S(2)}) collective-permute-start(bf16[8,192,1024]{2,1,0:T(8,128)(2,1)S(1)} %bitcast.51), channel_id=1, source_target_pairs={{0,64},{64,128},{128,192},{192,0},{1,65},{65,129},{129,193},{193,1... | collective-permute-start | bytes 9437192 | tf_op jit(solution)/shard_map/ppermute | solution.py:194
  125.6 71.3 %collective-permute-start.4 = (bf16[8,192,1024]{2,1,0:T(8,128)(2,1)S(1)}, bf16[8,192,1024]{2,1,0:T(8,128)(2,1)}, u32[]{:S(2)}, u32[]{:S(2)}) collective-permute-start(bf16[8,192,1024]{2,1,0:T(8,128)(2,1)S(1)} %bitcast.52), channel_id=1, source_target_pairs={{0,192},{64,0},{128,64},{192,128},{1,193},{65,1},{129,65},{193,129... | collective-permute-start | bytes 9437192 | tf_op jit(solution)/shard_map/ppermute | solution.py:195
  182.1 68.4 %all-to-all-start = ((bf16[8,384,896]{2,1,0:T(8,128)(2,1)}), bf16[8,384,896]{2,1,0:T(8,128)(2,1)}, u32[]{:S(2)}, u32[]{:S(2)}) async-start(bf16[8,384,896]{2,1,0:T(8,128)(2,1)} %shard_map.58.refs_0_), calls=%async_computation | async-start | bytes 11010048 | tf_op jit(solution)/shard_map/all_to_all | solution.py:188
  196.8 37.1 %collective-permute-start.6 = (bf16[4,192,1024]{2,1,0:T(8,128)(2,1)S(1)}, bf16[4,192,1024]{2,1,0:T(8,128)(2,1)}, u32[]{:S(2)}, u32[]{:S(2)}) collective-permute-start(bf16[4,192,1024]{2,1,0:T(8,128)(2,1)S(1)} %constant_dynamic-slice_fusion.1), channel_id=1, source_target_pairs={{0,64},{64,128},{128,192},{192,0},{1,65},{65,129},{129,193},{193,1... | collective-permute-start | bytes 4718600 | tf_op jit(solution)/shard_map/ppermute | solution.py:200
  198.4 36.7 %collective-permute-start.7 = (bf16[4,192,1024]{2,1,0:T(8,128)(2,1)S(1)}, bf16[4,192,1024]{2,1,0:T(8,128)(2,1)S(1)}, u32[]{:S(2)}, u32[]{:S(2)}) collective-permute-start(bf16[4,192,1024]{2,1,0:T(8,128)(2,1)S(1)} %constant_dynamic-slice_fusion), channel_id=1, source_target_pairs={{0,192},{64,0},{128,64},{192,128},{1,193},{65,1},{129,65},{193,129... | collective-permute-start | bytes 4718600 | tf_op jit(solution)/shard_map/ppermute | solution.py:201
  235.1 15.4 %copy-start.4 = (bf16[4,192,1024]{2,1,0:T(8,128)(2,1)}, bf16[4,192,1024]{2,1,0:T(8,128)(2,1)S(1)}, u32[]{:S(2)}) copy-start(bf16[4,192,1024]{2,1,0:T(8,128)(2,1)S(1)} %collective-permute-done.7.refs_3_) | copy-start | bytes 4718596
Sparse Core Ops, SparseCore 0:
  17.7 59.5 all-gather.4
  79.1 53.4 all-gather.2
where the time goes:
time: 272 us; the launch traced here: 271 us
  waiting for transfers between devices  152 us (56%)
  Pallas kernels  42.9 us (16%)
  starting transfers between devices  25.4 us (9%)
  between operations  19.6 us (7%)
  local copies, waits for them, and re-layouts  16.4 us (6%)
  other arithmetic  12.4 us (5%)
    all_to_all x2, waiting for transfers between devices, exchange(): return (rows, lax.all_to_all(rows, ('y', 'c'), 0, 0, tiled=True))  48.3 us
    all_gather x2, waiting for transfers between devices, local(): lax.all_gather(block, 'z', axis=1, tiled=True).reshape(-1, cols + META)  45.9 us
    pallas_call x2, Pallas kernels, product(): pl.pallas_call(functools.partial(product_kernel, tuple(spans)), grid=(sen...  24.2 us
    ppermute x1, waiting for transfers between devices, local(): lax.ppermute(lax.dynamic_slice_in_dim(left, start, half), 'x', ring(NX, 1))  21.7 us
    ppermute x1, waiting for transfers between devices, local(): traded = lax.ppermute(hidden, 'y', ring(NY, 2))  16.5 us
    pallas_call x2, Pallas kernels, dispatch(): pl.pallas_call(dispatch_kernel, grid=(pairs,), in_specs=[pl.BlockSpec((1,...  16.3 us
    ppermute x3, waiting for transfers between devices, columns(): return part if step == 0 else lax.ppermute(part, 'x', ring(NX, step))  15.1 us
    all_to_all x2, starting transfers between devices, exchange(): return (rows, lax.all_to_all(rows, ('y', 'c'), 0, 0, tiled=True))  12.6 us
  transfers between devices with their start and end apart: 12, of which 10 were waited for; matrix products, arithmetic and copies ran while one was open for 9% of the time, Pallas kernels for 11%

commit v1 on v0

--- a/solution.py
+++ b/solution.py
@@ -8,7 +8,7 @@
 from jax.sharding import Mesh, PartitionSpec as P
 
 NX, NY, NZ, NC = 4, 4, 8, 2
-GATHERS = ((0, 1), (3, 2))
+GATHERS = ((0,), (1, 3), (2,))
 SPACE = 56 * 1024 * 1024
 PARTS = 3
 META = 128
@@ -187,7 +187,7 @@
         rows = dispatch(*pick, tokens, cols, capacity, after)
         return rows, lax.all_to_all(rows, ("y", "c"), 0, 0, tiled=True)
 
-    rows0, arrived0 = exchange(gathered[0], cols, (traded,))
+    rows0, arrived0 = exchange(gathered[0], cols)
     flag = later(flag_here, rows0)
     own = jnp.where(flag == 1, traded, hidden).transpose(0, 2, 1, 3, 4)
     own = own.reshape(NY * NC, NZ * capacity, width)
@@ -200,8 +200,10 @@
         lax.ppermute(lax.dynamic_slice_in_dim(left, start, half), "x", ring(NX, 1)),
         lax.ppermute(lax.dynamic_slice_in_dim(right, start + half, half), "x", ring(NX, 3)),
     ]
-    total = product(None, arrived0, [[own], [left]])
-    total = product(total, arrived1, [[right], far])
+    total = product(None, arrived0, [[own]])
+    rows2, arrived2 = exchange(gathered[2], later(cols, rows1, total))
+    total = product(total, arrived1, [[left], [right]])
+    total = product(total, arrived2, [far])
     return total[None]
 
 

time: 272 us -> 263 us (0.967)
  waiting for transfers between devices: 152 us -> 123 us
  starting transfers between devices: 25.4 us -> 34.7 us
  Pallas kernels: 42.9 us -> 48.6 us
    all_to_all x2 -> x3, waiting for transfers between devices: 48.3 us -> 9.47 us  [exchange(): return (rows, lax.all_to_all(rows, ('y', 'c'), 0, 0, tiled=True))]
    all_gather x2 -> x3, waiting for transfers between devices: 45.9 us -> 68.2 us  [local(): lax.all_gather(block, 'z', axis=1, tiled=True).reshape(-1, cols + META)]
    ppermute x1, waiting for transfers between devices: 1.23 us -> 18.4 us  [local(): lax.ppermute(lax.dynamic_slice_in_dim(right, start + half, half), 'x', ri...]
    ppermute x1, waiting for transfers between devices: 21.7 us -> 4.96 us  [local(): lax.ppermute(lax.dynamic_slice_in_dim(left, start, half), 'x', ring(NX, 1))]
    ppermute x3, waiting for transfers between devices: 15.1 us -> 5.37 us  [columns(): return part if step == 0 else lax.ppermute(part, 'x', ring(NX, step))]
    all_to_all x2 -> x3, starting transfers between devices: 12.6 us -> 19.7 us  [exchange(): return (rows, lax.all_to_all(rows, ('y', 'c'), 0, 0, tiled=True))]
    pallas_call x2 -> x3, Pallas kernels: 24.2 us -> 28.4 us  [product(): pl.pallas_call(functools.partial(product_kernel, tuple(spans)), grid=(sen...]
    ppermute x1, waiting for transfers between devices: 3.79 us -> 0.01 us  [local(): left = lax.ppermute(own, 'x', ring(NX, 1))]
  transfers between devices with their start and end apart: 12 -> 14, of which waited for: 10 -> 9; matrix products, arithmetic and copies ran while one was open for 9% -> 11% of each run, Pallas kernels for 11% -> 15%
where the time goes in v1:
time: 263 us; the launch traced here: 261 us
  waiting for transfers between devices  123 us (47%)
  Pallas kernels  48.6 us (18%)
  starting transfers between devices  34.7 us (13%)
  between operations  20.9 us (8%)
  local copies, waits for them, and re-layouts  19.1 us (7%)
  other arithmetic  12.3 us (5%)
    all_gather x3, waiting for transfers between devices, local(): lax.all_gather(block, 'z', axis=1, tiled=True).reshape(-1, cols + META)  68.2 us
    pallas_call x3, Pallas kernels, product(): pl.pallas_call(functools.partial(product_kernel, tuple(spans)), grid=(sen...  28.4 us
    all_to_all x3, starting transfers between devices, exchange(): return (rows, lax.all_to_all(rows, ('y', 'c'), 0, 0, tiled=True))  19.7 us
    ppermute x1, waiting for transfers between devices, local(): lax.ppermute(lax.dynamic_slice_in_dim(right, start + half, half), 'x', ri...  18.4 us
    pallas_call x3, Pallas kernels, dispatch(): pl.pallas_call(dispatch_kernel, grid=(pairs,), in_specs=[pl.BlockSpec((1,...  17.5 us
    ppermute x1, waiting for transfers between devices, local(): traded = lax.ppermute(hidden, 'y', ring(NY, 2))  15.9 us
    all_to_all x3, waiting for transfers between devices, exchange(): return (rows, lax.all_to_all(rows, ('y', 'c'), 0, 0, tiled=True))  9.47 us
    ppermute x3, starting transfers between devices, columns(): return part if step == 0 else lax.ppermute(part, 'x', ring(NX, step))  5.98 us
  transfers between devices with their start and end apart: 14, of which 9 were waited for; matrix products, arithmetic and copies ran while one was open for 11% of the time, Pallas kernels for 15%

profile of v1, /device:TPU:1, one launch (start us, length us, event | category | flops | bytes accessed | tf_op | source)
XLA Modules:
  0.0 260.9 jit_solution(9994160250702982116)
XLA Ops:
  6.5 0.8 convert_convert_fusion
  7.4 0.8 reduce-precision_convert_fusion.1
  8.2 0.1 copy.37
  8.3 1.4 constant_dynamic-slice_fusion.4
  9.7 0.9 fusion.10
  10.7 2.1 collective-permute-start.1
  12.8 1.4 collective-permute-start.2
  14.2 3.9 %collective-permute-done.1 = bf16[128,1024]{1,0:T(8,128)(2,1)S(1)} collective-permute-done((bf16[128,1024]{1,0:T(8,128)(2,1)}, bf16[128,1024]{1,0:T(8,128)(2,1)S(1)}, u32[]{:S(2)}, u32[]{:S(2)}) %collective-permute-start.1) | collective-permute-done | bytes 262176 | tf_op jit(solution)/shard_map/ppermute | solution.py:174
  18.1 1.5 collective-permute-done.2
  19.5 0.9 pad_maximum_fusion
  20.4 2.1 copy.40
  22.5 3.6 %collective-permute-start.3 = (bf16[4,8,2,24,1024]{4,3,1,2,0:T(8,128)(2,1)}, bf16[4,8,2,24,1024]{4,3,1,2,0:T(8,128)(2,1)}, u32[]{:S(2)}, u32[]{:S(2)}) collective-permute-start(bf16[4,8,2,24,1024]{4,3,1,2,0:T(8,128)(2,1)} %copy.40), channel_id=1, source_target_pairs={{0,32},{16,48},{32,0},{48,16},{1,33},{17,49},{33,1},{49,17},{2,34}... | collective-permute-start | bytes 9437192 | tf_op jit(solution)/shard_map/ppermute | solution.py:167
  26.4 0.6 gather_fusion
  27.0 25.0 %all-gather.10.cloned.1.call-done.token_ref = bf16[1024,1024]{1,0:T(8,128)(2,1)} async-done(((bf16[128,1024]{1,0:T(8,128)(2,1)}), bf16[1024,1024]{1,0:T(8,128)(2,1)}) %all-gather.10.cloned.1.call-update) | async-done | bytes 2097168 | tf_op jit(solution)/shard_map/all_gather | solution.py:179
  52.0 1.0 dynamic_slice.41
  53.0 1.4 slice_add_fusion.4
  54.4 1.2 copy.39
  55.6 1.2 copy.38
  56.8 0.2 compare_reduce_fusion.2
  57.0 0.8 fusion.5
  57.8 0.8 fusion.2
  58.5 4.7 %shard_map.55.refs_0_ = bf16[8,192,896]{2,1,0:T(8,128)(2,1)} custom-call(f32[4,8,256]{2,1,0:T(8,128)} %bitcast.82, f32[4,8,256]{2,1,0:T(8,128)} %bitcast.79, bf16[1024,1024]{1,0:T(8,128)(2,1)} %all-gather.10.cloned.1.call-done.token_ref), custom_call_target="tpu_custom_call" | custom-call | flops 1024 | bytes 1024 | tf_op jit(solution)/shard_map/pallas_call | solution.py:39
  63.3 8.8 %all-to-all-start = ((bf16[8,192,896]{2,1,0:T(8,128)(2,1)}), bf16[8,192,896]{2,1,0:T(8,128)(2,1)}, u32[]{:S(2)}, u32[]{:S(2)}) async-start(bf16[8,192,896]{2,1,0:T(8,128)(2,1)} %shard_map.55.refs_0_), calls=%async_computation | async-start | bytes 5505024 | tf_op jit(solution)/shard_map/all_to_all | solution.py:188
  72.1 2.5 collective-permute-start
  74.6 0.6 dynamic_slice.34.value_ref
  75.2 1.1 shard_map.56
  77.0 15.9 %collective-permute-done.3 = bf16[4,8,2,24,1024]{4,3,1,2,0:T(8,128)(2,1)} collective-permute-done((bf16[4,8,2,24,1024]{4,3,1,2,0:T(8,128)(2,1)}, bf16[4,8,2,24,1024]{4,3,1,2,0:T(8,128)(2,1)}, u32[]{:S(2)}, u32[]{:S(2)}) %collective-permute-start.3) | collective-permute-done | bytes 3145760 | tf_op jit(solution)/shard_map/ppermute | solution.py:167
  92.9 2.0 broadcast_select_fusion
  94.9 0.5 shard_map.57
  97.4 13.7 %all-gather.6.cloned.1.call-done = bf16[2,1024,1024]{2,1,0:T(8,128)(2,1)} async-done(((bf16[2,128,1024]{2,1,0:T(8,128)(2,1)}), bf16[2,1024,1024]{2,1,0:T(8,128)(2,1)}) %all-gather.6.cloned.1.call-update) | async-done | bytes 4194320 | tf_op jit(solution)/shard_map/all_gather | solution.py:179
  111.1 1.3 constant_dynamic-slice_fusion.3
  112.3 0.1 convert_bitcast_fusion
  112.4 0.9 slice_add_fusion
  113.3 0.3 copy.43
  113.6 0.3 copy.42
  113.9 0.2 compare_reduce_fusion
  114.2 0.8 fusion.3
  115.0 0.8 fusion
  115.8 8.1 %shard_map.58.refs_0_ = bf16[8,384,896]{2,1,0:T(8,128)(2,1)} custom-call(f32[8,8,256]{2,1,0:T(8,128)} %bitcast.80, f32[8,8,256]{2,1,0:T(8,128)} %bitcast.75, bf16[2048,1024]{1,0:T(8,128)(2,1)} %bitcast.71), custom_call_target="tpu_custom_call" | custom-call | flops 1024 | bytes 1024 | tf_op jit(solution)/shard_map/pallas_call | solution.py:39
  124.0 5.7 %all-to-all-start.2 = ((bf16[8,384,896]{2,1,0:T(8,128)(2,1)}), bf16[8,384,896]{2,1,0:T(8,128)(2,1)}, u32[]{:S(2)}, u32[]{:S(2)}) async-start(bf16[8,384,896]{2,1,0:T(8,128)(2,1)} %shard_map.58.refs_0_), calls=%async_computation.2 | async-start | bytes 11010048 | tf_op jit(solution)/shard_map/all_to_all | solution.py:188
  129.7 0.7 all-gather.8.cloned.1.call-update
  130.4 2.4 collective-permute-start.6
  132.8 7.2 %shard_map.59.refs_1_.refs_3_ = f32[896,1024]{1,0:T(8,128)} custom-call(bf16[8,192,896]{2,1,0:T(8,128)(2,1)} %all-to-all-done.refs_0_, bf16[8,192,1024]{2,1,0:T(8,128)(2,1)} %bitcast.65), custom_call_target="tpu_custom_call" | custom-call | flops 1024 | bytes 1024 | tf_op jit(solution)/shard_map/pallas_call | solution.py:146
  140.0 0.5 shard_map.60
  142.4 29.5 %all-gather.8.cloned.1.call-done.token_ref = bf16[1024,1024]{1,0:T(8,128)(2,1)} async-done(((bf16[128,1024]{1,0:T(8,128)(2,1)}), bf16[1024,1024]{1,0:T(8,128)(2,1)}) %all-gather.8.cloned.1.call-update) | async-done | bytes 2097168 | tf_op jit(solution)/shard_map/all_gather | solution.py:179
  171.9 1.1 constant_dynamic-slice_fusion.2
  173.1 1.4 slice_add_fusion.2
  174.5 1.2 copy.45
  175.7 1.2 copy.44
  176.9 0.2 compare_reduce_fusion.1
  177.0 0.8 fusion.6
  177.8 0.7 fusion.1
  178.5 4.6 %shard_map.61 = bf16[8,192,896]{2,1,0:T(8,128)(2,1)} custom-call(f32[4,8,256]{2,1,0:T(8,128)} %bitcast.81, f32[4,8,256]{2,1,0:T(8,128)} %bitcast.78, bf16[1024,1024]{1,0:T(8,128)(2,1)} %all-gather.8.cloned.1.call-done.token_ref), custom_call_target="tpu_custom_call" | custom-call | flops 1024 | bytes 1024 | tf_op jit(solution)/shard_map/pallas_call | solution.py:39
  183.2 9.5 %all-to-all-done.2.refs_0_ = bf16[8,384,896]{2,1,0:T(8,128)(2,1)} async-done(((bf16[8,384,896]{2,1,0:T(8,128)(2,1)}), bf16[8,384,896]{2,1,0:T(8,128)(2,1)}, u32[]{:S(2)}, u32[]{:S(2)}) %all-to-all-start.2) | async-done | bytes 5505056 | tf_op jit(solution)/shard_map/all_to_all | solution.py:188
  192.7 5.2 %all-to-all-start.1 = ((bf16[8,192,896]{2,1,0:T(8,128)(2,1)}), bf16[8,192,896]{2,1,0:T(8,128)(2,1)}, u32[]{:S(2)}, u32[]{:S(2)}) async-start(bf16[8,192,896]{2,1,0:T(8,128)(2,1)} %shard_map.61), calls=%async_computation.1 | async-start | bytes 5505024 | tf_op jit(solution)/shard_map/all_to_all | solution.py:188
  197.8 0.5 shard_map.62
  200.9 2.7 %constant_dynamic-slice_fusion = bf16[4,192,1024]{2,1,0:T(8,128)(2,1)} fusion(bf16[8,192,1024]{2,1,0:T(8,128)(2,1)} %collective-permute-done.6.refs_2_, s32[]{:T(128)S(6)} %select_n.171), kind=kLoop, calls=%fused_computation.49 | loop fusion | bytes 3145732 | tf_op jit(solution)/shard_map/dynamic_slice | solution.py:201
  203.5 2.9 %collective-permute-start.7 = (bf16[4,192,1024]{2,1,0:T(8,128)(2,1)}, bf16[4,192,1024]{2,1,0:T(8,128)(2,1)}, u32[]{:S(2)}, u32[]{:S(2)}) collective-permute-start(bf16[4,192,1024]{2,1,0:T(8,128)(2,1)} %constant_dynamic-slice_fusion), channel_id=1, source_target_pairs={{0,192},{64,0},{128,64},{192,128},{1,193},{65,1},{129,65},{193,129... | collective-permute-start | bytes 4718600 | tf_op jit(solution)/shard_map/ppermute | solution.py:201
  207.0 1.5 constant_dynamic-slice_fusion.1
  208.6 12.5 %shard_map.63.refs_3_ = f32[896,1024]{1,0:T(8,128)} custom-call(bf16[8,384,896]{2,1,0:T(8,128)(2,1)} %all-to-all-done.2.refs_0_, bf16[8,192,1024]{2,1,0:T(8,128)(2,1)} %collective-permute-done.4.refs_1_, bf16[8,192,1024]{2,1,0:T(8,128)(2,1)} %collective-permute-done.6.refs_2_, f32[896,1024]{1,0:T(8,128)} %shard_map.59.refs_1_.refs_3_), custom_call_target="tpu_custom_call" | custom-call | flops 1024 | bytes 1024 | tf_op jit(solution)/shard_map/pallas_call | solution.py:146
  221.1 18.4 %collective-permute-done.7.refs_2_ = bf16[4,192,1024]{2,1,0:T(8,128)(2,1)} collective-permute-done((bf16[4,192,1024]{2,1,0:T(8,128)(2,1)}, bf16[4,192,1024]{2,1,0:T(8,128)(2,1)}, u32[]{:S(2)}, u32[]{:S(2)}) %collective-permute-start.7) | collective-permute-done | bytes 1572896 | tf_op jit(solution)/shard_map/ppermute | solution.py:201
  239.5 5.0 %collective-permute-done.5.refs_1_ = bf16[4,192,1024]{2,1,0:T(8,128)(2,1)S(1)} collective-permute-done((bf16[4,192,1024]{2,1,0:T(8,128)(2,1)S(1)}, bf16[4,192,1024]{2,1,0:T(8,128)(2,1)S(1)}, u32[]{:S(2)}, u32[]{:S(2)}) %collective-permute-start.5) | collective-permute-done | bytes 1572896 | tf_op jit(solution)/shard_map/ppermute | solution.py:200
  244.5 1.2 copy-done.3
  245.7 8.8 %shard_map.64 = f32[896,1024]{1,0:T(8,128)} custom-call(bf16[8,192,896]{2,1,0:T(8,128)(2,1)} %all-to-all-done.1.refs_0_, bf16[4,192,1024]{2,1,0:T(8,128)(2,1)} %copy-done.3, bf16[4,192,1024]{2,1,0:T(8,128)(2,1)} %collective-permute-done.7.refs_2_, f32[896,1024]{1,0:T(8,128)} %shard_map.63.refs_3_), custom_call_target="tpu_custom_call" | custom-call | flops 1024 | bytes 1024 | tf_op jit(solution)/shard_map/pallas_call | solution.py:146
  (30 shorter events, 0.5 us)
Async XLA Ops:
  6.5 13.9 %copy-start.2 = (bf16[1,1,64,24,1024]{4,3,2,1,0:T(8,128)(2,1)S(1)}, bf16[1,1,64,24,1024]{4,3,2,1,0:T(8,128)(2,1)}, u32[]{:S(2)}) copy-start(bf16[1,1,64,24,1024]{4,3,2,1,0:T(8,128)(2,1)} %param.8) | copy-start | bytes 9437188
  6.5 45.5 %all-gather.10.cloned.1.call-start = ((), (), s32[]{:S(2)}) async-start(), calls=%async_computation.5 | async-start | bytes 2359296 | tf_op jit(solution)/shard_map/all_gather | solution.py:179
  10.6 100.4 %all-gather.6.cloned.1.call-start = ((), (), s32[]{:S(2)}) async-start(), calls=%async_computation.3 | async-start | bytes 4718592 | tf_op jit(solution)/shard_map/all_gather | solution.py:179
  10.7 7.4 %collective-permute-start.1 = (bf16[128,1024]{1,0:T(8,128)(2,1)}, bf16[128,1024]{1,0:T(8,128)(2,1)S(1)}, u32[]{:S(2)}, u32[]{:S(2)}) collective-permute-start(bf16[128,1024]{1,0:T(8,128)(2,1)} %get-tuple-element.17), channel_id=1, source_target_pairs={{0,64},{64,128},{128,192},{192,0},{1,65},{65,129},{129,193},{193,1... | collective-permute-start | bytes 786440 | tf_op jit(solution)/shard_map/ppermute | solution.py:174
  12.8 6.7 %collective-permute-start.2 = (bf16[128,1024]{1,0:T(8,128)(2,1)}, bf16[128,1024]{1,0:T(8,128)(2,1)S(1)}, u32[]{:S(2)}, u32[]{:S(2)}) collective-permute-start(bf16[128,1024]{1,0:T(8,128)(2,1)} %get-tuple-element.18), channel_id=1, source_target_pairs={{0,192},{64,0},{128,64},{192,128},{1,193},{65,1},{129,65},{193,129... | collective-permute-start | bytes 786440 | tf_op jit(solution)/shard_map/ppermute | solution.py:174
  20.4 5.9 %copy-start = (s32[64]{0:T(128)S(1)}, s32[64]{0:T(128)}, u32[]{:S(2)}) copy-start(s32[64]{0:T(128)} %param.9) | copy-start | bytes 772
  22.5 70.4 %collective-permute-start.3 = (bf16[4,8,2,24,1024]{4,3,1,2,0:T(8,128)(2,1)}, bf16[4,8,2,24,1024]{4,3,1,2,0:T(8,128)(2,1)}, u32[]{:S(2)}, u32[]{:S(2)}) collective-permute-start(bf16[4,8,2,24,1024]{4,3,1,2,0:T(8,128)(2,1)} %copy.40), channel_id=1, source_target_pairs={{0,32},{16,48},{32,0},{48,16},{1,33},{17,49},{33,1},{49,17},{2,34}... | collective-permute-start | bytes 9437192 | tf_op jit(solution)/shard_map/ppermute | solution.py:167
  63.3 60.7 %all-to-all-start = ((bf16[8,192,896]{2,1,0:T(8,128)(2,1)}), bf16[8,192,896]{2,1,0:T(8,128)(2,1)}, u32[]{:S(2)}, u32[]{:S(2)}) async-start(bf16[8,192,896]{2,1,0:T(8,128)(2,1)} %shard_map.55.refs_0_), calls=%async_computation | async-start | bytes 5505024 | tf_op jit(solution)/shard_map/all_to_all | solution.py:188
  72.1 57.6 %collective-permute-start = (bf16[128,1024]{1,0:T(8,128)(2,1)S(1)}, bf16[128,1024]{1,0:T(8,128)(2,1)}, u32[]{:S(2)}, u32[]{:S(2)}) collective-permute-start(bf16[128,1024]{1,0:T(8,128)(2,1)S(1)} %get-tuple-element.16), channel_id=1, source_target_pairs={{0,128},{64,192},{128,0},{192,64},{1,129},{65,193},{129,1},{193,65... | collective-permute-start | bytes 786440 | tf_op jit(solution)/shard_map/ppermute | solution.py:174
  124.0 6.4 %copy-start.1 = (bf16[4,8,2,24,1024]{4,3,1,2,0:T(8,128)(2,1)S(1)}, bf16[4,8,2,24,1024]{4,3,1,2,0:T(8,128)(2,1)}, u32[]{:S(2)}) copy-start(bf16[4,8,2,24,1024]{4,3,1,2,0:T(8,128)(2,1)} %broadcast_select_fusion) | copy-start | bytes 9437188
  124.0 68.7 %all-to-all-start.2 = ((bf16[8,384,896]{2,1,0:T(8,128)(2,1)}), bf16[8,384,896]{2,1,0:T(8,128)(2,1)}, u32[]{:S(2)}, u32[]{:S(2)}) async-start(bf16[8,384,896]{2,1,0:T(8,128)(2,1)} %shard_map.58.refs_0_), calls=%async_computation.2 | async-start | bytes 11010048 | tf_op jit(solution)/shard_map/all_to_all | solution.py:188
  129.7 42.2 %all-gather.8.cloned.1.call-start = ((), (), s32[]{:S(2)}) async-start(), calls=%async_computation.4 | async-start | bytes 2359296 | tf_op jit(solution)/shard_map/all_gather | solution.py:179
  130.4 70.4 %collective-permute-start.6 = (bf16[8,192,1024]{2,1,0:T(8,128)(2,1)S(1)}, bf16[8,192,1024]{2,1,0:T(8,128)(2,1)}, u32[]{:S(2)}, u32[]{:S(2)}) collective-permute-start(bf16[8,192,1024]{2,1,0:T(8,128)(2,1)S(1)} %bitcast.66), channel_id=1, source_target_pairs={{0,192},{64,0},{128,64},{192,128},{1,193},{65,1},{129,65},{193,129... | collective-permute-start | bytes 9437192 | tf_op jit(solution)/shard_map/ppermute | solution.py:195
  132.8 74.2 %collective-permute-start.4 = (bf16[8,192,1024]{2,1,0:T(8,128)(2,1)S(1)}, bf16[8,192,1024]{2,1,0:T(8,128)(2,1)}, u32[]{:S(2)}, u32[]{:S(2)}) collective-permute-start(bf16[8,192,1024]{2,1,0:T(8,128)(2,1)S(1)} %bitcast.67), channel_id=1, source_target_pairs={{0,64},{64,128},{128,192},{192,0},{1,65},{65,129},{129,193},{193,1... | collective-permute-start | bytes 9437192 | tf_op jit(solution)/shard_map/ppermute | solution.py:194
  192.7 51.8 %all-to-all-start.1 = ((bf16[8,192,896]{2,1,0:T(8,128)(2,1)}), bf16[8,192,896]{2,1,0:T(8,128)(2,1)}, u32[]{:S(2)}, u32[]{:S(2)}) async-start(bf16[8,192,896]{2,1,0:T(8,128)(2,1)} %shard_map.61), calls=%async_computation.1 | async-start | bytes 5505024 | tf_op jit(solution)/shard_map/all_to_all | solution.py:188
  203.5 36.0 %collective-permute-start.7 = (bf16[4,192,1024]{2,1,0:T(8,128)(2,1)}, bf16[4,192,1024]{2,1,0:T(8,128)(2,1)}, u32[]{:S(2)}, u32[]{:S(2)}) collective-permute-start(bf16[4,192,1024]{2,1,0:T(8,128)(2,1)} %constant_dynamic-slice_fusion), channel_id=1, source_target_pairs={{0,192},{64,0},{128,64},{192,128},{1,193},{65,1},{129,65},{193,129... | collective-permute-start | bytes 4718600 | tf_op jit(solution)/shard_map/ppermute | solution.py:201
  208.5 35.9 %collective-permute-start.5 = (bf16[4,192,1024]{2,1,0:T(8,128)(2,1)S(1)}, bf16[4,192,1024]{2,1,0:T(8,128)(2,1)S(1)}, u32[]{:S(2)}, u32[]{:S(2)}) collective-permute-start(bf16[4,192,1024]{2,1,0:T(8,128)(2,1)S(1)} %constant_dynamic-slice_fusion.1), channel_id=1, source_target_pairs={{0,64},{64,128},{128,192},{192,0},{1,65},{65,129},{129,193},{193,1... | collective-permute-start | bytes 4718600 | tf_op jit(solution)/shard_map/ppermute | solution.py:200
  244.5 1.2 copy-start.3
Sparse Core Ops, SparseCore 0:
  10.8 41.1 all-gather.9
  53.8 57.2 all-gather.5
  132.3 39.5 all-gather.7

commit v2 on v1

--- a/solution.py
+++ b/solution.py
@@ -12,6 +12,7 @@
 SPACE = 56 * 1024 * 1024
 PARTS = 3
 META = 128
+HEAVY = pl.CostEstimate(flops=2 * 10**11, bytes_accessed=10**8, transcendentals=0)
 LIGHT = pl.CostEstimate(flops=1024, bytes_accessed=1024, transcendentals=0)
 
 
@@ -66,6 +67,18 @@
     )(jnp.asarray(value, jnp.int32).reshape(1), *after)[0]
 
 
+def tied(value, *after):
+    place = pl.BlockSpec(memory_space=pl.ANY)
+    return pl.pallas_call(
+        lambda *refs: None,
+        in_specs=[place] * (1 + len(after)),
+        out_specs=place,
+        out_shape=jax.ShapeDtypeStruct(value.shape, value.dtype),
+        input_output_aliases={0: 0},
+        cost_estimate=LIGHT,
+    )(value, *after)
+
+
 def ring(size, step):
     return [(i, (i + step) % size) for i in range(size)]
 
@@ -101,13 +114,13 @@
     return paired(target), paired(gate)
 
 
-def product_kernel(spans, *refs):
+def product_kernel(spans, summed, *refs):
     rows_ref, states, out_ref = refs[0], refs[1 : 1 + len(spans)], refs[-1]
     step = pl.program_id(0)
 
     @pl.when(step == 0)
     def _():
-        out_ref[...] = refs[-2][...] if len(refs) > len(spans) + 2 else jnp.zeros_like(out_ref)
+        out_ref[...] = refs[1 + len(spans)][...] if summed else jnp.zeros_like(out_ref)
 
     depth, width = states[0].shape[1:]
 
@@ -124,7 +137,7 @@
         pl.when((step >= low) & (step < high))(functools.partial(add, chunk, states_ref))
 
 
-def product(total, rows, states):
+def product(total, rows, states, after=(), cost=None):
     senders, _, cols = rows.shape
     group = senders // 2
     depth, width = states[0][0].shape[1:]
@@ -144,16 +157,17 @@
             )
             low += count
     return pl.pallas_call(
-        functools.partial(product_kernel, tuple(spans)),
+        functools.partial(product_kernel, tuple(spans), total is not None),
         grid=(senders // group,),
         in_specs=[pl.BlockSpec((group,) + rows.shape[1:], lambda i: (i, 0, 0))]
         + specs
-        + ([] if total is None else [whole]),
+        + ([] if total is None else [whole])
+        + [pl.BlockSpec(memory_space=pl.ANY)] * len(after),
         out_specs=whole,
         out_shape=jax.ShapeDtypeStruct((cols, width), jnp.float32),
         compiler_params=pltpu.CompilerParams(vmem_limit_bytes=SPACE),
-        cost_estimate=LIGHT,
-    )(rows, *arrays, *([] if total is None else [total]))
+        cost_estimate=cost or LIGHT,
+    )(rows, *arrays, *([] if total is None else [total]), *after)
 
 
 def local(grad_out, expert_ids, gate_weights, hidden_saved, swap_flags):
@@ -173,10 +187,12 @@
         part = jnp.concatenate([part, meta], axis=1)
         return part if step == 0 else lax.ppermute(part, "x", ring(NX, step))
 
-    gathered = []
-    for group in GATHERS:
+    def gather(group, after=()):
         block = jnp.stack([columns(s) for s in group])
-        gathered.append(lax.all_gather(block, "z", axis=1, tiled=True).reshape(-1, cols + META))
+        block = tied(block, *after) if after else block
+        return lax.all_gather(block, "z", axis=1, tiled=True).reshape(-1, cols + META)
+
+    gathered = [gather(group) for group in GATHERS[:2]]
 
     devices = ((jnp.arange(NY)[:, None] * NZ + z) * NC + jnp.arange(NC)[None]).reshape(-1)
     flags = jnp.take(swap_flags, devices)
@@ -191,18 +207,17 @@
     flag = later(flag_here, rows0)
     own = jnp.where(flag == 1, traded, hidden).transpose(0, 2, 1, 3, 4)
     own = own.reshape(NY * NC, NZ * capacity, width)
-    left = lax.ppermute(own, "x", ring(NX, 1))
-    right = lax.ppermute(own, "x", ring(NX, 3))
-    rows1, arrived1 = exchange(gathered[1], later(cols, own))
     half = own.shape[0] // 2
-    start = later(0, rows1)
-    far = [
-        lax.ppermute(lax.dynamic_slice_in_dim(left, start, half), "x", ring(NX, 1)),
-        lax.ppermute(lax.dynamic_slice_in_dim(right, start + half, half), "x", ring(NX, 3)),
-    ]
-    total = product(None, arrived0, [[own]])
+    own = [own[:half], own[half:]]
+    left0, right1 = lax.ppermute(own[0], "x", ring(NX, 1)), lax.ppermute(own[1], "x", ring(NX, 3))
+    left1, right0 = lax.ppermute(own[1], "x", ring(NX, 1)), lax.ppermute(own[0], "x", ring(NX, 3))
+    gathered.append(gather(GATHERS[2], (left0, right1)))
+    rows1, arrived1 = exchange(gathered[1], later(cols, *own))
+    left0, right1 = tied(left0, left1, right0), tied(right1, left1, right0)
+    far = [lax.ppermute(left0, "x", ring(NX, 1)), lax.ppermute(right1, "x", ring(NX, 3))]
+    total = product(None, arrived0, [own])
     rows2, arrived2 = exchange(gathered[2], later(cols, rows1, total))
-    total = product(total, arrived1, [[left], [right]])
+    total = product(total, arrived1, [[left0, left1], [right0, right1]], (), HEAVY)
     total = product(total, arrived2, [far])
     return total[None]
 

time: 263 us -> 254 us (0.966)
  waiting for transfers between devices: 123 us -> 115 us
  starting transfers between devices: 34.7 us -> 38.1 us
  between operations: 20.9 us -> 17.8 us
    all_gather x3, waiting for transfers between devices: 68.2 us -> 38.3 us  [gather(): lax.all_gather(block, 'z', axis=1, tiled=True).reshape(-1, cols + META)]
    all_to_all x3, waiting for transfers between devices: 9.47 us -> 23 us  [exchange(): return (rows, lax.all_to_all(rows, ('y', 'c'), 0, 0, tiled=True))]
    ppermute x4 -> x6, waiting for transfers between devices: 23.3 us -> 29.9 us  [the longest x1 29.9 us: local(): lax.ppermute(own[0], 'x', ring(NX, 3))]
    dynamic_slice x2 -> x0, local copies, waits for them, and re-layouts: 4.2 us -> none  [the longest x1 2.67 us: local(): lax.dynamic_slice_in_dim(right, start + half, half)]
    all_to_all x3, starting transfers between devices: 19.7 us -> 22.5 us  [exchange(): return (rows, lax.all_to_all(rows, ('y', 'c'), 0, 0, tiled=True))]
    ppermute x4 -> x6, starting transfers between devices: 5.37 us -> 7.83 us  [the longest x1 2.49 us: local(): lax.ppermute(own[0], 'x', ring(NX, 3))]
    pallas_call x3 -> x6, Pallas kernels: 28.4 us -> 29.7 us  [the longest x3 29.7 us: product(): pl.pallas_call(functools.partial(product_kernel, tuple(spans), total is n...]
  transfers between devices with their start and end apart: 14 -> 16, of which waited for: 9 -> 9; matrix products, arithmetic and copies ran while one was open for 11% -> 10% of each run, Pallas kernels for 15% -> 16%
where the time goes in v2:
time: 254 us; the launch traced here: 251 us
  waiting for transfers between devices  115 us (45%)
  Pallas kernels  49.4 us (19%)
  starting transfers between devices  38.1 us (15%)
  local copies, waits for them, and re-layouts  18.6 us (7%)
  between operations  17.8 us (7%)
  other arithmetic  10.5 us (4%)
    all_gather x3, waiting for transfers between devices, gather(): lax.all_gather(block, 'z', axis=1, tiled=True).reshape(-1, cols + META)  38.3 us
    ppermute x1, waiting for transfers between devices, local(): lax.ppermute(own[0], 'x', ring(NX, 3))  29.9 us
    pallas_call x3, Pallas kernels, product(): pl.pallas_call(functools.partial(product_kernel, tuple(spans), total is n...  29.7 us
    all_to_all x3, waiting for transfers between devices, exchange(): return (rows, lax.all_to_all(rows, ('y', 'c'), 0, 0, tiled=True))  23 us
    all_to_all x3, starting transfers between devices, exchange(): return (rows, lax.all_to_all(rows, ('y', 'c'), 0, 0, tiled=True))  22.5 us
    ppermute x1, waiting for transfers between devices, local(): traded = lax.ppermute(hidden, 'y', ring(NY, 2))  18.3 us
    pallas_call x3, Pallas kernels, dispatch(): pl.pallas_call(dispatch_kernel, grid=(pairs,), in_specs=[pl.BlockSpec((1,...  17.5 us
    ppermute x3, waiting for transfers between devices, columns(): return part if step == 0 else lax.ppermute(part, 'x', ring(NX, step))  5.15 us
  transfers between devices with their start and end apart: 16, of which 9 were waited for; matrix products, arithmetic and copies ran while one was open for 10% of the time, Pallas kernels for 16%

profile of v2, /device:TPU:1, one launch (start us, length us, event | category | flops | bytes accessed | tf_op | source)
XLA Modules:
  0.0 251.4 jit_solution(6145553965607007301)
XLA Ops:
  6.5 0.7 convert_convert_fusion
  7.2 0.7 reduce-precision_convert_fusion.1
  8.1 1.5 constant_dynamic-slice_fusion.3
  9.6 0.9 fusion.7
  10.6 2.1 collective-permute-start.4
  12.7 1.4 collective-permute-start.5
  14.1 3.9 %collective-permute-done.4 = bf16[128,1024]{1,0:T(8,128)(2,1)S(1)} collective-permute-done((bf16[128,1024]{1,0:T(8,128)(2,1)}, bf16[128,1024]{1,0:T(8,128)(2,1)S(1)}, u32[]{:S(2)}, u32[]{:S(2)}) %collective-permute-start.4) | collective-permute-done | bytes 262176 | tf_op jit(solution)/shard_map/ppermute | solution.py:188
  18.0 1.3 collective-permute-done.5
  19.2 0.8 pad_maximum_fusion
  20.1 2.1 copy.43
  22.2 3.8 %collective-permute-start.1 = (bf16[4,8,2,24,1024]{4,3,1,2,0:T(8,128)(2,1)}, bf16[4,8,2,24,1024]{4,3,1,2,0:T(8,128)(2,1)}, u32[]{:S(2)}, u32[]{:S(2)}) collective-permute-start(bf16[4,8,2,24,1024]{4,3,1,2,0:T(8,128)(2,1)} %copy.43), channel_id=1, source_target_pairs={{0,32},{16,48},{32,0},{48,16},{1,33},{17,49},{33,1},{49,17},{2,34}... | collective-permute-start | bytes 9437192 | tf_op jit(solution)/shard_map/ppermute | solution.py:181
  26.3 0.6 gather_fusion
  26.9 25.0 %all-gather.9.cloned.1.call-done.token_ref = bf16[1024,1024]{1,0:T(8,128)(2,1)} async-done(((bf16[128,1024]{1,0:T(8,128)(2,1)}), bf16[1024,1024]{1,0:T(8,128)(2,1)}) %all-gather.9.cloned.1.call-update) | async-done | bytes 2097168 | tf_op jit(solution)/shard_map/all_gather | solution.py:193
  51.9 1.0 dynamic_slice.33
  52.9 1.5 slice_add_fusion.4
  54.4 1.2 copy.42
  55.6 1.2 copy.41
  56.8 0.2 compare_reduce_fusion.2
  57.0 0.8 fusion.5
  57.7 0.8 fusion.2
  58.5 4.7 %shard_map.55.refs_0_ = bf16[8,192,896]{2,1,0:T(8,128)(2,1)} custom-call(f32[4,8,256]{2,1,0:T(8,128)} %bitcast.82, f32[4,8,256]{2,1,0:T(8,128)} %bitcast.79, bf16[1024,1024]{1,0:T(8,128)(2,1)} %all-gather.9.cloned.1.call-done.token_ref), custom_call_target="tpu_custom_call" | custom-call | flops 1024 | bytes 1024 | tf_op jit(solution)/shard_map/pallas_call | solution.py:40
  63.2 8.9 %all-to-all-start = ((bf16[8,192,896]{2,1,0:T(8,128)(2,1)}), bf16[8,192,896]{2,1,0:T(8,128)(2,1)}, u32[]{:S(2)}, u32[]{:S(2)}) async-start(bf16[8,192,896]{2,1,0:T(8,128)(2,1)} %shard_map.55.refs_0_), calls=%async_computation | async-start | bytes 5505024 | tf_op jit(solution)/shard_map/all_to_all | solution.py:204
  72.1 0.6 dynamic_slice.26.value_ref
  72.7 1.1 shard_map.56
  74.5 18.3 %collective-permute-done.1 = bf16[4,8,2,24,1024]{4,3,1,2,0:T(8,128)(2,1)} collective-permute-done((bf16[4,8,2,24,1024]{4,3,1,2,0:T(8,128)(2,1)}, bf16[4,8,2,24,1024]{4,3,1,2,0:T(8,128)(2,1)}, u32[]{:S(2)}, u32[]{:S(2)}) %collective-permute-start.1) | collective-permute-done | bytes 3145760 | tf_op jit(solution)/shard_map/ppermute | solution.py:181
  92.8 0.3 select_bitcast_fusion
  93.2 2.0 fusion.24
  95.2 0.5 collective-permute-start.2
  95.7 2.1 collective-permute-start.3
  97.9 0.5 collective-permute-start
  98.3 0.5 shard_map.58
  100.8 10.2 %all-gather.7.cloned.1.call-done = bf16[2,1024,1024]{2,1,0:T(8,128)(2,1)} async-done(((bf16[2,128,1024]{2,1,0:T(8,128)(2,1)}), bf16[2,1024,1024]{2,1,0:T(8,128)(2,1)}) %all-gather.7.cloned.1.call-update) | async-done | bytes 4194320 | tf_op jit(solution)/shard_map/all_gather | solution.py:193
  111.0 1.3 constant_dynamic-slice_fusion.1
  112.4 1.9 slice_add_fusion
  114.3 1.5 copy.46
  115.8 0.3 copy.45
  116.1 0.2 compare_reduce_fusion
  116.3 0.8 fusion.3
  117.2 0.8 fusion
  118.0 8.1 %shard_map.59.refs_0_ = bf16[8,384,896]{2,1,0:T(8,128)(2,1)} custom-call(f32[8,8,256]{2,1,0:T(8,128)} %bitcast.80, f32[8,8,256]{2,1,0:T(8,128)} %bitcast.75, bf16[2048,1024]{1,0:T(8,128)(2,1)} %bitcast.69), custom_call_target="tpu_custom_call" | custom-call | flops 1024 | bytes 1024 | tf_op jit(solution)/shard_map/pallas_call | solution.py:40
  126.1 5.2 %all-to-all-start.2 = ((bf16[8,384,896]{2,1,0:T(8,128)(2,1)}), bf16[8,384,896]{2,1,0:T(8,128)(2,1)}, u32[]{:S(2)}, u32[]{:S(2)}) async-start(bf16[8,384,896]{2,1,0:T(8,128)(2,1)} %shard_map.59.refs_0_), calls=%async_computation.2 | async-start | bytes 11010048 | tf_op jit(solution)/shard_map/all_to_all | solution.py:204
  131.4 0.7 copy-done.5
  132.0 0.5 copy-done.2
  132.6 2.5 collective-permute-start.7
  135.1 29.9 %collective-permute-done.7.refs_2_.refs_3_ = bf16[4,192,1024]{2,1,0:T(8,128)(2,1)S(1)} collective-permute-done((bf16[4,192,1024]{2,1,0:T(8,128)(2,1)}, bf16[4,192,1024]{2,1,0:T(8,128)(2,1)S(1)}, u32[]{:S(2)}, u32[]{:S(2)}) %collective-permute-start.7) | collective-permute-done | bytes 1572896 | tf_op jit(solution)/shard_map/ppermute | solution.py:213
  164.9 1.1 copy-done.3
  166.1 1.2 copy-done.4
  167.3 1.4 collective-permute-start.8
  168.7 7.7 %shard_map.60.refs_1_.refs_5_ = f32[896,1024]{1,0:T(8,128)} custom-call(bf16[8,192,896]{2,1,0:T(8,128)(2,1)} %all-to-all-done.refs_0_, bf16[4,192,1024]{2,1,0:T(8,128)(2,1)} %bitcast.15.refs_0_.refs_1_, bf16[4,192,1024]{2,1,0:T(8,128)(2,1)} %bitcast.16.refs_1_.refs_2_), custom_call_target="tpu_custom_call" | custom-call | flops 1024 | bytes 1024 | tf_op jit(solution)/shard_map/pallas_call | solution.py:159
  176.4 1.2 collective-permute-start.9
  177.6 0.5 shard_map.61
  180.0 3.1 %all-gather.5.cloned.1.call-done = bf16[1,1024,1024]{2,1,0:T(8,128)(2,1)} async-done(((bf16[1,128,1024]{2,1,0:T(8,128)(2,1)}), bf16[1,1024,1024]{2,1,0:T(8,128)(2,1)}) %all-gather.5.cloned.1.call-update) | async-done | bytes 2097168 | tf_op jit(solution)/shard_map/all_gather | solution.py:193
  183.2 1.1 constant_dynamic-slice_fusion
  184.3 0.5 slice_add_fusion.2
  184.9 0.2 copy.47
  185.1 0.2 compare_reduce_fusion.1
  185.3 0.8 fusion.6
  186.0 0.8 fusion.1
  186.8 4.7 %shard_map.62 = bf16[8,192,896]{2,1,0:T(8,128)(2,1)} custom-call(f32[4,8,256]{2,1,0:T(8,128)} %bitcast.81, f32[4,8,256]{2,1,0:T(8,128)} %bitcast.78, bf16[1024,1024]{1,0:T(8,128)(2,1)} %bitcast.70), custom_call_target="tpu_custom_call" | custom-call | flops 1024 | bytes 1024 | tf_op jit(solution)/shard_map/pallas_call | solution.py:40
  191.5 2.8 %all-to-all-done.2.refs_0_ = bf16[8,384,896]{2,1,0:T(8,128)(2,1)} async-done(((bf16[8,384,896]{2,1,0:T(8,128)(2,1)}), bf16[8,384,896]{2,1,0:T(8,128)(2,1)}, u32[]{:S(2)}, u32[]{:S(2)}) %all-to-all-start.2) | async-done | bytes 5505056 | tf_op jit(solution)/shard_map/all_to_all | solution.py:204
  194.3 8.4 %all-to-all-start.1 = ((bf16[8,192,896]{2,1,0:T(8,128)(2,1)}), bf16[8,192,896]{2,1,0:T(8,128)(2,1)}, u32[]{:S(2)}, u32[]{:S(2)}) async-start(bf16[8,192,896]{2,1,0:T(8,128)(2,1)} %shard_map.62), calls=%async_computation.1 | async-start | bytes 5505024 | tf_op jit(solution)/shard_map/all_to_all | solution.py:204
  202.6 13.3 %shard_map.65.refs_3_ = f32[896,1024]{1,0:T(8,128)} custom-call(bf16[8,384,896]{2,1,0:T(8,128)(2,1)} %all-to-all-done.2.refs_0_, bf16[4,192,1024]{2,1,0:T(8,128)(2,1)} %shard_map.63.refs_1_, bf16[4,192,1024]{2,1,0:T(8,128)(2,1)} %copy-done.4, bf16[4,192,1024]{2,1,0:T(8,128)(2,1)} %copy-done.3, bf16[4,192,1024]{2,1,0:T(8,128)(2,1)} %shard_map.64.refs_4_, ...), custom_call_target="tpu_custom_call" | custom-call | flops 199999995904 | bytes 100000000 | tf_op jit(solution)/shard_map/pallas_call | solution.py:159
  216.0 20.1 %all-to-all-done.1.refs_0_ = bf16[8,192,896]{2,1,0:T(8,128)(2,1)} async-done(((bf16[8,192,896]{2,1,0:T(8,128)(2,1)}), bf16[8,192,896]{2,1,0:T(8,128)(2,1)}, u32[]{:S(2)}, u32[]{:S(2)}) %all-to-all-start.1) | async-done | bytes 2752544 | tf_op jit(solution)/shard_map/all_to_all | solution.py:204
  236.1 8.8 %shard_map.66 = f32[896,1024]{1,0:T(8,128)} custom-call(bf16[8,192,896]{2,1,0:T(8,128)(2,1)} %all-to-all-done.1.refs_0_, bf16[4,192,1024]{2,1,0:T(8,128)(2,1)} %collective-permute-done.8.refs_1_, bf16[4,192,1024]{2,1,0:T(8,128)(2,1)} %collective-permute-done.9.refs_2_, f32[896,1024]{1,0:T(8,128)} %shard_map.65.refs_3_), custom_call_target="tpu_custom_call" | custom-call | flops 1024 | bytes 1024 | tf_op jit(solution)/shard_map/pallas_call | solution.py:159
  (41 shorter events, 0.9 us)
Async XLA Ops:
  6.5 45.4 %all-gather.9.cloned.1.call-start = ((), (), s32[]{:S(2)}) async-start(), calls=%async_computation.5 | async-start | bytes 2359296 | tf_op jit(solution)/shard_map/all_gather | solution.py:193
  8.1 12.0 %copy-start.1 = (bf16[1,1,64,24,1024]{4,3,2,1,0:T(8,128)(2,1)S(1)}, bf16[1,1,64,24,1024]{4,3,2,1,0:T(8,128)(2,1)}, u32[]{:S(2)}) copy-start(bf16[1,1,64,24,1024]{4,3,2,1,0:T(8,128)(2,1)} %param.8) | copy-start | bytes 9437188
  10.6 100.5 %all-gather.7.cloned.1.call-start = ((), (), s32[]{:S(2)}) async-start(), calls=%async_computation.4 | async-start | bytes 4718592 | tf_op jit(solution)/shard_map/all_gather | solution.py:193
  10.6 7.4 %collective-permute-start.4 = (bf16[128,1024]{1,0:T(8,128)(2,1)}, bf16[128,1024]{1,0:T(8,128)(2,1)S(1)}, u32[]{:S(2)}, u32[]{:S(2)}) collective-permute-start(bf16[128,1024]{1,0:T(8,128)(2,1)} %get-tuple-element.17), channel_id=1, source_target_pairs={{0,64},{64,128},{128,192},{192,0},{1,65},{65,129},{129,193},{193,1... | collective-permute-start | bytes 786440 | tf_op jit(solution)/shard_map/ppermute | solution.py:188
  12.7 6.5 %collective-permute-start.5 = (bf16[128,1024]{1,0:T(8,128)(2,1)S(1)}, bf16[128,1024]{1,0:T(8,128)(2,1)S(1)}, u32[]{:S(2)}, u32[]{:S(2)}) collective-permute-start(bf16[128,1024]{1,0:T(8,128)(2,1)S(1)} %get-tuple-element.20), channel_id=1, source_target_pairs={{0,192},{64,0},{128,64},{192,128},{1,193},{65,1},{129,65},{193,129... | collective-permute-start | bytes 786440 | tf_op jit(solution)/shard_map/ppermute | solution.py:188
  20.1 6.2 %copy-start = (s32[64]{0:T(128)S(1)}, s32[64]{0:T(128)}, u32[]{:S(2)}) copy-start(s32[64]{0:T(128)} %param.9) | copy-start | bytes 772
  22.2 70.6 %collective-permute-start.1 = (bf16[4,8,2,24,1024]{4,3,1,2,0:T(8,128)(2,1)}, bf16[4,8,2,24,1024]{4,3,1,2,0:T(8,128)(2,1)}, u32[]{:S(2)}, u32[]{:S(2)}) collective-permute-start(bf16[4,8,2,24,1024]{4,3,1,2,0:T(8,128)(2,1)} %copy.43), channel_id=1, source_target_pairs={{0,32},{16,48},{32,0},{48,16},{1,33},{17,49},{33,1},{49,17},{2,34}... | collective-permute-start | bytes 9437192 | tf_op jit(solution)/shard_map/ppermute | solution.py:181
  63.2 62.9 %all-to-all-start = ((bf16[8,192,896]{2,1,0:T(8,128)(2,1)}), bf16[8,192,896]{2,1,0:T(8,128)(2,1)}, u32[]{:S(2)}, u32[]{:S(2)}) async-start(bf16[8,192,896]{2,1,0:T(8,128)(2,1)} %shard_map.55.refs_0_), calls=%async_computation | async-start | bytes 5505024 | tf_op jit(solution)/shard_map/all_to_all | solution.py:204
  93.2 4.7 %copy-start.6 = (bf16[128,1024]{1,0:T(8,128)(2,1)S(1)}, bf16[128,1024]{1,0:T(8,128)(2,1)}, u32[]{:S(2)}) copy-start(bf16[128,1024]{1,0:T(8,128)(2,1)} %get-tuple-element.18) | copy-start | bytes 786436
  95.2 36.1 %collective-permute-start.2 = (bf16[4,192,1024]{2,1,0:T(8,128)(2,1)}, bf16[4,192,1024]{2,1,0:T(8,128)(2,1)S(1)}, u32[]{:S(2)}, u32[]{:S(2)}) collective-permute-start(bf16[4,192,1024]{2,1,0:T(8,128)(2,1)} %bitcast.15.refs_0_.refs_1_), channel_id=1, source_target_pairs={{0,64},{64,128},{128,192},{192,0},{1,65},{65,129},{129,193},{193,1... | collective-permute-start | bytes 4718600 | tf_op jit(solution)/shard_map/ppermute | solution.py:212
  95.7 35.6 %collective-permute-start.3 = (bf16[4,192,1024]{2,1,0:T(8,128)(2,1)}, bf16[4,192,1024]{2,1,0:T(8,128)(2,1)}, u32[]{:S(2)}, u32[]{:S(2)}) collective-permute-start(bf16[4,192,1024]{2,1,0:T(8,128)(2,1)} %bitcast.16.refs_1_.refs_2_), channel_id=1, source_target_pairs={{0,192},{64,0},{128,64},{192,128},{1,193},{65,1},{129,65},{193,129... | collective-permute-start | bytes 4718600 | tf_op jit(solution)/shard_map/ppermute | solution.py:212
  97.9 33.5 %collective-permute-start = (bf16[128,1024]{1,0:T(8,128)(2,1)S(1)}, bf16[128,1024]{1,0:T(8,128)(2,1)S(1)}, u32[]{:S(2)}, u32[]{:S(2)}) collective-permute-start(bf16[128,1024]{1,0:T(8,128)(2,1)S(1)} %copy-done.6), channel_id=1, source_target_pairs={{0,128},{64,192},{128,0},{192,64},{1,129},{65,193},{129,1},{193,65... | collective-permute-start | bytes 786440 | tf_op jit(solution)/shard_map/ppermute | solution.py:188
  126.1 68.2 %all-to-all-start.2 = ((bf16[8,384,896]{2,1,0:T(8,128)(2,1)}), bf16[8,384,896]{2,1,0:T(8,128)(2,1)}, u32[]{:S(2)}, u32[]{:S(2)}) async-start(bf16[8,384,896]{2,1,0:T(8,128)(2,1)} %shard_map.59.refs_0_), calls=%async_computation.2 | async-start | bytes 11010048 | tf_op jit(solution)/shard_map/all_to_all | solution.py:204
  131.3 51.9 %all-gather.5.cloned.1.call-start = ((), (), s32[]{:S(2)}) async-start(), calls=%async_computation.3 | async-start | bytes 2359296 | tf_op jit(solution)/shard_map/all_gather | solution.py:193
  131.3 0.7 copy-start.5
  131.3 1.2 copy-start.2
  132.6 32.4 %collective-permute-start.7 = (bf16[4,192,1024]{2,1,0:T(8,128)(2,1)}, bf16[4,192,1024]{2,1,0:T(8,128)(2,1)S(1)}, u32[]{:S(2)}, u32[]{:S(2)}) collective-permute-start(bf16[4,192,1024]{2,1,0:T(8,128)(2,1)} %bitcast.15.refs_0_.refs_1_), channel_id=1, source_target_pairs={{0,192},{64,0},{128,64},{192,128},{1,193},{65,1},{129,65},{193,129... | collective-permute-start | bytes 4718600 | tf_op jit(solution)/shard_map/ppermute | solution.py:213
  135.1 29.9 %collective-permute-start.6 = (bf16[4,192,1024]{2,1,0:T(8,128)(2,1)}, bf16[4,192,1024]{2,1,0:T(8,128)(2,1)S(1)}, u32[]{:S(2)}, u32[]{:S(2)}) collective-permute-start(bf16[4,192,1024]{2,1,0:T(8,128)(2,1)} %bitcast.16.refs_1_.refs_2_), channel_id=1, source_target_pairs={{0,64},{64,128},{128,192},{192,0},{1,65},{65,129},{129,193},{193,1... | collective-permute-start | bytes 4718600 | tf_op jit(solution)/shard_map/ppermute | solution.py:213
  164.9 1.2 copy-start.3
  166.1 1.2 copy-start.4
  167.3 48.7 %collective-permute-start.8 = (bf16[4,192,1024]{2,1,0:T(8,128)(2,1)}, bf16[4,192,1024]{2,1,0:T(8,128)(2,1)}, u32[]{:S(2)}, u32[]{:S(2)}) collective-permute-start(bf16[4,192,1024]{2,1,0:T(8,128)(2,1)} %shard_map.63.refs_1_), channel_id=1, source_target_pairs={{0,64},{64,128},{128,192},{192,0},{1,65},{65,129},{129,193},{193,1... | collective-permute-start | bytes 4718600 | tf_op jit(solution)/shard_map/ppermute | solution.py:217
  176.4 39.5 %collective-permute-start.9 = (bf16[4,192,1024]{2,1,0:T(8,128)(2,1)}, bf16[4,192,1024]{2,1,0:T(8,128)(2,1)}, u32[]{:S(2)}, u32[]{:S(2)}) collective-permute-start(bf16[4,192,1024]{2,1,0:T(8,128)(2,1)} %shard_map.64.refs_4_), channel_id=1, source_target_pairs={{0,192},{64,0},{128,64},{192,128},{1,193},{65,1},{129,65},{193,129... | collective-permute-start | bytes 4718600 | tf_op jit(solution)/shard_map/ppermute | solution.py:217
  194.3 41.8 %all-to-all-start.1 = ((bf16[8,192,896]{2,1,0:T(8,128)(2,1)}), bf16[8,192,896]{2,1,0:T(8,128)(2,1)}, u32[]{:S(2)}, u32[]{:S(2)}) async-start(bf16[8,192,896]{2,1,0:T(8,128)(2,1)} %shard_map.62), calls=%async_computation.1 | async-start | bytes 5505024 | tf_op jit(solution)/shard_map/all_to_all | solution.py:204
Sparse Core Ops, SparseCore 0:
  10.7 41.1 all-gather.8
  53.7 57.2 all-gather.6
  133.9 49.1 all-gather.4

commit v3 on v2

--- a/solution.py
+++ b/solution.py
@@ -9,6 +9,7 @@
 
 NX, NY, NZ, NC = 4, 4, 8, 2
 GATHERS = ((0,), (1, 3), (2,))
+
 SPACE = 56 * 1024 * 1024
 PARTS = 3
 META = 128
@@ -18,35 +19,38 @@
 
 def dispatch_kernel(target_ref, gate_ref, token_ref, *refs):
     out_ref = refs[-1]
-    dests, rows = out_ref.shape[:2]
-    tokens = target_ref.shape[2]
+    pairs, dests, tokens = target_ref.shape
+    rows = out_ref.shape[1] // pairs
     slot = lax.broadcasted_iota(jnp.int32, (rows, tokens), 0).astype(jnp.float32)
-    picks, weights = [], []
-    for r in range(dests):
-        hit = slot == target_ref[0, r : r + 1, :]
-        picks.append(jnp.where(hit, 1.0, 0.0))
-        weights.append(jnp.sum(jnp.where(hit, gate_ref[0, r : r + 1, :], 0.0), axis=1, keepdims=True))
-    pick = jnp.concatenate(picks, axis=0).astype(jnp.bfloat16)
-    weight = jnp.concatenate(weights, axis=0)
-    scaled = jnp.dot(pick, token_ref[...], preferred_element_type=jnp.float32) * weight
-    scaled = scaled.astype(jnp.bfloat16)
-    for r in range(dests):
-        out_ref[r] = scaled[r * rows : (r + 1) * rows]
+    for pair in range(pairs):
+        picks, weights = [], []
+        for r in range(dests):
+            hit = slot == target_ref[pair, r : r + 1, :]
+            picks.append(jnp.where(hit, 1.0, 0.0))
+            weights.append(jnp.sum(jnp.where(hit, gate_ref[pair, r : r + 1, :], 0.0), axis=1, keepdims=True))
+        pick = jnp.concatenate(picks, axis=0).astype(jnp.bfloat16)
+        weight = jnp.concatenate(weights, axis=0)
+        block = token_ref[pair * tokens : (pair + 1) * tokens, :]
+        scaled = jnp.dot(pick, block, preferred_element_type=jnp.float32) * weight
+        scaled = scaled.astype(jnp.bfloat16)
+        for r in range(dests):
+            out_ref[r, pair * rows : (pair + 1) * rows, :] = scaled[r * rows : (r + 1) * rows]
 
 
 def dispatch(target, gate, tokens, cols, capacity, after=()):
     pairs, dests, width = target.shape
     rows = 2 * capacity
+    group = max(1, pairs // 2)
     return pl.pallas_call(
         dispatch_kernel,
-        grid=(pairs,),
+        grid=(pairs // group,),
         in_specs=[
-            pl.BlockSpec((1, dests, width), lambda i: (i, 0, 0)),
-            pl.BlockSpec((1, dests, width), lambda i: (i, 0, 0)),
-            pl.BlockSpec((width, cols), lambda i: (i, 0)),
+            pl.BlockSpec((group, dests, width), lambda i: (i, 0, 0)),
+            pl.BlockSpec((group, dests, width), lambda i: (i, 0, 0)),
+            pl.BlockSpec((group * width, cols), lambda i: (i, 0)),
         ]
         + [pl.BlockSpec(memory_space=pl.ANY)] * len(after),
-        out_specs=pl.BlockSpec((dests, rows, cols), lambda i: (0, i, 0)),
+        out_specs=pl.BlockSpec((dests, group * rows, cols), lambda i: (0, i, 0)),
         out_shape=jax.ShapeDtypeStruct((dests, pairs * rows, cols), jnp.bfloat16),
         compiler_params=pltpu.CompilerParams(vmem_limit_bytes=SPACE),
         cost_estimate=LIGHT,
@@ -177,8 +181,9 @@
     tok, cols = grad_out.shape[0], grad_out.shape[1] // NX
     top = expert_ids.shape[1]
     flag_here = lax.dynamic_index_in_dim(swap_flags, (y * NZ + z) * NC + c, 0, False)
-    hidden = hidden_saved.reshape(NY, NZ, NC, capacity, width)
-    traded = lax.ppermute(hidden, "y", ring(NY, 2))
+    traded = lax.ppermute(hidden_saved.reshape(-1, width), "y", ring(NY, 2))
+    traded = traded.reshape(NY, NZ, NC, capacity, width)
+    hidden = hidden_saved.reshape(traded.shape)
 
     meta = routing(expert_ids, gate_weights)
 

time: 254 us -> 251 us (0.988)
  Pallas kernels: 49.4 us -> 44.2 us
  waiting for transfers between devices: 115 us -> 120 us
    pallas_call x3, Pallas kernels: 17.5 us -> 12.4 us  [dispatch(): pl.pallas_call(dispatch_kernel, grid=(pairs // group,), in_specs=[pl.Bloc...]
  transfers between devices with their start and end apart: 16 -> 16, of which waited for: 9 -> 10; matrix products, arithmetic and copies ran while one was open for 10% -> 9% of each run, Pallas kernels for 16% -> 14%
where the time goes in v3:
time: 251 us; the launch traced here: 250 us
  waiting for transfers between devices  120 us (48%)
  Pallas kernels  44.2 us (18%)
  starting transfers between devices  37.2 us (15%)
  between operations  17.9 us (7%)
  local copies, waits for them, and re-layouts  17.7 us (7%)
  other arithmetic  11.7 us (5%)
    all_gather x3, waiting for transfers between devices, gather(): lax.all_gather(block, 'z', axis=1, tiled=True).reshape(-1, cols + META)  37.6 us
    ppermute x1, waiting for transfers between devices, local(): lax.ppermute(own[0], 'x', ring(NX, 3))  29.7 us
    pallas_call x3, Pallas kernels, product(): pl.pallas_call(functools.partial(product_kernel, tuple(spans), total is n...  29.7 us
    all_to_all x3, waiting for transfers between devices, exchange(): return (rows, lax.all_to_all(rows, ('y', 'c'), 0, 0, tiled=True))  25.5 us
    all_to_all x3, starting transfers between devices, exchange(): return (rows, lax.all_to_all(rows, ('y', 'c'), 0, 0, tiled=True))  21.4 us
    ppermute x1, waiting for transfers between devices, local(): traded = lax.ppermute(hidden_saved.reshape(-1, width), 'y', ring(NY, 2))  20.4 us
    pallas_call x3, Pallas kernels, dispatch(): pl.pallas_call(dispatch_kernel, grid=(pairs // group,), in_specs=[pl.Bloc...  12.4 us
    ppermute x3, waiting for transfers between devices, columns(): return part if step == 0 else lax.ppermute(part, 'x', ring(NX, step))  6.26 us
  transfers between devices with their start and end apart: 16, of which 10 were waited for; matrix products, arithmetic and copies ran while one was open for 9% of the time, Pallas kernels for 14%

profile of v3, /device:TPU:1, one launch (start us, length us, event | category | flops | bytes accessed | tf_op | source)
XLA Modules:
  0.0 250.5 jit_solution(1769741589022368750)
XLA Ops:
  6.5 0.7 convert_convert_fusion
  7.2 0.7 reduce-precision_convert_fusion.1
  8.1 1.4 constant_dynamic-slice_fusion.3
  9.4 0.8 fusion.7
  10.3 2.1 collective-permute-start.4
  12.5 1.4 collective-permute-start.5
  13.8 3.7 %collective-permute-done.4 = bf16[128,1024]{1,0:T(8,128)(2,1)S(1)} collective-permute-done((bf16[128,1024]{1,0:T(8,128)(2,1)S(1)}, bf16[128,1024]{1,0:T(8,128)(2,1)S(1)}, u32[]{:S(2)}, u32[]{:S(2)}) %collective-permute-start.4) | collective-permute-done | bytes 262176 | tf_op jit(solution)/shard_map/ppermute | solution.py:193
  17.5 1.5 collective-permute-done.5
  19.0 0.8 pad_maximum_fusion
  19.8 3.7 %collective-permute-start.1 = (bf16[1536,1024]{1,0:T(8,128)(2,1)}, bf16[1536,1024]{1,0:T(8,128)(2,1)}, u32[]{:S(2)}, u32[]{:S(2)}) collective-permute-start(bf16[1536,1024]{1,0:T(8,128)(2,1)} %bitcast.13), channel_id=1, source_target_pairs={{0,32},{16,48},{32,0},{48,16},{1,33},{17,49},{33,1},{49,17},{2,34}... | collective-permute-start | bytes 9437192 | tf_op jit(solution)/shard_map/ppermute | solution.py:184
  23.8 0.6 gather_fusion
  24.4 27.2 %all-gather.9.cloned.1.call-done.token_ref = bf16[1024,1024]{1,0:T(8,128)(2,1)} async-done(((bf16[128,1024]{1,0:T(8,128)(2,1)}), bf16[1024,1024]{1,0:T(8,128)(2,1)}) %all-gather.9.cloned.1.call-update) | async-done | bytes 2097168 | tf_op jit(solution)/shard_map/all_gather | solution.py:198
  51.7 1.0 dynamic_slice.33
  52.7 0.5 slice_add_fusion.4
  53.3 0.2 copy.40
  53.5 0.2 compare_reduce_fusion.2
  53.7 0.8 fusion.5
  54.4 0.8 fusion.2
  55.2 3.5 %shard_map.55.refs_0_ = bf16[8,192,896]{2,1,0:T(8,128)(2,1)} custom-call(f32[4,8,256]{2,1,0:T(8,128)} %bitcast.82, f32[4,8,256]{2,1,0:T(8,128)} %bitcast.79, bf16[1024,1024]{1,0:T(8,128)(2,1)} %all-gather.9.cloned.1.call-done.token_ref), custom_call_target="tpu_custom_call" | custom-call | flops 1024 | bytes 1024 | tf_op jit(solution)/shard_map/pallas_call | solution.py:44
  58.7 8.8 %all-to-all-start = ((bf16[8,192,896]{2,1,0:T(8,128)(2,1)}), bf16[8,192,896]{2,1,0:T(8,128)(2,1)S(1)}, u32[]{:S(2)}, u32[]{:S(2)}) async-start(bf16[8,192,896]{2,1,0:T(8,128)(2,1)} %shard_map.55.refs_0_), calls=%async_computation | async-start | bytes 5505024 | tf_op jit(solution)/shard_map/all_to_all | solution.py:209
  67.5 0.6 dynamic_slice.26.value_ref
  68.1 1.1 shard_map.56
  70.0 20.4 %collective-permute-done.1 = bf16[1536,1024]{1,0:T(8,128)(2,1)} collective-permute-done((bf16[1536,1024]{1,0:T(8,128)(2,1)}, bf16[1536,1024]{1,0:T(8,128)(2,1)}, u32[]{:S(2)}, u32[]{:S(2)}) %collective-permute-start.1) | collective-permute-done | bytes 3145760 | tf_op jit(solution)/shard_map/ppermute | solution.py:184
  90.3 2.2 select_bitcast_fusion
  92.6 0.3 fusion.24
  92.9 1.3 copy.43
  94.2 1.3 copy.42
  95.5 0.7 collective-permute-start.2
  96.2 2.0 collective-permute-start.3
  98.2 0.7 collective-permute-start
  98.9 0.5 shard_map.58
  101.3 9.5 %all-gather.7.cloned.1.call-done = bf16[2,1024,1024]{2,1,0:T(8,128)(2,1)} async-done(((bf16[2,128,1024]{2,1,0:T(8,128)(2,1)}), bf16[2,1024,1024]{2,1,0:T(8,128)(2,1)}) %all-gather.7.cloned.1.call-update) | async-done | bytes 4194320 | tf_op jit(solution)/shard_map/all_gather | solution.py:198
  110.7 1.3 constant_dynamic-slice_fusion.1
  112.1 2.2 slice_add_fusion
  114.3 1.5 copy.45
  115.8 1.5 copy.44
  117.3 0.2 compare_reduce_fusion
  117.6 0.9 fusion.3
  118.4 0.8 fusion
  119.2 5.2 %shard_map.59.refs_0_ = bf16[8,384,896]{2,1,0:T(8,128)(2,1)} custom-call(f32[8,8,256]{2,1,0:T(8,128)} %bitcast.80, f32[8,8,256]{2,1,0:T(8,128)} %bitcast.75, bf16[2048,1024]{1,0:T(8,128)(2,1)} %bitcast.69), custom_call_target="tpu_custom_call" | custom-call | flops 1024 | bytes 1024 | tf_op jit(solution)/shard_map/pallas_call | solution.py:44
  124.4 1.6 copy-done.1
  126.1 5.2 %all-to-all-start.2 = ((bf16[8,384,896]{2,1,0:T(8,128)(2,1)}), bf16[8,384,896]{2,1,0:T(8,128)(2,1)}, u32[]{:S(2)}, u32[]{:S(2)}) async-start(bf16[8,384,896]{2,1,0:T(8,128)(2,1)} %shard_map.59.refs_0_), calls=%async_computation.2 | async-start | bytes 11010048 | tf_op jit(solution)/shard_map/all_to_all | solution.py:209
  131.3 1.1 collective-permute-done
  132.4 0.7 copy-done.4
  133.2 2.2 collective-permute-start.7
  135.4 29.7 %collective-permute-done.7.refs_2_.refs_3_ = bf16[4,192,1024]{2,1,0:T(8,128)(2,1)S(1)} collective-permute-done((bf16[4,192,1024]{2,1,0:T(8,128)(2,1)}, bf16[4,192,1024]{2,1,0:T(8,128)(2,1)S(1)}, u32[]{:S(2)}, u32[]{:S(2)}) %collective-permute-start.7) | collective-permute-done | bytes 1572896 | tf_op jit(solution)/shard_map/ppermute | solution.py:218
  165.1 1.2 copy-done.2
  166.3 1.2 copy-done.3
  167.6 0.4 collective-permute-start.8
  168.0 7.7 %shard_map.60.refs_1_.refs_5_ = f32[896,1024]{1,0:T(8,128)} custom-call(bf16[8,192,896]{2,1,0:T(8,128)(2,1)} %copy-done.1, bf16[4,192,1024]{2,1,0:T(8,128)(2,1)} %bitcast.17.refs_0_.refs_1_, bf16[4,192,1024]{2,1,0:T(8,128)(2,1)} %bitcast.18.refs_1_.refs_2_), custom_call_target="tpu_custom_call" | custom-call | flops 1024 | bytes 1024 | tf_op jit(solution)/shard_map/pallas_call | solution.py:163
  175.6 2.6 %collective-permute-start.9 = (bf16[4,192,1024]{2,1,0:T(8,128)(2,1)}, bf16[4,192,1024]{2,1,0:T(8,128)(2,1)}, u32[]{:S(2)}, u32[]{:S(2)}) collective-permute-start(bf16[4,192,1024]{2,1,0:T(8,128)(2,1)} %shard_map.64.refs_4_), channel_id=1, source_target_pairs={{0,192},{64,0},{128,64},{192,128},{1,193},{65,1},{129,65},{193,129... | collective-permute-start | bytes 4718600 | tf_op jit(solution)/shard_map/ppermute | solution.py:222
  178.2 0.5 shard_map.61
  180.8 1.0 all-gather.5.cloned.1.call-done
  181.8 1.1 constant_dynamic-slice_fusion
  182.9 0.5 slice_add_fusion.2
  183.6 0.2 copy.46
  183.9 0.8 fusion.6
  184.7 0.8 fusion.1
  185.4 3.6 %shard_map.62 = bf16[8,192,896]{2,1,0:T(8,128)(2,1)} custom-call(f32[4,8,256]{2,1,0:T(8,128)} %bitcast.81, f32[4,8,256]{2,1,0:T(8,128)} %bitcast.78, bf16[1024,1024]{1,0:T(8,128)(2,1)} %bitcast.70), custom_call_target="tpu_custom_call" | custom-call | flops 1024 | bytes 1024 | tf_op jit(solution)/shard_map/pallas_call | solution.py:44
  189.0 5.2 %all-to-all-done.2.refs_0_ = bf16[8,384,896]{2,1,0:T(8,128)(2,1)} async-done(((bf16[8,384,896]{2,1,0:T(8,128)(2,1)}), bf16[8,384,896]{2,1,0:T(8,128)(2,1)}, u32[]{:S(2)}, u32[]{:S(2)}) %all-to-all-start.2) | async-done | bytes 5505056 | tf_op jit(solution)/shard_map/all_to_all | solution.py:209
  194.3 7.4 %all-to-all-start.1 = ((bf16[8,192,896]{2,1,0:T(8,128)(2,1)}), bf16[8,192,896]{2,1,0:T(8,128)(2,1)}, u32[]{:S(2)}, u32[]{:S(2)}) async-start(bf16[8,192,896]{2,1,0:T(8,128)(2,1)} %shard_map.62), calls=%async_computation.1 | async-start | bytes 5505024 | tf_op jit(solution)/shard_map/all_to_all | solution.py:209
  201.7 13.2 %shard_map.65.refs_3_ = f32[896,1024]{1,0:T(8,128)} custom-call(bf16[8,384,896]{2,1,0:T(8,128)(2,1)} %all-to-all-done.2.refs_0_, bf16[4,192,1024]{2,1,0:T(8,128)(2,1)} %shard_map.63.refs_1_, bf16[4,192,1024]{2,1,0:T(8,128)(2,1)} %copy-done.3, bf16[4,192,1024]{2,1,0:T(8,128)(2,1)} %copy-done.2, bf16[4,192,1024]{2,1,0:T(8,128)(2,1)} %shard_map.64.refs_4_, ...), custom_call_target="tpu_custom_call" | custom-call | flops 199999995904 | bytes 100000000 | tf_op jit(solution)/shard_map/pallas_call | solution.py:163
  214.9 20.2 %all-to-all-done.1.refs_0_ = bf16[8,192,896]{2,1,0:T(8,128)(2,1)} async-done(((bf16[8,192,896]{2,1,0:T(8,128)(2,1)}), bf16[8,192,896]{2,1,0:T(8,128)(2,1)}, u32[]{:S(2)}, u32[]{:S(2)}) %all-to-all-start.1) | async-done | bytes 2752544 | tf_op jit(solution)/shard_map/all_to_all | solution.py:209
  235.2 8.8 %shard_map.66 = f32[896,1024]{1,0:T(8,128)} custom-call(bf16[8,192,896]{2,1,0:T(8,128)(2,1)} %all-to-all-done.1.refs_0_, bf16[4,192,1024]{2,1,0:T(8,128)(2,1)} %collective-permute-done.8.refs_1_, bf16[4,192,1024]{2,1,0:T(8,128)(2,1)} %collective-permute-done.9.refs_2_, f32[896,1024]{1,0:T(8,128)} %shard_map.65.refs_3_), custom_call_target="tpu_custom_call" | custom-call | flops 1024 | bytes 1024 | tf_op jit(solution)/shard_map/pallas_call | solution.py:163
  (38 shorter events, 1.2 us)
Async XLA Ops:
  6.5 45.1 %all-gather.9.cloned.1.call-start = ((), (), s32[]{:S(2)}) async-start(), calls=%async_computation.5 | async-start | bytes 2359296 | tf_op jit(solution)/shard_map/all_gather | solution.py:198
  8.1 15.7 %copy-start = (s32[64]{0:T(128)S(1)}, s32[64]{0:T(128)}, u32[]{:S(2)}) copy-start(s32[64]{0:T(128)} %param.9) | copy-start | bytes 772
  10.3 100.4 %all-gather.7.cloned.1.call-start = ((), (), s32[]{:S(2)}) async-start(), calls=%async_computation.4 | async-start | bytes 4718592 | tf_op jit(solution)/shard_map/all_gather | solution.py:198
  10.3 7.1 %collective-permute-start.4 = (bf16[128,1024]{1,0:T(8,128)(2,1)S(1)}, bf16[128,1024]{1,0:T(8,128)(2,1)S(1)}, u32[]{:S(2)}, u32[]{:S(2)}) collective-permute-start(bf16[128,1024]{1,0:T(8,128)(2,1)S(1)} %get-tuple-element.17), channel_id=1, source_target_pairs={{0,64},{64,128},{128,192},{192,0},{1,65},{65,129},{129,193},{193,1... | collective-permute-start | bytes 786440 | tf_op jit(solution)/shard_map/ppermute | solution.py:193
  12.5 6.5 %collective-permute-start.5 = (bf16[128,1024]{1,0:T(8,128)(2,1)S(1)}, bf16[128,1024]{1,0:T(8,128)(2,1)S(1)}, u32[]{:S(2)}, u32[]{:S(2)}) collective-permute-start(bf16[128,1024]{1,0:T(8,128)(2,1)S(1)} %get-tuple-element.20), channel_id=1, source_target_pairs={{0,192},{64,0},{128,64},{192,128},{1,193},{65,1},{129,65},{193,129... | collective-permute-start | bytes 786440 | tf_op jit(solution)/shard_map/ppermute | solution.py:193
  19.8 70.5 %collective-permute-start.1 = (bf16[1536,1024]{1,0:T(8,128)(2,1)}, bf16[1536,1024]{1,0:T(8,128)(2,1)}, u32[]{:S(2)}, u32[]{:S(2)}) collective-permute-start(bf16[1536,1024]{1,0:T(8,128)(2,1)} %bitcast.13), channel_id=1, source_target_pairs={{0,32},{16,48},{32,0},{48,16},{1,33},{17,49},{33,1},{49,17},{2,34}... | collective-permute-start | bytes 9437192 | tf_op jit(solution)/shard_map/ppermute | solution.py:184
  58.7 65.7 %all-to-all-start = ((bf16[8,192,896]{2,1,0:T(8,128)(2,1)}), bf16[8,192,896]{2,1,0:T(8,128)(2,1)S(1)}, u32[]{:S(2)}, u32[]{:S(2)}) async-start(bf16[8,192,896]{2,1,0:T(8,128)(2,1)} %shard_map.55.refs_0_), calls=%async_computation | async-start | bytes 5505024 | tf_op jit(solution)/shard_map/all_to_all | solution.py:209
  95.5 36.9 %collective-permute-start.2 = (bf16[4,192,1024]{2,1,0:T(8,128)(2,1)}, bf16[4,192,1024]{2,1,0:T(8,128)(2,1)}, u32[]{:S(2)}, u32[]{:S(2)}) collective-permute-start(bf16[4,192,1024]{2,1,0:T(8,128)(2,1)} %bitcast.17.refs_0_.refs_1_), channel_id=1, source_target_pairs={{0,64},{64,128},{128,192},{192,0},{1,65},{65,129},{129,193},{193,1... | collective-permute-start | bytes 4718600 | tf_op jit(solution)/shard_map/ppermute | solution.py:217
  96.2 36.2 %collective-permute-start.3 = (bf16[4,192,1024]{2,1,0:T(8,128)(2,1)}, bf16[4,192,1024]{2,1,0:T(8,128)(2,1)}, u32[]{:S(2)}, u32[]{:S(2)}) collective-permute-start(bf16[4,192,1024]{2,1,0:T(8,128)(2,1)} %bitcast.18.refs_1_.refs_2_), channel_id=1, source_target_pairs={{0,192},{64,0},{128,64},{192,128},{1,193},{65,1},{129,65},{193,129... | collective-permute-start | bytes 4718600 | tf_op jit(solution)/shard_map/ppermute | solution.py:217
  98.2 34.2 %collective-permute-start = (bf16[128,1024]{1,0:T(8,128)(2,1)S(1)}, bf16[128,1024]{1,0:T(8,128)(2,1)S(1)}, u32[]{:S(2)}, u32[]{:S(2)}) collective-permute-start(bf16[128,1024]{1,0:T(8,128)(2,1)S(1)} %get-tuple-element.18), channel_id=1, source_target_pairs={{0,128},{64,192},{128,0},{192,64},{1,129},{65,193},{129,1},{193,65... | collective-permute-start | bytes 786440 | tf_op jit(solution)/shard_map/ppermute | solution.py:193
  124.4 1.6 copy-start.1
  126.1 68.2 %all-to-all-start.2 = ((bf16[8,384,896]{2,1,0:T(8,128)(2,1)}), bf16[8,384,896]{2,1,0:T(8,128)(2,1)}, u32[]{:S(2)}, u32[]{:S(2)}) async-start(bf16[8,384,896]{2,1,0:T(8,128)(2,1)} %shard_map.59.refs_0_), calls=%async_computation.2 | async-start | bytes 11010048 | tf_op jit(solution)/shard_map/all_to_all | solution.py:209
  131.3 50.5 %all-gather.5.cloned.1.call-start = ((), (), s32[]{:S(2)}) async-start(), calls=%async_computation.3 | async-start | bytes 2359296 | tf_op jit(solution)/shard_map/all_gather | solution.py:198
  132.4 0.7 copy-start.4
  133.2 32.0 %collective-permute-start.7 = (bf16[4,192,1024]{2,1,0:T(8,128)(2,1)}, bf16[4,192,1024]{2,1,0:T(8,128)(2,1)S(1)}, u32[]{:S(2)}, u32[]{:S(2)}) collective-permute-start(bf16[4,192,1024]{2,1,0:T(8,128)(2,1)} %bitcast.17.refs_0_.refs_1_), channel_id=1, source_target_pairs={{0,192},{64,0},{128,64},{192,128},{1,193},{65,1},{129,65},{193,129... | collective-permute-start | bytes 4718600 | tf_op jit(solution)/shard_map/ppermute | solution.py:218
  135.4 29.7 %collective-permute-start.6 = (bf16[4,192,1024]{2,1,0:T(8,128)(2,1)}, bf16[4,192,1024]{2,1,0:T(8,128)(2,1)S(1)}, u32[]{:S(2)}, u32[]{:S(2)}) collective-permute-start(bf16[4,192,1024]{2,1,0:T(8,128)(2,1)} %bitcast.18.refs_1_.refs_2_), channel_id=1, source_target_pairs={{0,64},{64,128},{128,192},{192,0},{1,65},{65,129},{129,193},{193,1... | collective-permute-start | bytes 4718600 | tf_op jit(solution)/shard_map/ppermute | solution.py:218
  165.1 1.2 copy-start.2
  166.3 1.2 copy-start.3
  167.6 47.3 %collective-permute-start.8 = (bf16[4,192,1024]{2,1,0:T(8,128)(2,1)}, bf16[4,192,1024]{2,1,0:T(8,128)(2,1)}, u32[]{:S(2)}, u32[]{:S(2)}) collective-permute-start(bf16[4,192,1024]{2,1,0:T(8,128)(2,1)} %shard_map.63.refs_1_), channel_id=1, source_target_pairs={{0,64},{64,128},{128,192},{192,0},{1,65},{65,129},{129,193},{193,1... | collective-permute-start | bytes 4718600 | tf_op jit(solution)/shard_map/ppermute | solution.py:222
  175.6 39.3 %collective-permute-start.9 = (bf16[4,192,1024]{2,1,0:T(8,128)(2,1)}, bf16[4,192,1024]{2,1,0:T(8,128)(2,1)}, u32[]{:S(2)}, u32[]{:S(2)}) collective-permute-start(bf16[4,192,1024]{2,1,0:T(8,128)(2,1)} %shard_map.64.refs_4_), channel_id=1, source_target_pairs={{0,192},{64,0},{128,64},{192,128},{1,193},{65,1},{129,65},{193,129... | collective-permute-start | bytes 4718600 | tf_op jit(solution)/shard_map/ppermute | solution.py:222
  194.3 40.9 %all-to-all-start.1 = ((bf16[8,192,896]{2,1,0:T(8,128)(2,1)}), bf16[8,192,896]{2,1,0:T(8,128)(2,1)}, u32[]{:S(2)}, u32[]{:S(2)}) async-start(bf16[8,192,896]{2,1,0:T(8,128)(2,1)} %shard_map.62), calls=%async_computation.1 | async-start | bytes 5505024 | tf_op jit(solution)/shard_map/all_to_all | solution.py:209
Sparse Core Ops, SparseCore 0:
  10.4 41.1 all-gather.8
  53.5 57.2 all-gather.6
  133.9 47.8 all-gather.4

commit v4 on v3

--- a/solution.py
+++ b/solution.py
@@ -17,44 +17,59 @@
 LIGHT = pl.CostEstimate(flops=1024, bytes_accessed=1024, transcendentals=0)
 
 
-def dispatch_kernel(target_ref, gate_ref, token_ref, *refs):
+def dispatch_kernel(tok, top, capacity, cols, wanted_ref, token_ref, *refs):
     out_ref = refs[-1]
-    pairs, dests, tokens = target_ref.shape
-    rows = out_ref.shape[1] // pairs
-    slot = lax.broadcasted_iota(jnp.int32, (rows, tokens), 0).astype(jnp.float32)
-    for pair in range(pairs):
+    dests, rows, width = wanted_ref.shape[0], 2 * capacity, 2 * tok
+    slot = lax.broadcasted_iota(jnp.int32, (rows, width), 0).astype(jnp.float32)
+    before = lax.broadcasted_iota(jnp.int32, (tok, tok), 0) < lax.broadcasted_iota(jnp.int32, (tok, tok), 1)
+    before = jnp.where(before, 1.0, 0.0).astype(jnp.bfloat16)
+    for pair in range(token_ref.shape[0] // width):
+        span = slice(pair * width, (pair + 1) * width)
+        meta = token_ref[span, cols:].astype(jnp.float32).T
+        ids, gates = meta[:top], 0.0
+        for i in reversed(range(PARTS)):
+            gates = gates + meta[(i + 1) * top : (i + 2) * top]
+        members, chosen = [], []
+        for r in range(dests):
+            match = ids == wanted_ref[r]
+            members.append(jnp.sum(jnp.where(match, 1.0, 0.0), axis=0, keepdims=True))
+            chosen.append(jnp.sum(jnp.where(match, gates, 0.0), axis=0, keepdims=True))
+        member = jnp.concatenate(members, axis=0)
+        member = jnp.concatenate([member[:, :tok], member[:, tok:]], axis=0)
+        place = jnp.dot(member.astype(jnp.bfloat16), before, preferred_element_type=jnp.float32)
+        first = jnp.where(member[:dests] > 0.5, place[:dests], -1.0)
+        second = jnp.where(member[dests:] > 0.5, place[dests:] + capacity, -1.0)
+        target = jnp.concatenate([first, second], axis=1)
         picks, weights = [], []
         for r in range(dests):
-            hit = slot == target_ref[pair, r : r + 1, :]
+            hit = slot == target[r : r + 1, :]
             picks.append(jnp.where(hit, 1.0, 0.0))
-            weights.append(jnp.sum(jnp.where(hit, gate_ref[pair, r : r + 1, :], 0.0), axis=1, keepdims=True))
+            weights.append(jnp.sum(jnp.where(hit, chosen[r], 0.0), axis=1, keepdims=True))
         pick = jnp.concatenate(picks, axis=0).astype(jnp.bfloat16)
         weight = jnp.concatenate(weights, axis=0)
-        block = token_ref[pair * tokens : (pair + 1) * tokens, :]
-        scaled = jnp.dot(pick, block, preferred_element_type=jnp.float32) * weight
+        scaled = jnp.dot(pick, token_ref[span, :cols], preferred_element_type=jnp.float32) * weight
         scaled = scaled.astype(jnp.bfloat16)
         for r in range(dests):
             out_ref[r, pair * rows : (pair + 1) * rows, :] = scaled[r * rows : (r + 1) * rows]
 
 
-def dispatch(target, gate, tokens, cols, capacity, after=()):
-    pairs, dests, width = target.shape
-    rows = 2 * capacity
-    group = max(1, pairs // 2)
-    return pl.pallas_call(
-        dispatch_kernel,
-        grid=(pairs // group,),
+def dispatch(wanted, tokens, tok, top, capacity, after=()):
+    total, dests = tokens.shape[0], wanted.shape[0]
+    cols, rows = tokens.shape[1] - META, total // tok * capacity
+    steps = 2
+    return pl.pallas_call(
+        functools.partial(dispatch_kernel, tok, top, capacity, cols),
+        grid=(steps,),
         in_specs=[
-            pl.BlockSpec((group, dests, width), lambda i: (i, 0, 0)),
-            pl.BlockSpec((group, dests, width), lambda i: (i, 0, 0)),
-            pl.BlockSpec((group * width, cols), lambda i: (i, 0)),
+            pl.BlockSpec(memory_space=pltpu.SMEM),
+            pl.BlockSpec((total // steps, tokens.shape[1]), lambda i: (i, 0)),
         ]
         + [pl.BlockSpec(memory_space=pl.ANY)] * len(after),
-        out_specs=pl.BlockSpec((dests, group * rows, cols), lambda i: (0, i, 0)),
-        out_shape=jax.ShapeDtypeStruct((dests, pairs * rows, cols), jnp.bfloat16),
+        out_specs=pl.BlockSpec((dests, rows // steps, cols), lambda i: (0, i, 0)),
+        out_shape=jax.ShapeDtypeStruct((dests, rows, cols), jnp.bfloat16),
         compiler_params=pltpu.CompilerParams(vmem_limit_bytes=SPACE),
         cost_estimate=LIGHT,
-    )(target, gate, tokens, *after)
+    )(wanted, tokens, *after)
 
 
 def later_kernel(value_ref, *refs):
@@ -95,27 +110,6 @@
         gates = gates - high
     meta = jnp.concatenate(columns, axis=1)
     return jnp.pad(meta, ((0, 0), (0, META - meta.shape[1]))).astype(jnp.bfloat16)
-
-
-def tables(meta, tok, top, wanted, capacity):
-    sources = meta.shape[0] // tok
-    meta = meta.astype(jnp.float32).reshape(sources, tok, -1).transpose(0, 2, 1)
-    ids, gates = meta[:, :top], 0.0
-    for i in reversed(range(PARTS)):
-        gates = gates + meta[:, (i + 1) * top : (i + 2) * top]
-    match = ids[:, None] == wanted[None, :, None, None]
-    member = jnp.any(match, axis=2)
-    gate = jnp.sum(jnp.where(match, gates[:, None], 0.0), axis=2)
-    before = (jnp.arange(tok)[:, None] < jnp.arange(tok)[None, :]).astype(jnp.bfloat16)
-    slot = jnp.dot(member.astype(jnp.bfloat16), before, preferred_element_type=jnp.float32)
-    odd = (jnp.arange(sources) % 2 * capacity).astype(jnp.float32)
-    target = jnp.where(member, slot + odd[:, None, None], -1.0)
-
-    def paired(table):
-        table = table.reshape(sources // 2, 2, len(wanted), tok).transpose(0, 2, 1, 3)
-        return table.reshape(sources // 2, len(wanted), 2 * tok)
-
-    return paired(target), paired(gate)
 
 
 def product_kernel(spans, summed, *refs):
@@ -203,12 +197,11 @@
     flags = jnp.take(swap_flags, devices)
     wanted = jnp.where(flags == 1, (devices + experts // 2) % experts, devices).astype(jnp.float32)
 
-    def exchange(tokens, place, after=()):
-        pick = tables(lax.dynamic_slice_in_dim(tokens, place, META, 1), tok, top, wanted, capacity)
-        rows = dispatch(*pick, tokens, cols, capacity, after)
+    def exchange(tokens, after=()):
+        rows = dispatch(wanted, tokens, tok, top, capacity, after)
         return rows, lax.all_to_all(rows, ("y", "c"), 0, 0, tiled=True)
 
-    rows0, arrived0 = exchange(gathered[0], cols)
+    rows0, arrived0 = exchange(gathered[0])
     flag = later(flag_here, rows0)
     own = jnp.where(flag == 1, traded, hidden).transpose(0, 2, 1, 3, 4)
     own = own.reshape(NY * NC, NZ * capacity, width)
@@ -217,11 +210,11 @@
     left0, right1 = lax.ppermute(own[0], "x", ring(NX, 1)), lax.ppermute(own[1], "x", ring(NX, 3))
     left1, right0 = lax.ppermute(own[1], "x", ring(NX, 1)), lax.ppermute(own[0], "x", ring(NX, 3))
     gathered.append(gather(GATHERS[2], (left0, right1)))
-    rows1, arrived1 = exchange(gathered[1], later(cols, *own))
+    rows1, arrived1 = exchange(gathered[1], tuple(own))
     left0, right1 = tied(left0, left1, right0), tied(right1, left1, right0)
     far = [lax.ppermute(left0, "x", ring(NX, 1)), lax.ppermute(right1, "x", ring(NX, 3))]
     total = product(None, arrived0, [own])
-    rows2, arrived2 = exchange(gathered[2], later(cols, rows1, total))
+    rows2, arrived2 = exchange(gathered[2], (rows1, total))
     total = product(total, arrived1, [[left0, left1], [right0, right1]], (), HEAVY)
     total = product(total, arrived2, [far])
     return total[None]

time: 251 us -> 250 us (level)
  waiting for transfers between devices: 120 us -> 134 us
  local copies, waits for them, and re-layouts: 17.7 us -> 9.34 us
  other arithmetic: 11.7 us -> 5.9 us
  between operations: 17.9 us -> 13.8 us
  starting transfers between devices: 37.2 us -> 39.8 us
    ppermute x3, waiting for transfers between devices: 6.26 us -> 13 us  [columns(): return part if step == 0 else lax.ppermute(part, 'x', ring(NX, step))]
    ppermute x1, waiting for transfers between devices: 29.7 us -> 33.1 us  [local(): lax.ppermute(own[0], 'x', ring(NX, 3))]
    all_to_all x3, waiting for transfers between devices: 25.5 us -> 22.1 us  [exchange(): return (rows, lax.all_to_all(rows, ('y', 'c'), 0, 0, tiled=True))]
    dynamic_slice x3 -> x0, local copies, waits for them, and re-layouts: 3.31 us -> none  [exchange(): lax.dynamic_slice_in_dim(tokens, place, META, 1)]
    pallas_call x3, Pallas kernels: 12.4 us -> 15.5 us  [dispatch(): pl.pallas_call(functools.partial(dispatch_kernel, tok, top, capacity, col...]
    add x3 -> x0, other arithmetic: 3.13 us -> none  [tables(): gates = gates + meta[:, (i + 1) * top:(i + 2) * top]]
    ppermute x1, waiting for transfers between devices: 0.01 us -> 3.01 us  [local(): lax.ppermute(own[1], 'x', ring(NX, 1))]
    ppermute x1, waiting for transfers between devices: 20.4 us -> 23.1 us  [local(): traded = lax.ppermute(hidden_saved.reshape(-1, width), 'y', ring(NY, 2))]
  transfers between devices with their start and end apart: 16 -> 16, of which waited for: 10 -> 11; matrix products, arithmetic and copies ran while one was open for 9% -> 3% of each run, Pallas kernels for 14% -> 15%
where the time goes in v4:
time: 250 us; the launch traced here: 249 us
  waiting for transfers between devices  134 us (54%)
  Pallas kernels  46.3 us (19%)
  starting transfers between devices  39.8 us (16%)
  between operations  13.8 us (6%)
  local copies, waits for them, and re-layouts  9.34 us (4%)
  other arithmetic  5.9 us (2%)
    all_gather x3, waiting for transfers between devices, gather(): lax.all_gather(block, 'z', axis=1, tiled=True).reshape(-1, cols + META)  39.2 us
    ppermute x1, waiting for transfers between devices, local(): lax.ppermute(own[0], 'x', ring(NX, 3))  33.1 us
    pallas_call x3, Pallas kernels, product(): pl.pallas_call(functools.partial(product_kernel, tuple(spans), total is n...  29.7 us
    ppermute x1, waiting for transfers between devices, local(): traded = lax.ppermute(hidden_saved.reshape(-1, width), 'y', ring(NY, 2))  23.1 us
    all_to_all x3, starting transfers between devices, exchange(): return (rows, lax.all_to_all(rows, ('y', 'c'), 0, 0, tiled=True))  23 us
    all_to_all x3, waiting for transfers between devices, exchange(): return (rows, lax.all_to_all(rows, ('y', 'c'), 0, 0, tiled=True))  22.1 us
    pallas_call x3, Pallas kernels, dispatch(): pl.pallas_call(functools.partial(dispatch_kernel, tok, top, capacity, col...  15.5 us
    ppermute x3, waiting for transfers between devices, columns(): return part if step == 0 else lax.ppermute(part, 'x', ring(NX, step))  13 us
  transfers between devices with their start and end apart: 16, of which 11 were waited for; matrix products, arithmetic and copies ran while one was open for 3% of the time, Pallas kernels for 15%

profile of v4, /device:TPU:1, one launch (start us, length us, event | category | flops | bytes accessed | tf_op | source)
XLA Modules:
  0.0 249.1 jit_solution(11790955764361437970)
XLA Ops:
  6.5 0.0 all-gather.9.cloned.1.call-start
  6.5 0.7 convert_convert_fusion
  7.2 0.7 reduce-precision_convert_fusion.1
  7.9 0.1 copy.18
  8.1 0.0 copy-start
  8.1 1.4 constant_dynamic-slice_fusion.1
  9.4 0.8 fusion.1
  10.3 0.0 all-gather.9.cloned.1.call-update
  10.3 0.0 all-gather.7.cloned.1.call-start
  10.3 2.1 collective-permute-start.4
  12.5 1.4 collective-permute-start.5
  13.8 3.7 %collective-permute-done.4 = bf16[128,1024]{1,0:T(8,128)(2,1)S(1)} collective-permute-done((bf16[128,1024]{1,0:T(8,128)(2,1)S(1)}, bf16[128,1024]{1,0:T(8,128)(2,1)S(1)}, u32[]{:S(2)}, u32[]{:S(2)}) %collective-permute-start.4) | collective-permute-done | bytes 262176 | tf_op jit(solution)/shard_map/ppermute | solution.py:187
  17.5 1.5 collective-permute-done.5
  19.0 0.8 pad_maximum_fusion
  19.8 0.0 all-gather.7.cloned.1.call-update
  19.8 3.7 %collective-permute-start.1 = (bf16[1536,1024]{1,0:T(8,128)(2,1)}, bf16[1536,1024]{1,0:T(8,128)(2,1)}, u32[]{:S(2)}, u32[]{:S(2)}) collective-permute-start(bf16[1536,1024]{1,0:T(8,128)(2,1)} %bitcast.3), channel_id=1, source_target_pairs={{0,32},{16,48},{32,0},{48,16},{1,33},{17,49},{33,1},{49,17},{2,34}... | collective-permute-start | bytes 9437192 | tf_op jit(solution)/shard_map/ppermute | solution.py:178
  23.5 0.1 iota_add_fusion
  23.6 0.1 add.117
  23.7 0.1 add.115
  23.8 0.0 copy-done
  23.8 0.6 gather_fusion
  24.4 0.5 fusion.9.wanted_ref
  24.9 26.7 %all-gather.9.cloned.1.call-done.token_ref = bf16[1024,1024]{1,0:T(8,128)(2,1)} async-done(((bf16[128,1024]{1,0:T(8,128)(2,1)}), bf16[1024,1024]{1,0:T(8,128)(2,1)}) %all-gather.9.cloned.1.call-update) | async-done | bytes 2097168 | tf_op jit(solution)/shard_map/all_gather | solution.py:192
  51.7 4.4 %shard_map.55.refs_0_ = bf16[8,192,896]{2,1,0:T(8,128)(2,1)} custom-call(f32[8]{0:T(128)} %fusion.9.wanted_ref, bf16[1024,1024]{1,0:T(8,128)(2,1)} %all-gather.9.cloned.1.call-done.token_ref), custom_call_target="tpu_custom_call" | custom-call | flops 1024 | bytes 1024 | tf_op jit(solution)/shard_map/pallas_call | solution.py:60
  56.0 8.9 %all-to-all-start = ((bf16[8,192,896]{2,1,0:T(8,128)(2,1)}), bf16[8,192,896]{2,1,0:T(8,128)(2,1)S(1)}, u32[]{:S(2)}, u32[]{:S(2)}) async-start(bf16[8,192,896]{2,1,0:T(8,128)(2,1)} %shard_map.55.refs_0_), calls=%async_computation | async-start | bytes 5505024 | tf_op jit(solution)/shard_map/all_to_all | solution.py:202
  64.9 0.6 dynamic_slice.17.value_ref
  65.5 1.1 shard_map.56
  67.3 23.1 %collective-permute-done.1 = bf16[1536,1024]{1,0:T(8,128)(2,1)} collective-permute-done((bf16[1536,1024]{1,0:T(8,128)(2,1)}, bf16[1536,1024]{1,0:T(8,128)(2,1)}, u32[]{:S(2)}, u32[]{:S(2)}) %collective-permute-start.1) | collective-permute-done | bytes 3145760 | tf_op jit(solution)/shard_map/ppermute | solution.py:178
  90.4 2.2 select_bitcast_fusion
  92.6 0.3 fusion.10
  92.9 1.3 copy.20
  94.3 1.3 copy.19
  95.5 0.7 collective-permute-start.2
  96.3 2.0 collective-permute-start.3
  98.2 12.5 %all-gather.7.cloned.1.call-done = bf16[2,1024,1024]{2,1,0:T(8,128)(2,1)} async-done(((bf16[2,128,1024]{2,1,0:T(8,128)(2,1)}), bf16[2,1024,1024]{2,1,0:T(8,128)(2,1)}) %all-gather.7.cloned.1.call-update) | async-done | bytes 4194320 | tf_op jit(solution)/shard_map/all_gather | solution.py:192
  110.7 6.7 %shard_map.58.refs_0_ = bf16[8,384,896]{2,1,0:T(8,128)(2,1)} custom-call(f32[8]{0:T(128)} %fusion.9.wanted_ref, bf16[2048,1024]{1,0:T(8,128)(2,1)} %bitcast.16, bf16[4,192,1024]{2,1,0:T(8,128)(2,1)} %bitcast.7.refs_0_.refs_1_, bf16[4,192,1024]{2,1,0:T(8,128)(2,1)} %bitcast.8.refs_1_.refs_2_), custom_call_target="tpu_custom_call" | custom-call | flops 1024 | bytes 1024 | tf_op jit(solution)/shard_map/pallas_call | solution.py:60
  117.5 2.3 all-to-all-done.refs_0_
  119.7 0.0 copy-start.1
  119.7 1.6 copy-done.1
  121.4 7.1 %all-to-all-start.2 = ((bf16[8,384,896]{2,1,0:T(8,128)(2,1)}), bf16[8,384,896]{2,1,0:T(8,128)(2,1)}, u32[]{:S(2)}, u32[]{:S(2)}) async-start(bf16[8,384,896]{2,1,0:T(8,128)(2,1)} %shard_map.58.refs_0_), calls=%async_computation.2 | async-start | bytes 11010048 | tf_op jit(solution)/shard_map/all_to_all | solution.py:202
  128.5 0.0 all-gather.5.cloned.1.call-start
  128.5 2.1 collective-permute-start
  130.6 7.9 %collective-permute-done = bf16[128,1024]{1,0:T(8,128)(2,1)S(1)} collective-permute-done((bf16[128,1024]{1,0:T(8,128)(2,1)S(1)}, bf16[128,1024]{1,0:T(8,128)(2,1)S(1)}, u32[]{:S(2)}, u32[]{:S(2)}) %collective-permute-start) | collective-permute-done | bytes 262176 | tf_op jit(solution)/shard_map/ppermute | solution.py:187
  138.5 0.0 collective-permute-done.2.refs_1_.refs_0_
  138.5 0.0 collective-permute-done.3.refs_2_.refs_0_
  138.5 0.7 copy-done.4
  139.2 0.0 all-gather.5.cloned.1.call-update
  139.2 2.2 collective-permute-start.7
  141.4 0.0 collective-permute-start.6
  141.4 33.1 %collective-permute-done.7.refs_2_.refs_3_ = bf16[4,192,1024]{2,1,0:T(8,128)(2,1)S(1)} collective-permute-done((bf16[4,192,1024]{2,1,0:T(8,128)(2,1)}, bf16[4,192,1024]{2,1,0:T(8,128)(2,1)S(1)}, u32[]{:S(2)}, u32[]{:S(2)}) %collective-permute-start.7) | collective-permute-done | bytes 1572896 | tf_op jit(solution)/shard_map/ppermute | solution.py:211
  174.5 3.0 %collective-permute-done.6.refs_1_.refs_2_ = bf16[4,192,1024]{2,1,0:T(8,128)(2,1)S(1)} collective-permute-done((bf16[4,192,1024]{2,1,0:T(8,128)(2,1)}, bf16[4,192,1024]{2,1,0:T(8,128)(2,1)S(1)}, u32[]{:S(2)}, u32[]{:S(2)}) %collective-permute-start.6) | collective-permute-done | bytes 1572896 | tf_op jit(solution)/shard_map/ppermute | solution.py:211
  177.5 0.0 copy-done.2
  177.5 1.2 copy-done.3
  178.7 0.0 collective-permute-start.8
  178.7 2.7 %collective-permute-start.9 = (bf16[4,192,1024]{2,1,0:T(8,128)(2,1)}, bf16[4,192,1024]{2,1,0:T(8,128)(2,1)}, u32[]{:S(2)}, u32[]{:S(2)}) collective-permute-start(bf16[4,192,1024]{2,1,0:T(8,128)(2,1)} %shard_map.62.refs_4_), channel_id=1, source_target_pairs={{0,192},{64,0},{128,64},{192,128},{1,193},{65,1},{129,65},{193,129... | collective-permute-start | bytes 4718600 | tf_op jit(solution)/shard_map/ppermute | solution.py:215
  181.4 7.6 %shard_map.59.refs_1_.refs_5_ = f32[896,1024]{1,0:T(8,128)} custom-call(bf16[8,192,896]{2,1,0:T(8,128)(2,1)} %copy-done.1, bf16[4,192,1024]{2,1,0:T(8,128)(2,1)} %bitcast.7.refs_0_.refs_1_, bf16[4,192,1024]{2,1,0:T(8,128)(2,1)} %bitcast.8.refs_1_.refs_2_), custom_call_target="tpu_custom_call" | custom-call | flops 1024 | bytes 1024 | tf_op jit(solution)/shard_map/pallas_call | solution.py:157
  189.0 4.4 %shard_map.60 = bf16[8,192,896]{2,1,0:T(8,128)(2,1)} custom-call(f32[8]{0:T(128)} %fusion.9.wanted_ref, bf16[1024,1024]{1,0:T(8,128)(2,1)} %bitcast.17, bf16[8,384,896]{2,1,0:T(8,128)(2,1)} %shard_map.58.refs_0_, f32[896,1024]{1,0:T(8,128)} %shard_map.59.refs_1_.refs_5_), custom_call_target="tpu_custom_call" | custom-call | flops 1024 | bytes 1024 | tf_op jit(solution)/shard_map/pallas_call | solution.py:60
  193.4 0.0 all-to-all-done.2.refs_0_
  193.4 6.9 %all-to-all-start.1 = ((bf16[8,192,896]{2,1,0:T(8,128)(2,1)}), bf16[8,192,896]{2,1,0:T(8,128)(2,1)}, u32[]{:S(2)}, u32[]{:S(2)}) async-start(bf16[8,192,896]{2,1,0:T(8,128)(2,1)} %shard_map.60), calls=%async_computation.1 | async-start | bytes 5505024 | tf_op jit(solution)/shard_map/all_to_all | solution.py:202
  200.4 13.3 %shard_map.63.refs_3_ = f32[896,1024]{1,0:T(8,128)} custom-call(bf16[8,384,896]{2,1,0:T(8,128)(2,1)} %all-to-all-done.2.refs_0_, bf16[4,192,1024]{2,1,0:T(8,128)(2,1)} %shard_map.61.refs_1_, bf16[4,192,1024]{2,1,0:T(8,128)(2,1)} %copy-done.3, bf16[4,192,1024]{2,1,0:T(8,128)(2,1)} %copy-done.2, bf16[4,192,1024]{2,1,0:T(8,128)(2,1)} %shard_map.62.refs_4_, ...), custom_call_target="tpu_custom_call" | custom-call | flops 199999995904 | bytes 100000000 | tf_op jit(solution)/shard_map/pallas_call | solution.py:157
  213.7 0.3 collective-permute-done.8.refs_1_
  214.0 0.0 collective-permute-done.9.refs_2_
  214.0 19.8 %all-to-all-done.1.refs_0_ = bf16[8,192,896]{2,1,0:T(8,128)(2,1)} async-done(((bf16[8,192,896]{2,1,0:T(8,128)(2,1)}), bf16[8,192,896]{2,1,0:T(8,128)(2,1)}, u32[]{:S(2)}, u32[]{:S(2)}) %all-to-all-start.1) | async-done | bytes 2752544 | tf_op jit(solution)/shard_map/all_to_all | solution.py:202
  233.8 8.8 %shard_map.64 = f32[896,1024]{1,0:T(8,128)} custom-call(bf16[8,192,896]{2,1,0:T(8,128)(2,1)} %all-to-all-done.1.refs_0_, bf16[4,192,1024]{2,1,0:T(8,128)(2,1)} %collective-permute-done.8.refs_1_, bf16[4,192,1024]{2,1,0:T(8,128)(2,1)} %collective-permute-done.9.refs_2_, f32[896,1024]{1,0:T(8,128)} %shard_map.63.refs_3_), custom_call_target="tpu_custom_call" | custom-call | flops 1024 | bytes 1024 | tf_op jit(solution)/shard_map/pallas_call | solution.py:157
  (11 shorter events, 0.0 us)
Async XLA Ops:
  6.5 45.1 %all-gather.9.cloned.1.call-start = ((), (), s32[]{:S(2)}) async-start(), calls=%async_computation.5 | async-start | bytes 2359296 | tf_op jit(solution)/shard_map/all_gather | solution.py:192
  8.1 15.7 %copy-start = (s32[64]{0:T(128)S(1)}, s32[64]{0:T(128)}, u32[]{:S(2)}) copy-start(s32[64]{0:T(128)} %param.9) | copy-start | bytes 772
  10.3 100.4 %all-gather.7.cloned.1.call-start = ((), (), s32[]{:S(2)}) async-start(), calls=%async_computation.4 | async-start | bytes 4718592 | tf_op jit(solution)/shard_map/all_gather | solution.py:192
  10.3 7.1 %collective-permute-start.4 = (bf16[128,1024]{1,0:T(8,128)(2,1)S(1)}, bf16[128,1024]{1,0:T(8,128)(2,1)S(1)}, u32[]{:S(2)}, u32[]{:S(2)}) collective-permute-start(bf16[128,1024]{1,0:T(8,128)(2,1)S(1)} %get-tuple-element.11), channel_id=1, source_target_pairs={{0,64},{64,128},{128,192},{192,0},{1,65},{65,129},{129,193},{193,1... | collective-permute-start | bytes 786440 | tf_op jit(solution)/shard_map/ppermute | solution.py:187
  12.5 6.5 %collective-permute-start.5 = (bf16[128,1024]{1,0:T(8,128)(2,1)S(1)}, bf16[128,1024]{1,0:T(8,128)(2,1)S(1)}, u32[]{:S(2)}, u32[]{:S(2)}) collective-permute-start(bf16[128,1024]{1,0:T(8,128)(2,1)S(1)} %get-tuple-element.14), channel_id=1, source_target_pairs={{0,192},{64,0},{128,64},{192,128},{1,193},{65,1},{129,65},{193,129... | collective-permute-start | bytes 786440 | tf_op jit(solution)/shard_map/ppermute | solution.py:187
  19.8 70.5 %collective-permute-start.1 = (bf16[1536,1024]{1,0:T(8,128)(2,1)}, bf16[1536,1024]{1,0:T(8,128)(2,1)}, u32[]{:S(2)}, u32[]{:S(2)}) collective-permute-start(bf16[1536,1024]{1,0:T(8,128)(2,1)} %bitcast.3), channel_id=1, source_target_pairs={{0,32},{16,48},{32,0},{48,16},{1,33},{17,49},{33,1},{49,17},{2,34}... | collective-permute-start | bytes 9437192 | tf_op jit(solution)/shard_map/ppermute | solution.py:178
  56.0 63.7 %all-to-all-start = ((bf16[8,192,896]{2,1,0:T(8,128)(2,1)}), bf16[8,192,896]{2,1,0:T(8,128)(2,1)S(1)}, u32[]{:S(2)}, u32[]{:S(2)}) async-start(bf16[8,192,896]{2,1,0:T(8,128)(2,1)} %shard_map.55.refs_0_), calls=%async_computation | async-start | bytes 5505024 | tf_op jit(solution)/shard_map/all_to_all | solution.py:202
  95.5 43.0 %collective-permute-start.2 = (bf16[4,192,1024]{2,1,0:T(8,128)(2,1)}, bf16[4,192,1024]{2,1,0:T(8,128)(2,1)}, u32[]{:S(2)}, u32[]{:S(2)}) collective-permute-start(bf16[4,192,1024]{2,1,0:T(8,128)(2,1)} %bitcast.7.refs_0_.refs_1_), channel_id=1, source_target_pairs={{0,64},{64,128},{128,192},{192,0},{1,65},{65,129},{129,193},{193,1... | collective-permute-start | bytes 4718600 | tf_op jit(solution)/shard_map/ppermute | solution.py:210
  96.3 42.2 %collective-permute-start.3 = (bf16[4,192,1024]{2,1,0:T(8,128)(2,1)}, bf16[4,192,1024]{2,1,0:T(8,128)(2,1)}, u32[]{:S(2)}, u32[]{:S(2)}) collective-permute-start(bf16[4,192,1024]{2,1,0:T(8,128)(2,1)} %bitcast.8.refs_1_.refs_2_), channel_id=1, source_target_pairs={{0,192},{64,0},{128,64},{192,128},{1,193},{65,1},{129,65},{193,129... | collective-permute-start | bytes 4718600 | tf_op jit(solution)/shard_map/ppermute | solution.py:210
  119.7 1.6 copy-start.1
  121.4 72.1 %all-to-all-start.2 = ((bf16[8,384,896]{2,1,0:T(8,128)(2,1)}), bf16[8,384,896]{2,1,0:T(8,128)(2,1)}, u32[]{:S(2)}, u32[]{:S(2)}) async-start(bf16[8,384,896]{2,1,0:T(8,128)(2,1)} %shard_map.58.refs_0_), calls=%async_computation.2 | async-start | bytes 11010048 | tf_op jit(solution)/shard_map/all_to_all | solution.py:202
  128.5 60.5 %all-gather.5.cloned.1.call-start = ((), (), s32[]{:S(2)}) async-start(), calls=%async_computation.3 | async-start | bytes 2359296 | tf_op jit(solution)/shard_map/all_gather | solution.py:192
  128.5 10.0 %collective-permute-start = (bf16[128,1024]{1,0:T(8,128)(2,1)S(1)}, bf16[128,1024]{1,0:T(8,128)(2,1)S(1)}, u32[]{:S(2)}, u32[]{:S(2)}) collective-permute-start(bf16[128,1024]{1,0:T(8,128)(2,1)S(1)} %get-tuple-element.12), channel_id=1, source_target_pairs={{0,128},{64,192},{128,0},{192,64},{1,129},{65,193},{129,1},{193,65... | collective-permute-start | bytes 786440 | tf_op jit(solution)/shard_map/ppermute | solution.py:187
  138.5 0.7 copy-start.4
  139.2 35.3 %collective-permute-start.7 = (bf16[4,192,1024]{2,1,0:T(8,128)(2,1)}, bf16[4,192,1024]{2,1,0:T(8,128)(2,1)S(1)}, u32[]{:S(2)}, u32[]{:S(2)}) collective-permute-start(bf16[4,192,1024]{2,1,0:T(8,128)(2,1)} %bitcast.7.refs_0_.refs_1_), channel_id=1, source_target_pairs={{0,192},{64,0},{128,64},{192,128},{1,193},{65,1},{129,65},{193,129... | collective-permute-start | bytes 4718600 | tf_op jit(solution)/shard_map/ppermute | solution.py:211
  141.4 36.1 %collective-permute-start.6 = (bf16[4,192,1024]{2,1,0:T(8,128)(2,1)}, bf16[4,192,1024]{2,1,0:T(8,128)(2,1)S(1)}, u32[]{:S(2)}, u32[]{:S(2)}) collective-permute-start(bf16[4,192,1024]{2,1,0:T(8,128)(2,1)} %bitcast.8.refs_1_.refs_2_), channel_id=1, source_target_pairs={{0,64},{64,128},{128,192},{192,0},{1,65},{65,129},{129,193},{193,1... | collective-permute-start | bytes 4718600 | tf_op jit(solution)/shard_map/ppermute | solution.py:211
  174.5 3.0 %copy-start.2 = (bf16[4,192,1024]{2,1,0:T(8,128)(2,1)}, bf16[4,192,1024]{2,1,0:T(8,128)(2,1)S(1)}, u32[]{:S(2)}) copy-start(bf16[4,192,1024]{2,1,0:T(8,128)(2,1)S(1)} %collective-permute-done.7.refs_2_.refs_3_) | copy-start | bytes 4718596
  177.5 1.2 copy-start.3
  178.7 35.3 %collective-permute-start.8 = (bf16[4,192,1024]{2,1,0:T(8,128)(2,1)}, bf16[4,192,1024]{2,1,0:T(8,128)(2,1)}, u32[]{:S(2)}, u32[]{:S(2)}) collective-permute-start(bf16[4,192,1024]{2,1,0:T(8,128)(2,1)} %shard_map.61.refs_1_), channel_id=1, source_target_pairs={{0,64},{64,128},{128,192},{192,0},{1,65},{65,129},{129,193},{193,1... | collective-permute-start | bytes 4718600 | tf_op jit(solution)/shard_map/ppermute | solution.py:215
  178.7 35.3 %collective-permute-start.9 = (bf16[4,192,1024]{2,1,0:T(8,128)(2,1)}, bf16[4,192,1024]{2,1,0:T(8,128)(2,1)}, u32[]{:S(2)}, u32[]{:S(2)}) collective-permute-start(bf16[4,192,1024]{2,1,0:T(8,128)(2,1)} %shard_map.62.refs_4_), channel_id=1, source_target_pairs={{0,192},{64,0},{128,64},{192,128},{1,193},{65,1},{129,65},{193,129... | collective-permute-start | bytes 4718600 | tf_op jit(solution)/shard_map/ppermute | solution.py:215
  193.4 40.4 %all-to-all-start.1 = ((bf16[8,192,896]{2,1,0:T(8,128)(2,1)}), bf16[8,192,896]{2,1,0:T(8,128)(2,1)}, u32[]{:S(2)}, u32[]{:S(2)}) async-start(bf16[8,192,896]{2,1,0:T(8,128)(2,1)} %shard_map.60), calls=%async_computation.1 | async-start | bytes 5505024 | tf_op jit(solution)/shard_map/all_to_all | solution.py:202
Sparse Core Ops, SparseCore 0:
  10.4 41.2 all-gather.8
  53.5 57.2 all-gather.6
  139.3 40.1 all-gather.4

commit v5 on v4

--- a/solution.py
+++ b/solution.py
@@ -209,12 +209,12 @@
     own = [own[:half], own[half:]]
     left0, right1 = lax.ppermute(own[0], "x", ring(NX, 1)), lax.ppermute(own[1], "x", ring(NX, 3))
     left1, right0 = lax.ppermute(own[1], "x", ring(NX, 1)), lax.ppermute(own[0], "x", ring(NX, 3))
-    gathered.append(gather(GATHERS[2], (left0, right1)))
+    total = product(None, arrived0, [own])
+    gathered.append(gather(GATHERS[2], (left0, right1, total)))
     rows1, arrived1 = exchange(gathered[1], tuple(own))
     left0, right1 = tied(left0, left1, right0), tied(right1, left1, right0)
     far = [lax.ppermute(left0, "x", ring(NX, 1)), lax.ppermute(right1, "x", ring(NX, 3))]
-    total = product(None, arrived0, [own])
-    rows2, arrived2 = exchange(gathered[2], (rows1, total))
+    rows2, arrived2 = exchange(gathered[2], (rows1,))
     total = product(total, arrived1, [[left0, left1], [right0, right1]], (), HEAVY)
     total = product(total, arrived2, [far])
     return total[None]

time: 250 us -> 245 us (0.980)
    ppermute x3, waiting for transfers between devices: 13 us -> 5.15 us  [columns(): return part if step == 0 else lax.ppermute(part, 'x', ring(NX, step))]
    all_gather x3, waiting for transfers between devices: 39.2 us -> 43.1 us  [gather(): lax.all_gather(block, 'z', axis=1, tiled=True).reshape(-1, cols + META)]
    all_to_all x3, waiting for transfers between devices: 22.1 us -> 25.4 us  [exchange(): return (rows, lax.all_to_all(rows, ('y', 'c'), 0, 0, tiled=True))]
    ppermute x1, waiting for transfers between devices: 0.32 us -> 3.43 us  [local(): lax.ppermute(left0, 'x', ring(NX, 1))]
  transfers between devices with their start and end apart: 16 -> 16, of which waited for: 11 -> 11; matrix products, arithmetic and copies ran while one was open for 3% -> 2% of each run, Pallas kernels for 15% -> 15%
where the time goes in v5:
time: 245 us; the launch traced here: 244 us
  waiting for transfers between devices  135 us (55%)
  Pallas kernels  46.3 us (19%)
  starting transfers between devices  37.9 us (15%)
  between operations  13.8 us (6%)
  local copies, waits for them, and re-layouts  6.87 us (3%)
  other arithmetic  4.14 us (2%)
    all_gather x3, waiting for transfers between devices, gather(): lax.all_gather(block, 'z', axis=1, tiled=True).reshape(-1, cols + META)  43.1 us
    ppermute x1, waiting for transfers between devices, local(): lax.ppermute(own[0], 'x', ring(NX, 3))  33.1 us
    pallas_call x3, Pallas kernels, product(): pl.pallas_call(functools.partial(product_kernel, tuple(spans), total is n...  29.7 us
    all_to_all x3, waiting for transfers between devices, exchange(): return (rows, lax.all_to_all(rows, ('y', 'c'), 0, 0, tiled=True))  25.4 us
    ppermute x1, waiting for transfers between devices, local(): traded = lax.ppermute(hidden_saved.reshape(-1, width), 'y', ring(NY, 2))  23.2 us
    all_to_all x3, starting transfers between devices, exchange(): return (rows, lax.all_to_all(rows, ('y', 'c'), 0, 0, tiled=True))  21.1 us
    pallas_call x3, Pallas kernels, dispatch(): pl.pallas_call(functools.partial(dispatch_kernel, tok, top, capacity, col...  15.4 us
    ppermute x3, starting transfers between devices, columns(): return part if step == 0 else lax.ppermute(part, 'x', ring(NX, step))  5.39 us
  transfers between devices with their start and end apart: 16, of which 11 were waited for; matrix products, arithmetic and copies ran while one was open for 2% of the time, Pallas kernels for 15%

profile of v5, /device:TPU:1, one launch (start us, length us, event | category | flops | bytes accessed | tf_op | source)
XLA Modules:
  0.0 244.1 jit_solution(7039590632526367574)
XLA Ops:
  6.5 0.0 all-gather.9.cloned.1.call-start
  6.5 0.7 convert_convert_fusion
  7.2 0.7 reduce-precision_convert_fusion.1
  7.9 0.1 copy.18
  8.1 0.0 copy-start.6
  8.1 0.0 copy-start
  8.1 1.5 constant_dynamic-slice_fusion.1
  9.6 0.9 fusion.1
  10.5 0.0 all-gather.9.cloned.1.call-update
  10.5 0.0 all-gather.7.cloned.1.call-start
  10.6 2.1 collective-permute-start.4
  12.7 1.4 collective-permute-start.5
  14.1 3.9 %collective-permute-done.4 = bf16[128,1024]{1,0:T(8,128)(2,1)S(1)} collective-permute-done((bf16[128,1024]{1,0:T(8,128)(2,1)}, bf16[128,1024]{1,0:T(8,128)(2,1)S(1)}, u32[]{:S(2)}, u32[]{:S(2)}) %collective-permute-start.4) | collective-permute-done | bytes 262176 | tf_op jit(solution)/shard_map/ppermute | solution.py:187
  17.9 1.3 collective-permute-done.5
  19.2 0.8 pad_maximum_fusion
  20.0 0.0 all-gather.7.cloned.1.call-update
  20.1 3.9 %collective-permute-start.1 = (bf16[1536,1024]{1,0:T(8,128)(2,1)S(1)}, bf16[1536,1024]{1,0:T(8,128)(2,1)}, u32[]{:S(2)}, u32[]{:S(2)}) collective-permute-start(bf16[1536,1024]{1,0:T(8,128)(2,1)S(1)} %bitcast.25), channel_id=1, source_target_pairs={{0,32},{16,48},{32,0},{48,16},{1,33},{17,49},{33,1},{49,17},{2,34}... | collective-permute-start | bytes 9437192 | tf_op jit(solution)/shard_map/ppermute | solution.py:178
  24.0 0.1 iota_add_fusion
  24.0 0.1 add.117
  24.1 0.1 add.115
  24.2 0.6 gather_fusion
  24.9 0.6 fusion.9.wanted_ref
  25.5 26.4 %all-gather.9.cloned.1.call-done.token_ref = bf16[1024,1024]{1,0:T(8,128)(2,1)} async-done(((bf16[128,1024]{1,0:T(8,128)(2,1)}), bf16[1024,1024]{1,0:T(8,128)(2,1)}) %all-gather.9.cloned.1.call-update) | async-done | bytes 2097168 | tf_op jit(solution)/shard_map/all_gather | solution.py:192
  51.9 4.4 %shard_map.55.refs_0_ = bf16[8,192,896]{2,1,0:T(8,128)(2,1)} custom-call(f32[8]{0:T(128)} %fusion.9.wanted_ref, bf16[1024,1024]{1,0:T(8,128)(2,1)} %all-gather.9.cloned.1.call-done.token_ref), custom_call_target="tpu_custom_call" | custom-call | flops 1024 | bytes 1024 | tf_op jit(solution)/shard_map/pallas_call | solution.py:60
  56.2 8.8 %all-to-all-start = ((bf16[8,192,896]{2,1,0:T(8,128)(2,1)}), bf16[8,192,896]{2,1,0:T(8,128)(2,1)}, u32[]{:S(2)}, u32[]{:S(2)}) async-start(bf16[8,192,896]{2,1,0:T(8,128)(2,1)} %shard_map.55.refs_0_), calls=%async_computation | async-start | bytes 5505024 | tf_op jit(solution)/shard_map/all_to_all | solution.py:202
  65.0 0.6 dynamic_slice.17.value_ref
  65.6 1.1 shard_map.56
  67.3 23.2 %collective-permute-done.1 = bf16[1536,1024]{1,0:T(8,128)(2,1)} collective-permute-done((bf16[1536,1024]{1,0:T(8,128)(2,1)S(1)}, bf16[1536,1024]{1,0:T(8,128)(2,1)}, u32[]{:S(2)}, u32[]{:S(2)}) %collective-permute-start.1) | collective-permute-done | bytes 3145760 | tf_op jit(solution)/shard_map/ppermute | solution.py:178
  90.6 0.3 select_bitcast_fusion
  90.9 0.3 fusion.10
  91.2 0.1 copy.20
  91.4 0.1 copy.19
  91.5 0.0 copy-start.3
  91.5 0.6 collective-permute-start.2
  92.1 2.2 collective-permute-start.3
  94.3 16.7 %all-gather.7.cloned.1.call-done = bf16[2,1024,1024]{2,1,0:T(8,128)(2,1)} async-done(((bf16[2,128,1024]{2,1,0:T(8,128)(2,1)}), bf16[2,1024,1024]{2,1,0:T(8,128)(2,1)}) %all-gather.7.cloned.1.call-update) | async-done | bytes 4194320 | tf_op jit(solution)/shard_map/all_gather | solution.py:192
  111.0 0.0 copy-done.1
  111.0 6.7 %shard_map.59.refs_0_ = bf16[8,384,896]{2,1,0:T(8,128)(2,1)} custom-call(f32[8]{0:T(128)} %fusion.9.wanted_ref, bf16[2048,1024]{1,0:T(8,128)(2,1)} %bitcast.24, bf16[4,192,1024]{2,1,0:T(8,128)(2,1)} %bitcast.21, bf16[4,192,1024]{2,1,0:T(8,128)(2,1)} %bitcast.17), custom_call_target="tpu_custom_call" | custom-call | flops 1024 | bytes 1024 | tf_op jit(solution)/shard_map/pallas_call | solution.py:60
  117.7 2.4 all-to-all-done.refs_0_
  120.1 7.2 %all-to-all-start.2 = ((bf16[8,384,896]{2,1,0:T(8,128)(2,1)}), bf16[8,384,896]{2,1,0:T(8,128)(2,1)}, u32[]{:S(2)}, u32[]{:S(2)}) async-start(bf16[8,384,896]{2,1,0:T(8,128)(2,1)} %shard_map.59.refs_0_), calls=%async_computation.2 | async-start | bytes 11010048 | tf_op jit(solution)/shard_map/all_to_all | solution.py:202
  127.2 1.9 collective-permute-start
  129.1 7.6 %shard_map.57.refs_3_.refs_5_ = f32[896,1024]{1,0:T(8,128)} custom-call(bf16[8,192,896]{2,1,0:T(8,128)(2,1)} %all-to-all-done.refs_0_, bf16[4,192,1024]{2,1,0:T(8,128)(2,1)} %bitcast.22, bf16[4,192,1024]{2,1,0:T(8,128)(2,1)} %bitcast.18), custom_call_target="tpu_custom_call" | custom-call | flops 1024 | bytes 1024 | tf_op jit(solution)/shard_map/pallas_call | solution.py:157
  136.8 0.0 collective-permute-done
  136.8 0.0 collective-permute-done.2.refs_1_.refs_0_
  136.8 0.0 collective-permute-done.3.refs_2_.refs_0_
  136.8 0.7 copy-done.7
  137.5 0.0 all-gather.5.cloned.1.call-update
  137.5 1.4 copy-done.4
  138.9 2.0 collective-permute-start.7
  140.9 0.0 copy-done.2
  140.9 0.0 collective-permute-start.6
  140.9 33.1 %collective-permute-done.7.refs_2_.refs_3_ = bf16[4,192,1024]{2,1,0:T(8,128)(2,1)S(1)} collective-permute-done((bf16[4,192,1024]{2,1,0:T(8,128)(2,1)S(1)}, bf16[4,192,1024]{2,1,0:T(8,128)(2,1)S(1)}, u32[]{:S(2)}, u32[]{:S(2)}) %collective-permute-start.7) | collective-permute-done | bytes 1572896 | tf_op jit(solution)/shard_map/ppermute | solution.py:211
  174.0 1.1 copy-done.5
  175.2 1.7 collective-permute-done.6.refs_1_.refs_2_
  176.9 0.0 collective-permute-start.8
  176.9 2.7 %collective-permute-start.9 = (bf16[4,192,1024]{2,1,0:T(8,128)(2,1)}, bf16[4,192,1024]{2,1,0:T(8,128)(2,1)}, u32[]{:S(2)}, u32[]{:S(2)}) collective-permute-start(bf16[4,192,1024]{2,1,0:T(8,128)(2,1)} %shard_map.62.refs_4_), channel_id=1, source_target_pairs={{0,192},{64,0},{128,64},{192,128},{1,193},{65,1},{129,65},{193,129... | collective-permute-start | bytes 4718600 | tf_op jit(solution)/shard_map/ppermute | solution.py:216
  179.6 4.4 %shard_map.60 = bf16[8,192,896]{2,1,0:T(8,128)(2,1)} custom-call(f32[8]{0:T(128)} %fusion.9.wanted_ref, bf16[1024,1024]{1,0:T(8,128)(2,1)} %bitcast.27, bf16[8,384,896]{2,1,0:T(8,128)(2,1)} %shard_map.59.refs_0_), custom_call_target="tpu_custom_call" | custom-call | flops 1024 | bytes 1024 | tf_op jit(solution)/shard_map/pallas_call | solution.py:60
  183.9 6.3 %all-to-all-done.2.refs_0_ = bf16[8,384,896]{2,1,0:T(8,128)(2,1)} async-done(((bf16[8,384,896]{2,1,0:T(8,128)(2,1)}), bf16[8,384,896]{2,1,0:T(8,128)(2,1)}, u32[]{:S(2)}, u32[]{:S(2)}) %all-to-all-start.2) | async-done | bytes 5505056 | tf_op jit(solution)/shard_map/all_to_all | solution.py:202
  190.2 5.2 %all-to-all-start.1 = ((bf16[8,192,896]{2,1,0:T(8,128)(2,1)}), bf16[8,192,896]{2,1,0:T(8,128)(2,1)}, u32[]{:S(2)}, u32[]{:S(2)}) async-start(bf16[8,192,896]{2,1,0:T(8,128)(2,1)} %shard_map.60), calls=%async_computation.1 | async-start | bytes 5505024 | tf_op jit(solution)/shard_map/all_to_all | solution.py:202
  195.4 13.3 %shard_map.63.refs_3_ = f32[896,1024]{1,0:T(8,128)} custom-call(bf16[8,384,896]{2,1,0:T(8,128)(2,1)} %all-to-all-done.2.refs_0_, bf16[4,192,1024]{2,1,0:T(8,128)(2,1)} %shard_map.61.refs_1_, bf16[4,192,1024]{2,1,0:T(8,128)(2,1)} %collective-permute-done.6.refs_1_.refs_2_, bf16[4,192,1024]{2,1,0:T(8,128)(2,1)} %copy-done.5, ...), custom_call_target="tpu_custom_call" | custom-call | flops 199999995904 | bytes 100000000 | tf_op jit(solution)/shard_map/pallas_call | solution.py:157
  208.7 3.4 %collective-permute-done.8.refs_1_ = bf16[4,192,1024]{2,1,0:T(8,128)(2,1)} collective-permute-done((bf16[4,192,1024]{2,1,0:T(8,128)(2,1)}, bf16[4,192,1024]{2,1,0:T(8,128)(2,1)}, u32[]{:S(2)}, u32[]{:S(2)}) %collective-permute-start.8) | collective-permute-done | bytes 1572896 | tf_op jit(solution)/shard_map/ppermute | solution.py:216
  212.1 0.0 collective-permute-done.9.refs_2_
  212.1 16.7 %all-to-all-done.1.refs_0_ = bf16[8,192,896]{2,1,0:T(8,128)(2,1)} async-done(((bf16[8,192,896]{2,1,0:T(8,128)(2,1)}), bf16[8,192,896]{2,1,0:T(8,128)(2,1)}, u32[]{:S(2)}, u32[]{:S(2)}) %all-to-all-start.1) | async-done | bytes 2752544 | tf_op jit(solution)/shard_map/all_to_all | solution.py:202
  228.8 8.8 %shard_map.64 = f32[896,1024]{1,0:T(8,128)} custom-call(bf16[8,192,896]{2,1,0:T(8,128)(2,1)} %all-to-all-done.1.refs_0_, bf16[4,192,1024]{2,1,0:T(8,128)(2,1)} %collective-permute-done.8.refs_1_, bf16[4,192,1024]{2,1,0:T(8,128)(2,1)} %collective-permute-done.9.refs_2_, f32[896,1024]{1,0:T(8,128)} %shard_map.63.refs_3_), custom_call_target="tpu_custom_call" | custom-call | flops 1024 | bytes 1024 | tf_op jit(solution)/shard_map/pallas_call | solution.py:157
  (17 shorter events, 0.0 us)
Async XLA Ops:
  6.5 45.4 %all-gather.9.cloned.1.call-start = ((), (), s32[]{:S(2)}) async-start(), calls=%async_computation.5 | async-start | bytes 2359296 | tf_op jit(solution)/shard_map/all_gather | solution.py:192
  8.1 12.0 %copy-start.6 = (bf16[1,1,64,24,1024]{4,3,2,1,0:T(8,128)(2,1)S(1)}, bf16[1,1,64,24,1024]{4,3,2,1,0:T(8,128)(2,1)}, u32[]{:S(2)}) copy-start(bf16[1,1,64,24,1024]{4,3,2,1,0:T(8,128)(2,1)} %param.8) | copy-start | bytes 9437188
  8.1 16.1 %copy-start = (s32[64]{0:T(128)S(1)}, s32[64]{0:T(128)}, u32[]{:S(2)}) copy-start(s32[64]{0:T(128)} %param.9) | copy-start | bytes 772
  10.5 100.4 %all-gather.7.cloned.1.call-start = ((), (), s32[]{:S(2)}) async-start(), calls=%async_computation.4 | async-start | bytes 4718592 | tf_op jit(solution)/shard_map/all_gather | solution.py:192
  10.6 7.4 %collective-permute-start.4 = (bf16[128,1024]{1,0:T(8,128)(2,1)}, bf16[128,1024]{1,0:T(8,128)(2,1)S(1)}, u32[]{:S(2)}, u32[]{:S(2)}) collective-permute-start(bf16[128,1024]{1,0:T(8,128)(2,1)} %get-tuple-element.11), channel_id=1, source_target_pairs={{0,64},{64,128},{128,192},{192,0},{1,65},{65,129},{129,193},{193,1... | collective-permute-start | bytes 786440 | tf_op jit(solution)/shard_map/ppermute | solution.py:187
  12.7 6.5 %collective-permute-start.5 = (bf16[128,1024]{1,0:T(8,128)(2,1)S(1)}, bf16[128,1024]{1,0:T(8,128)(2,1)S(1)}, u32[]{:S(2)}, u32[]{:S(2)}) collective-permute-start(bf16[128,1024]{1,0:T(8,128)(2,1)S(1)} %get-tuple-element.14), channel_id=1, source_target_pairs={{0,192},{64,0},{128,64},{192,128},{1,193},{65,1},{129,65},{193,129... | collective-permute-start | bytes 786440 | tf_op jit(solution)/shard_map/ppermute | solution.py:187
  20.1 70.5 %collective-permute-start.1 = (bf16[1536,1024]{1,0:T(8,128)(2,1)S(1)}, bf16[1536,1024]{1,0:T(8,128)(2,1)}, u32[]{:S(2)}, u32[]{:S(2)}) collective-permute-start(bf16[1536,1024]{1,0:T(8,128)(2,1)S(1)} %bitcast.25), channel_id=1, source_target_pairs={{0,32},{16,48},{32,0},{48,16},{1,33},{17,49},{33,1},{49,17},{2,34}... | collective-permute-start | bytes 9437192 | tf_op jit(solution)/shard_map/ppermute | solution.py:178
  56.2 63.8 %all-to-all-start = ((bf16[8,192,896]{2,1,0:T(8,128)(2,1)}), bf16[8,192,896]{2,1,0:T(8,128)(2,1)}, u32[]{:S(2)}, u32[]{:S(2)}) async-start(bf16[8,192,896]{2,1,0:T(8,128)(2,1)} %shard_map.55.refs_0_), calls=%async_computation | async-start | bytes 5505024 | tf_op jit(solution)/shard_map/all_to_all | solution.py:202
  91.4 19.6 %copy-start.1 = (bf16[2,2,8,24,1024]{4,3,2,1,0:T(8,128)(2,1)}, bf16[2,2,8,24,1024]{4,3,2,1,0:T(8,128)(2,1)S(1)}, u32[]{:S(2)}) copy-start(bf16[2,2,8,24,1024]{4,3,2,1,0:T(8,128)(2,1)S(1)} %copy.20) | copy-start | bytes 4718596
  91.5 19.4 %copy-start.3 = (bf16[2,2,8,24,1024]{4,3,2,1,0:T(8,128)(2,1)}, bf16[2,2,8,24,1024]{4,3,2,1,0:T(8,128)(2,1)S(1)}, u32[]{:S(2)}) copy-start(bf16[2,2,8,24,1024]{4,3,2,1,0:T(8,128)(2,1)S(1)} %copy.19) | copy-start | bytes 4718596
  91.5 45.2 %collective-permute-start.2 = (bf16[4,192,1024]{2,1,0:T(8,128)(2,1)S(1)}, bf16[4,192,1024]{2,1,0:T(8,128)(2,1)}, u32[]{:S(2)}, u32[]{:S(2)}) collective-permute-start(bf16[4,192,1024]{2,1,0:T(8,128)(2,1)S(1)} %bitcast.20), channel_id=1, source_target_pairs={{0,64},{64,128},{128,192},{192,0},{1,65},{65,129},{129,193},{193,1... | collective-permute-start | bytes 4718600 | tf_op jit(solution)/shard_map/ppermute | solution.py:210
  92.1 44.6 %collective-permute-start.3 = (bf16[4,192,1024]{2,1,0:T(8,128)(2,1)S(1)}, bf16[4,192,1024]{2,1,0:T(8,128)(2,1)}, u32[]{:S(2)}, u32[]{:S(2)}) collective-permute-start(bf16[4,192,1024]{2,1,0:T(8,128)(2,1)S(1)} %bitcast.16), channel_id=1, source_target_pairs={{0,192},{64,0},{128,64},{192,128},{1,193},{65,1},{129,65},{193,129... | collective-permute-start | bytes 4718600 | tf_op jit(solution)/shard_map/ppermute | solution.py:210
  120.1 70.1 %all-to-all-start.2 = ((bf16[8,384,896]{2,1,0:T(8,128)(2,1)}), bf16[8,384,896]{2,1,0:T(8,128)(2,1)}, u32[]{:S(2)}, u32[]{:S(2)}) async-start(bf16[8,384,896]{2,1,0:T(8,128)(2,1)} %shard_map.59.refs_0_), calls=%async_computation.2 | async-start | bytes 11010048 | tf_op jit(solution)/shard_map/all_to_all | solution.py:202
  127.2 52.3 %all-gather.5.cloned.1.call-start = ((), (), s32[]{:S(2)}) async-start(), calls=%async_computation.3 | async-start | bytes 2359296 | tf_op jit(solution)/shard_map/all_gather | solution.py:192
  127.2 9.6 %collective-permute-start = (bf16[128,1024]{1,0:T(8,128)(2,1)}, bf16[128,1024]{1,0:T(8,128)(2,1)S(1)}, u32[]{:S(2)}, u32[]{:S(2)}) collective-permute-start(bf16[128,1024]{1,0:T(8,128)(2,1)} %get-tuple-element.12), channel_id=1, source_target_pairs={{0,128},{64,192},{128,0},{192,64},{1,129},{65,193},{129,1},{193,65... | collective-permute-start | bytes 786440 | tf_op jit(solution)/shard_map/ppermute | solution.py:187
  136.8 0.7 copy-start.7
  137.5 1.4 copy-start.4
  137.5 3.4 %copy-start.2 = (bf16[2,2,8,24,1024]{4,3,2,1,0:T(8,128)(2,1)S(1)}, bf16[2,2,8,24,1024]{4,3,2,1,0:T(8,128)(2,1)}, u32[]{:S(2)}) copy-start(bf16[2,2,8,24,1024]{4,3,2,1,0:T(8,128)(2,1)} %copy-done.1) | copy-start | bytes 4718596
  138.9 35.1 %collective-permute-start.7 = (bf16[4,192,1024]{2,1,0:T(8,128)(2,1)S(1)}, bf16[4,192,1024]{2,1,0:T(8,128)(2,1)S(1)}, u32[]{:S(2)}, u32[]{:S(2)}) collective-permute-start(bf16[4,192,1024]{2,1,0:T(8,128)(2,1)S(1)} %bitcast.23), channel_id=1, source_target_pairs={{0,192},{64,0},{128,64},{192,128},{1,193},{65,1},{129,65},{193,129... | collective-permute-start | bytes 4718600 | tf_op jit(solution)/shard_map/ppermute | solution.py:211
  140.9 35.9 %collective-permute-start.6 = (bf16[4,192,1024]{2,1,0:T(8,128)(2,1)S(1)}, bf16[4,192,1024]{2,1,0:T(8,128)(2,1)}, u32[]{:S(2)}, u32[]{:S(2)}) collective-permute-start(bf16[4,192,1024]{2,1,0:T(8,128)(2,1)S(1)} %bitcast.19), channel_id=1, source_target_pairs={{0,64},{64,128},{128,192},{192,0},{1,65},{65,129},{129,193},{193,1... | collective-permute-start | bytes 4718600 | tf_op jit(solution)/shard_map/ppermute | solution.py:211
  174.0 1.1 copy-start.5
  176.9 35.2 %collective-permute-start.8 = (bf16[4,192,1024]{2,1,0:T(8,128)(2,1)}, bf16[4,192,1024]{2,1,0:T(8,128)(2,1)}, u32[]{:S(2)}, u32[]{:S(2)}) collective-permute-start(bf16[4,192,1024]{2,1,0:T(8,128)(2,1)} %shard_map.61.refs_1_), channel_id=1, source_target_pairs={{0,64},{64,128},{128,192},{192,0},{1,65},{65,129},{129,193},{193,1... | collective-permute-start | bytes 4718600 | tf_op jit(solution)/shard_map/ppermute | solution.py:216
  176.9 35.2 %collective-permute-start.9 = (bf16[4,192,1024]{2,1,0:T(8,128)(2,1)}, bf16[4,192,1024]{2,1,0:T(8,128)(2,1)}, u32[]{:S(2)}, u32[]{:S(2)}) collective-permute-start(bf16[4,192,1024]{2,1,0:T(8,128)(2,1)} %shard_map.62.refs_4_), channel_id=1, source_target_pairs={{0,192},{64,0},{128,64},{192,128},{1,193},{65,1},{129,65},{193,129... | collective-permute-start | bytes 4718600 | tf_op jit(solution)/shard_map/ppermute | solution.py:216
  190.2 38.6 %all-to-all-start.1 = ((bf16[8,192,896]{2,1,0:T(8,128)(2,1)}), bf16[8,192,896]{2,1,0:T(8,128)(2,1)}, u32[]{:S(2)}, u32[]{:S(2)}) async-start(bf16[8,192,896]{2,1,0:T(8,128)(2,1)} %shard_map.60), calls=%async_computation.1 | async-start | bytes 5505024 | tf_op jit(solution)/shard_map/all_to_all | solution.py:202
Sparse Core Ops, SparseCore 0:
  10.7 41.1 all-gather.8
  53.7 57.2 all-gather.6
  137.6 40.0 all-gather.4

commit v6 on v5

--- a/solution.py
+++ b/solution.py
@@ -116,23 +116,26 @@
     rows_ref, states, out_ref = refs[0], refs[1 : 1 + len(spans)], refs[-1]
     step = pl.program_id(0)
 
-    @pl.when(step == 0)
-    def _():
-        out_ref[...] = refs[1 + len(spans)][...] if summed else jnp.zeros_like(out_ref)
-
     depth, width = states[0].shape[1:]
 
-    def add(chunk, states_ref):
+    def add(chunk, start, states_ref):
         rows = rows_ref[:, chunk * depth : (chunk + 1) * depth, :]
-        out_ref[...] += lax.dot_general(
+        term = lax.dot_general(
             rows.reshape(-1, rows.shape[-1]),
             states_ref[...].reshape(-1, width),
             (((0,), (0,)), ((), ())),
             preferred_element_type=jnp.float32,
         )
-
-    for (chunk, low, high), states_ref in zip(spans, states):
-        pl.when((step >= low) & (step < high))(functools.partial(add, chunk, states_ref))
+        if not start:
+            out_ref[...] += term
+        elif summed:
+            out_ref[...] = refs[1 + len(spans)][...] + term
+        else:
+            out_ref[...] = term
+
+    assert spans[0] == (0, 0, 1)
+    for n, ((chunk, low, high), states_ref) in enumerate(zip(spans, states)):
+        pl.when((step >= low) & (step < high))(functools.partial(add, chunk, n == 0, states_ref))
 
 
 def product(total, rows, states, after=(), cost=None):

time: 245 us -> 244 us (level)
  transfers between devices with their start and end apart: 16 -> 16, of which waited for: 11 -> 12; matrix products, arithmetic and copies ran while one was open for 2% -> 2% of each run, Pallas kernels for 15% -> 15%
where the time goes in v6:
time: 244 us
  waiting for transfers between devices  135 us (55%)
  Pallas kernels  45.6 us (19%)
  starting transfers between devices  38 us (16%)
  between operations  13.8 us (6%)
  local copies, waits for them, and re-layouts  6.88 us (3%)
  other arithmetic  4.14 us (2%)
    all_gather x3, waiting for transfers between devices, gather(): lax.all_gather(block, 'z', axis=1, tiled=True).reshape(-1, cols + META)  43.1 us
    ppermute x1, waiting for transfers between devices, local(): lax.ppermute(own[0], 'x', ring(NX, 3))  32.9 us
    pallas_call x3, Pallas kernels, product(): pl.pallas_call(functools.partial(product_kernel, tuple(spans), total is n...  29 us
    all_to_all x3, waiting for transfers between devices, exchange(): return (rows, lax.all_to_all(rows, ('y', 'c'), 0, 0, tiled=True))  25.4 us
    ppermute x1, waiting for transfers between devices, local(): traded = lax.ppermute(hidden_saved.reshape(-1, width), 'y', ring(NY, 2))  23.2 us
    all_to_all x3, starting transfers between devices, exchange(): return (rows, lax.all_to_all(rows, ('y', 'c'), 0, 0, tiled=True))  21.1 us
    pallas_call x3, Pallas kernels, dispatch(): pl.pallas_call(functools.partial(dispatch_kernel, tok, top, capacity, col...  15.4 us
    ppermute x3, starting transfers between devices, columns(): return part if step == 0 else lax.ppermute(part, 'x', ring(NX, step))  5.39 us
  transfers between devices with their start and end apart: 16, of which 12 were waited for; matrix products, arithmetic and copies ran while one was open for 2% of the time, Pallas kernels for 15%

profile of v6, /device:TPU:1, one launch (start us, length us, event | category | flops | bytes accessed | tf_op | source)
XLA Modules:
  0.0 243.9 jit_solution(1751307114997640128)
XLA Ops:
  6.5 0.0 all-gather.9.cloned.1.call-start
  6.5 0.7 convert_convert_fusion
  7.2 0.7 reduce-precision_convert_fusion.1
  7.9 0.1 copy.18
  8.1 0.0 copy-start.6
  8.1 0.0 copy-start
  8.1 1.5 constant_dynamic-slice_fusion.1
  9.6 0.9 fusion.1
  10.5 0.0 all-gather.9.cloned.1.call-update
  10.5 0.0 all-gather.7.cloned.1.call-start
  10.6 2.1 collective-permute-start.4
  12.7 1.4 collective-permute-start.5
  14.1 3.9 %collective-permute-done.4 = bf16[128,1024]{1,0:T(8,128)(2,1)S(1)} collective-permute-done((bf16[128,1024]{1,0:T(8,128)(2,1)}, bf16[128,1024]{1,0:T(8,128)(2,1)S(1)}, u32[]{:S(2)}, u32[]{:S(2)}) %collective-permute-start.4) | collective-permute-done | bytes 262176 | tf_op jit(solution)/shard_map/ppermute | solution.py:190
  17.9 1.3 collective-permute-done.5
  19.2 0.8 pad_maximum_fusion
  20.0 0.0 all-gather.7.cloned.1.call-update
  20.1 0.0 copy-done.6
  20.1 3.9 %collective-permute-start.1 = (bf16[1536,1024]{1,0:T(8,128)(2,1)S(1)}, bf16[1536,1024]{1,0:T(8,128)(2,1)}, u32[]{:S(2)}, u32[]{:S(2)}) collective-permute-start(bf16[1536,1024]{1,0:T(8,128)(2,1)S(1)} %bitcast.25), channel_id=1, source_target_pairs={{0,32},{16,48},{32,0},{48,16},{1,33},{17,49},{33,1},{49,17},{2,34}... | collective-permute-start | bytes 9437192 | tf_op jit(solution)/shard_map/ppermute | solution.py:181
  24.0 0.1 iota_add_fusion
  24.0 0.1 add.117
  24.1 0.1 add.115
  24.2 0.0 copy-done
  24.2 0.6 gather_fusion
  24.9 0.6 fusion.9.wanted_ref
  25.5 26.4 %all-gather.9.cloned.1.call-done.token_ref = bf16[1024,1024]{1,0:T(8,128)(2,1)} async-done(((bf16[128,1024]{1,0:T(8,128)(2,1)}), bf16[1024,1024]{1,0:T(8,128)(2,1)}) %all-gather.9.cloned.1.call-update) | async-done | bytes 2097168 | tf_op jit(solution)/shard_map/all_gather | solution.py:195
  51.9 4.4 %shard_map.55.refs_0_ = bf16[8,192,896]{2,1,0:T(8,128)(2,1)} custom-call(f32[8]{0:T(128)} %fusion.9.wanted_ref, bf16[1024,1024]{1,0:T(8,128)(2,1)} %all-gather.9.cloned.1.call-done.token_ref), custom_call_target="tpu_custom_call" | custom-call | flops 1024 | bytes 1024 | tf_op jit(solution)/shard_map/pallas_call | solution.py:60
  56.2 8.8 %all-to-all-start = ((bf16[8,192,896]{2,1,0:T(8,128)(2,1)}), bf16[8,192,896]{2,1,0:T(8,128)(2,1)}, u32[]{:S(2)}, u32[]{:S(2)}) async-start(bf16[8,192,896]{2,1,0:T(8,128)(2,1)} %shard_map.55.refs_0_), calls=%async_computation | async-start | bytes 5505024 | tf_op jit(solution)/shard_map/all_to_all | solution.py:205
  65.0 0.6 dynamic_slice.17.value_ref
  65.6 1.1 shard_map.56
  67.3 23.2 %collective-permute-done.1 = bf16[1536,1024]{1,0:T(8,128)(2,1)} collective-permute-done((bf16[1536,1024]{1,0:T(8,128)(2,1)S(1)}, bf16[1536,1024]{1,0:T(8,128)(2,1)}, u32[]{:S(2)}, u32[]{:S(2)}) %collective-permute-start.1) | collective-permute-done | bytes 3145760 | tf_op jit(solution)/shard_map/ppermute | solution.py:181
  90.6 0.3 select_bitcast_fusion
  90.9 0.3 fusion.10
  91.2 0.1 copy.20
  91.4 0.1 copy.19
  91.5 0.6 collective-permute-start.2
  92.1 2.2 collective-permute-start.3
  94.3 16.7 %all-gather.7.cloned.1.call-done = bf16[2,1024,1024]{2,1,0:T(8,128)(2,1)} async-done(((bf16[2,128,1024]{2,1,0:T(8,128)(2,1)}), bf16[2,1024,1024]{2,1,0:T(8,128)(2,1)}) %all-gather.7.cloned.1.call-update) | async-done | bytes 4194320 | tf_op jit(solution)/shard_map/all_gather | solution.py:195
  111.0 6.7 %shard_map.59.refs_0_ = bf16[8,384,896]{2,1,0:T(8,128)(2,1)} custom-call(f32[8]{0:T(128)} %fusion.9.wanted_ref, bf16[2048,1024]{1,0:T(8,128)(2,1)} %bitcast.24, bf16[4,192,1024]{2,1,0:T(8,128)(2,1)} %bitcast.21, bf16[4,192,1024]{2,1,0:T(8,128)(2,1)} %bitcast.17), custom_call_target="tpu_custom_call" | custom-call | flops 1024 | bytes 1024 | tf_op jit(solution)/shard_map/pallas_call | solution.py:60
  117.7 2.4 all-to-all-done.refs_0_
  120.1 7.2 %all-to-all-start.2 = ((bf16[8,384,896]{2,1,0:T(8,128)(2,1)}), bf16[8,384,896]{2,1,0:T(8,128)(2,1)}, u32[]{:S(2)}, u32[]{:S(2)}) async-start(bf16[8,384,896]{2,1,0:T(8,128)(2,1)} %shard_map.59.refs_0_), calls=%async_computation.2 | async-start | bytes 11010048 | tf_op jit(solution)/shard_map/all_to_all | solution.py:205
  127.2 1.9 collective-permute-start
  129.1 7.4 %shard_map.57.refs_3_.refs_5_ = f32[896,1024]{1,0:T(8,128)} custom-call(bf16[8,192,896]{2,1,0:T(8,128)(2,1)} %all-to-all-done.refs_0_, bf16[4,192,1024]{2,1,0:T(8,128)(2,1)} %bitcast.22, bf16[4,192,1024]{2,1,0:T(8,128)(2,1)} %bitcast.18), custom_call_target="tpu_custom_call" | custom-call | flops 1024 | bytes 1024 | tf_op jit(solution)/shard_map/pallas_call | solution.py:160
  136.5 0.1 collective-permute-done
  136.7 0.0 collective-permute-done.2.refs_1_.refs_0_
  136.7 0.0 collective-permute-done.3.refs_2_.refs_0_
  136.7 0.7 copy-done.7
  137.4 0.0 all-gather.5.cloned.1.call-update
  137.4 1.4 copy-done.4
  138.8 2.1 collective-permute-start.7
  140.9 0.0 copy-done.2
  140.9 0.0 collective-permute-start.6
  140.9 32.9 %collective-permute-done.7.refs_2_.refs_3_ = bf16[4,192,1024]{2,1,0:T(8,128)(2,1)S(1)} collective-permute-done((bf16[4,192,1024]{2,1,0:T(8,128)(2,1)S(1)}, bf16[4,192,1024]{2,1,0:T(8,128)(2,1)S(1)}, u32[]{:S(2)}, u32[]{:S(2)}) %collective-permute-start.7) | collective-permute-done | bytes 1572896 | tf_op jit(solution)/shard_map/ppermute | solution.py:214
  173.8 1.1 copy-done.5
  175.0 1.9 collective-permute-done.6.refs_1_.refs_2_
  176.9 0.0 collective-permute-start.8
  176.9 2.7 %collective-permute-start.9 = (bf16[4,192,1024]{2,1,0:T(8,128)(2,1)}, bf16[4,192,1024]{2,1,0:T(8,128)(2,1)}, u32[]{:S(2)}, u32[]{:S(2)}) collective-permute-start(bf16[4,192,1024]{2,1,0:T(8,128)(2,1)} %shard_map.62.refs_4_), channel_id=1, source_target_pairs={{0,192},{64,0},{128,64},{192,128},{1,193},{65,1},{129,65},{193,129... | collective-permute-start | bytes 4718600 | tf_op jit(solution)/shard_map/ppermute | solution.py:219
  179.6 4.4 %shard_map.60 = bf16[8,192,896]{2,1,0:T(8,128)(2,1)} custom-call(f32[8]{0:T(128)} %fusion.9.wanted_ref, bf16[1024,1024]{1,0:T(8,128)(2,1)} %bitcast.27, bf16[8,384,896]{2,1,0:T(8,128)(2,1)} %shard_map.59.refs_0_), custom_call_target="tpu_custom_call" | custom-call | flops 1024 | bytes 1024 | tf_op jit(solution)/shard_map/pallas_call | solution.py:60
  183.9 6.3 %all-to-all-done.2.refs_0_ = bf16[8,384,896]{2,1,0:T(8,128)(2,1)} async-done(((bf16[8,384,896]{2,1,0:T(8,128)(2,1)}), bf16[8,384,896]{2,1,0:T(8,128)(2,1)}, u32[]{:S(2)}, u32[]{:S(2)}) %all-to-all-start.2) | async-done | bytes 5505056 | tf_op jit(solution)/shard_map/all_to_all | solution.py:205
  190.2 5.2 %all-to-all-start.1 = ((bf16[8,192,896]{2,1,0:T(8,128)(2,1)}), bf16[8,192,896]{2,1,0:T(8,128)(2,1)}, u32[]{:S(2)}, u32[]{:S(2)}) async-start(bf16[8,192,896]{2,1,0:T(8,128)(2,1)} %shard_map.60), calls=%async_computation.1 | async-start | bytes 5505024 | tf_op jit(solution)/shard_map/all_to_all | solution.py:205
  195.4 13.1 %shard_map.63.refs_3_ = f32[896,1024]{1,0:T(8,128)} custom-call(bf16[8,384,896]{2,1,0:T(8,128)(2,1)} %all-to-all-done.2.refs_0_, bf16[4,192,1024]{2,1,0:T(8,128)(2,1)} %shard_map.61.refs_1_, bf16[4,192,1024]{2,1,0:T(8,128)(2,1)} %collective-permute-done.6.refs_1_.refs_2_, bf16[4,192,1024]{2,1,0:T(8,128)(2,1)} %copy-done.5, ...), custom_call_target="tpu_custom_call" | custom-call | flops 199999995904 | bytes 100000000 | tf_op jit(solution)/shard_map/pallas_call | solution.py:160
  208.4 3.7 %collective-permute-done.8.refs_1_ = bf16[4,192,1024]{2,1,0:T(8,128)(2,1)} collective-permute-done((bf16[4,192,1024]{2,1,0:T(8,128)(2,1)}, bf16[4,192,1024]{2,1,0:T(8,128)(2,1)}, u32[]{:S(2)}, u32[]{:S(2)}) %collective-permute-start.8) | collective-permute-done | bytes 1572896 | tf_op jit(solution)/shard_map/ppermute | solution.py:219
  212.1 0.0 collective-permute-done.9.refs_2_
  212.1 16.7 %all-to-all-done.1.refs_0_ = bf16[8,192,896]{2,1,0:T(8,128)(2,1)} async-done(((bf16[8,192,896]{2,1,0:T(8,128)(2,1)}), bf16[8,192,896]{2,1,0:T(8,128)(2,1)}, u32[]{:S(2)}, u32[]{:S(2)}) %all-to-all-start.1) | async-done | bytes 2752544 | tf_op jit(solution)/shard_map/all_to_all | solution.py:205
  228.8 8.5 %shard_map.64 = f32[896,1024]{1,0:T(8,128)} custom-call(bf16[8,192,896]{2,1,0:T(8,128)(2,1)} %all-to-all-done.1.refs_0_, bf16[4,192,1024]{2,1,0:T(8,128)(2,1)} %collective-permute-done.8.refs_1_, bf16[4,192,1024]{2,1,0:T(8,128)(2,1)} %collective-permute-done.9.refs_2_, f32[896,1024]{1,0:T(8,128)} %shard_map.63.refs_3_), custom_call_target="tpu_custom_call" | custom-call | flops 1024 | bytes 1024 | tf_op jit(solution)/shard_map/pallas_call | solution.py:160
  (17 shorter events, 0.0 us)
Async XLA Ops:
  6.5 45.4 %all-gather.9.cloned.1.call-start = ((), (), s32[]{:S(2)}) async-start(), calls=%async_computation.5 | async-start | bytes 2359296 | tf_op jit(solution)/shard_map/all_gather | solution.py:195
  8.1 12.0 %copy-start.6 = (bf16[1,1,64,24,1024]{4,3,2,1,0:T(8,128)(2,1)S(1)}, bf16[1,1,64,24,1024]{4,3,2,1,0:T(8,128)(2,1)}, u32[]{:S(2)}) copy-start(bf16[1,1,64,24,1024]{4,3,2,1,0:T(8,128)(2,1)} %param.8) | copy-start | bytes 9437188
  8.1 16.1 %copy-start = (s32[64]{0:T(128)S(1)}, s32[64]{0:T(128)}, u32[]{:S(2)}) copy-start(s32[64]{0:T(128)} %param.9) | copy-start | bytes 772
  10.5 100.4 %all-gather.7.cloned.1.call-start = ((), (), s32[]{:S(2)}) async-start(), calls=%async_computation.4 | async-start | bytes 4718592 | tf_op jit(solution)/shard_map/all_gather | solution.py:195
  10.6 7.4 %collective-permute-start.4 = (bf16[128,1024]{1,0:T(8,128)(2,1)}, bf16[128,1024]{1,0:T(8,128)(2,1)S(1)}, u32[]{:S(2)}, u32[]{:S(2)}) collective-permute-start(bf16[128,1024]{1,0:T(8,128)(2,1)} %get-tuple-element.11), channel_id=1, source_target_pairs={{0,64},{64,128},{128,192},{192,0},{1,65},{65,129},{129,193},{193,1... | collective-permute-start | bytes 786440 | tf_op jit(solution)/shard_map/ppermute | solution.py:190
  12.7 6.5 %collective-permute-start.5 = (bf16[128,1024]{1,0:T(8,128)(2,1)S(1)}, bf16[128,1024]{1,0:T(8,128)(2,1)S(1)}, u32[]{:S(2)}, u32[]{:S(2)}) collective-permute-start(bf16[128,1024]{1,0:T(8,128)(2,1)S(1)} %get-tuple-element.14), channel_id=1, source_target_pairs={{0,192},{64,0},{128,64},{192,128},{1,193},{65,1},{129,65},{193,129... | collective-permute-start | bytes 786440 | tf_op jit(solution)/shard_map/ppermute | solution.py:190
  20.1 70.5 %collective-permute-start.1 = (bf16[1536,1024]{1,0:T(8,128)(2,1)S(1)}, bf16[1536,1024]{1,0:T(8,128)(2,1)}, u32[]{:S(2)}, u32[]{:S(2)}) collective-permute-start(bf16[1536,1024]{1,0:T(8,128)(2,1)S(1)} %bitcast.25), channel_id=1, source_target_pairs={{0,32},{16,48},{32,0},{48,16},{1,33},{17,49},{33,1},{49,17},{2,34}... | collective-permute-start | bytes 9437192 | tf_op jit(solution)/shard_map/ppermute | solution.py:181
  56.2 63.8 %all-to-all-start = ((bf16[8,192,896]{2,1,0:T(8,128)(2,1)}), bf16[8,192,896]{2,1,0:T(8,128)(2,1)}, u32[]{:S(2)}, u32[]{:S(2)}) async-start(bf16[8,192,896]{2,1,0:T(8,128)(2,1)} %shard_map.55.refs_0_), calls=%async_computation | async-start | bytes 5505024 | tf_op jit(solution)/shard_map/all_to_all | solution.py:205
  91.4 19.6 %copy-start.1 = (bf16[2,2,8,24,1024]{4,3,2,1,0:T(8,128)(2,1)}, bf16[2,2,8,24,1024]{4,3,2,1,0:T(8,128)(2,1)S(1)}, u32[]{:S(2)}) copy-start(bf16[2,2,8,24,1024]{4,3,2,1,0:T(8,128)(2,1)S(1)} %copy.20) | copy-start | bytes 4718596
  91.5 19.4 %copy-start.3 = (bf16[2,2,8,24,1024]{4,3,2,1,0:T(8,128)(2,1)}, bf16[2,2,8,24,1024]{4,3,2,1,0:T(8,128)(2,1)S(1)}, u32[]{:S(2)}) copy-start(bf16[2,2,8,24,1024]{4,3,2,1,0:T(8,128)(2,1)S(1)} %copy.19) | copy-start | bytes 4718596
  91.5 45.1 %collective-permute-start.2 = (bf16[4,192,1024]{2,1,0:T(8,128)(2,1)S(1)}, bf16[4,192,1024]{2,1,0:T(8,128)(2,1)}, u32[]{:S(2)}, u32[]{:S(2)}) collective-permute-start(bf16[4,192,1024]{2,1,0:T(8,128)(2,1)S(1)} %bitcast.20), channel_id=1, source_target_pairs={{0,64},{64,128},{128,192},{192,0},{1,65},{65,129},{129,193},{193,1... | collective-permute-start | bytes 4718600 | tf_op jit(solution)/shard_map/ppermute | solution.py:213
  92.1 44.5 %collective-permute-start.3 = (bf16[4,192,1024]{2,1,0:T(8,128)(2,1)S(1)}, bf16[4,192,1024]{2,1,0:T(8,128)(2,1)}, u32[]{:S(2)}, u32[]{:S(2)}) collective-permute-start(bf16[4,192,1024]{2,1,0:T(8,128)(2,1)S(1)} %bitcast.16), channel_id=1, source_target_pairs={{0,192},{64,0},{128,64},{192,128},{1,193},{65,1},{129,65},{193,129... | collective-permute-start | bytes 4718600 | tf_op jit(solution)/shard_map/ppermute | solution.py:213
  120.1 70.1 %all-to-all-start.2 = ((bf16[8,384,896]{2,1,0:T(8,128)(2,1)}), bf16[8,384,896]{2,1,0:T(8,128)(2,1)}, u32[]{:S(2)}, u32[]{:S(2)}) async-start(bf16[8,384,896]{2,1,0:T(8,128)(2,1)} %shard_map.59.refs_0_), calls=%async_computation.2 | async-start | bytes 11010048 | tf_op jit(solution)/shard_map/all_to_all | solution.py:205
  127.2 52.3 %all-gather.5.cloned.1.call-start = ((), (), s32[]{:S(2)}) async-start(), calls=%async_computation.3 | async-start | bytes 2359296 | tf_op jit(solution)/shard_map/all_gather | solution.py:195
  127.2 9.5 %collective-permute-start = (bf16[128,1024]{1,0:T(8,128)(2,1)}, bf16[128,1024]{1,0:T(8,128)(2,1)S(1)}, u32[]{:S(2)}, u32[]{:S(2)}) collective-permute-start(bf16[128,1024]{1,0:T(8,128)(2,1)} %get-tuple-element.12), channel_id=1, source_target_pairs={{0,128},{64,192},{128,0},{192,64},{1,129},{65,193},{129,1},{193,65... | collective-permute-start | bytes 786440 | tf_op jit(solution)/shard_map/ppermute | solution.py:190
  136.7 0.7 copy-start.7
  137.4 1.4 copy-start.4
  137.4 3.6 %copy-start.2 = (bf16[2,2,8,24,1024]{4,3,2,1,0:T(8,128)(2,1)S(1)}, bf16[2,2,8,24,1024]{4,3,2,1,0:T(8,128)(2,1)}, u32[]{:S(2)}) copy-start(bf16[2,2,8,24,1024]{4,3,2,1,0:T(8,128)(2,1)} %copy-done.1) | copy-start | bytes 4718596
  138.8 35.0 %collective-permute-start.7 = (bf16[4,192,1024]{2,1,0:T(8,128)(2,1)S(1)}, bf16[4,192,1024]{2,1,0:T(8,128)(2,1)S(1)}, u32[]{:S(2)}, u32[]{:S(2)}) collective-permute-start(bf16[4,192,1024]{2,1,0:T(8,128)(2,1)S(1)} %bitcast.23), channel_id=1, source_target_pairs={{0,192},{64,0},{128,64},{192,128},{1,193},{65,1},{129,65},{193,129... | collective-permute-start | bytes 4718600 | tf_op jit(solution)/shard_map/ppermute | solution.py:214
  140.9 35.9 %collective-permute-start.6 = (bf16[4,192,1024]{2,1,0:T(8,128)(2,1)S(1)}, bf16[4,192,1024]{2,1,0:T(8,128)(2,1)}, u32[]{:S(2)}, u32[]{:S(2)}) collective-permute-start(bf16[4,192,1024]{2,1,0:T(8,128)(2,1)S(1)} %bitcast.19), channel_id=1, source_target_pairs={{0,64},{64,128},{128,192},{192,0},{1,65},{65,129},{129,193},{193,1... | collective-permute-start | bytes 4718600 | tf_op jit(solution)/shard_map/ppermute | solution.py:214
  173.8 1.1 copy-start.5
  176.9 35.2 %collective-permute-start.8 = (bf16[4,192,1024]{2,1,0:T(8,128)(2,1)}, bf16[4,192,1024]{2,1,0:T(8,128)(2,1)}, u32[]{:S(2)}, u32[]{:S(2)}) collective-permute-start(bf16[4,192,1024]{2,1,0:T(8,128)(2,1)} %shard_map.61.refs_1_), channel_id=1, source_target_pairs={{0,64},{64,128},{128,192},{192,0},{1,65},{65,129},{129,193},{193,1... | collective-permute-start | bytes 4718600 | tf_op jit(solution)/shard_map/ppermute | solution.py:219
  176.9 35.2 %collective-permute-start.9 = (bf16[4,192,1024]{2,1,0:T(8,128)(2,1)}, bf16[4,192,1024]{2,1,0:T(8,128)(2,1)}, u32[]{:S(2)}, u32[]{:S(2)}) collective-permute-start(bf16[4,192,1024]{2,1,0:T(8,128)(2,1)} %shard_map.62.refs_4_), channel_id=1, source_target_pairs={{0,192},{64,0},{128,64},{192,128},{1,193},{65,1},{129,65},{193,129... | collective-permute-start | bytes 4718600 | tf_op jit(solution)/shard_map/ppermute | solution.py:219
  190.2 38.6 %all-to-all-start.1 = ((bf16[8,192,896]{2,1,0:T(8,128)(2,1)}), bf16[8,192,896]{2,1,0:T(8,128)(2,1)}, u32[]{:S(2)}, u32[]{:S(2)}) async-start(bf16[8,192,896]{2,1,0:T(8,128)(2,1)} %shard_map.60), calls=%async_computation.1 | async-start | bytes 5505024 | tf_op jit(solution)/shard_map/all_to_all | solution.py:205
Sparse Core Ops, SparseCore 0:
  10.7 41.1 all-gather.8
  53.7 57.2 all-gather.6
  137.5 40.2 all-gather.4
